TPU v7x, 32 devices: a whole 2x2x4 slice. The times are simulated.
32 devices in a mesh: rep: 4 (over z), fsdp: 8 (over y, x, core).
Axes of the slice: x: 2, y: 2, z: 4, core: 2. Of those that a mesh axis runs over, the one named last changes fastest.
Arguments:
- query_rows: bfloat16 [12288, 3072], P(('rep', 'fsdp')), may hold values from -48 to 48
- key_rows: bfloat16 [12288, 3072], P(('rep', 'fsdp')), may hold values from -48 to 48
- value_rows: bfloat16 [12288, 3072], P(('rep', 'fsdp')), may hold values from -6 to 6
- out_grad: bfloat16 [12288, 3072], P(('rep', 'fsdp')), may hold values from -6 to 6
- out_weight: bfloat16 [3072, 3072], P('fsdp'), may hold values from -0.109375 to 0.109375
- segment_ids: int32 [12288], P(('rep', 'fsdp')), may hold values from -1 to 1023, as said below
Outputs:
- query_grad: bfloat16 [12288, 3072], P(('rep', 'fsdp'))
- key_grad: bfloat16 [12288, 3072], P(('rep', 'fsdp'))
- value_grad: bfloat16 [12288, 3072], P(('rep', 'fsdp'))
- weight_grad: float32 [3072, 3072], P('fsdp')
Inputs may be any that keep to these rules, and one draw needn't show every extreme that they name: `segment_ids`: each aligned block of 384 rows holds whole images in contiguous runs of rows followed by padding rows with id -1; an image id appears in no other block; every image and every block's live part has a multiple of 12 rows, at least 4 such units live a block; in each aligned run of 8 blocks exactly one block has no padding, and every other block has at most 192 live rows.
All inputs are finite; a program needn't handle non-finite values.
Results may differ from a plain program's by a relative error of at most 0.02.
Values may be sent and summed in bfloat16 or wider, within the bound.
No kernel may reach another device: no remote copies, remote signals or barrier semaphores. Data moves between devices by JAX's collectives and lax.ppermute only.
A program may use at most 192 MiB of HBM per device.

v0:
```python
import functools
import math

import jax
import jax.numpy as jnp
from jax import lax
from jax.experimental import pallas as pl
from jax.experimental.pallas import tpu as pltpu
from jax.sharding import PartitionSpec as P

E = 128
BLOCK_HEADS = 3
BLOCK = BLOCK_HEADS * E
PARTS = 2
SUM_PARTS = 4
F32 = jnp.float32
BF16 = jnp.bfloat16
LOG2_E = math.log2(math.e)
FAR = -1e30
VMEM_LIMIT = 48 * 1024 * 1024


def dot(a, b, a_dim, b_dim):
    return lax.dot_general(a, b, (((a_dim,), (b_dim,)), ((), ())), preferred_element_type=F32)


def forward_kernel(order, ids_column, ids_row, query, key, value, attended, weights, bias):
    @pl.when(pl.program_id(0) == 0)
    def _():
        allowed = (ids_column[...] == ids_row[...]) & (ids_column[...] >= 0)
        bias[...] = jnp.where(allowed, 0.0, FAR)

    scale = LOG2_E / math.sqrt(E)
    for head in range(BLOCK_HEADS):
        columns = slice(head * E, (head + 1) * E)
        logits = dot(key[:, columns], query[:, columns], 1, 1) * scale + bias[...]
        top = jnp.maximum(jnp.max(logits, axis=0, keepdims=True), 0.5 * FAR)
        raw = jnp.exp2(logits - top)
        total = jnp.sum(raw, axis=0, keepdims=True)
        half = (raw * (1.0 / jnp.maximum(total, 0.5))).astype(BF16)
        weights[head] = half
        attended[:, columns] = dot(half, value[:, columns], 0, 0).astype(BF16)


def forward(order, segment_ids, query_rows, key_rows, value_rows):
    rows, width = query_rows.shape
    blocks = width // BLOCK
    absolute = pl.BlockSpec((rows, BLOCK), lambda j, order: (0, order[j]))
    return pl.pallas_call(
        forward_kernel,
        grid_spec=pltpu.PrefetchScalarGridSpec(
            num_scalar_prefetch=1,
            grid=(blocks,),
            in_specs=[
                pl.BlockSpec((rows, 1), lambda j, order: (0, 0)),
                pl.BlockSpec((1, rows), lambda j, order: (0, 0)),
                absolute,
                absolute,
                absolute,
            ],
            out_specs=[
                pl.BlockSpec((rows, BLOCK), lambda j, order: (0, j)),
                pl.BlockSpec((BLOCK_HEADS, rows, rows), lambda j, order: (j, 0, 0)),
            ],
            scratch_shapes=[pltpu.VMEM((rows, rows), F32)],
        ),
        out_shape=[
            jax.ShapeDtypeStruct((rows, width), BF16),
            jax.ShapeDtypeStruct((width // E, rows, rows), BF16),
        ],
        compiler_params=pltpu.CompilerParams(vmem_limit_bytes=VMEM_LIMIT),
        cost_estimate=pl.CostEstimate(
            flops=4 * rows * rows * width,
            bytes_accessed=8 * rows * width + 2 * rows * rows * (width // E),
            transcendentals=rows * rows * (width // E),
        ),
        name="attention_forward",
    )(order, segment_ids.reshape(rows, 1), segment_ids.reshape(1, rows), query_rows, key_rows, value_rows)


def backward_kernel(
    order, grad_main, grad_low, grad_high, query, key, value, weights, grad_query, grad_key, grad_value
):
    grad_all = jnp.concatenate([grad_main[...], grad_low[...], grad_high[...]], axis=0)
    inverse_root = 1.0 / math.sqrt(E)
    for head in range(BLOCK_HEADS):
        columns = slice(head * E, (head + 1) * E)
        grad = grad_all[:, columns]
        half = weights[head]
        grad_probs = dot(value[:, columns], grad, 1, 1)
        wide = half.astype(F32)
        row_dot = jnp.sum(wide * grad_probs, axis=0, keepdims=True)
        grad_logits = (wide * (grad_probs - row_dot)).astype(BF16)
        grad_value[:, columns] = dot(half, grad, 1, 0).astype(BF16)
        grad_key[:, columns] = (dot(grad_logits, query[:, columns], 1, 0) * inverse_root).astype(BF16)
        grad_query[:, columns] = (dot(grad_logits, key[:, columns], 0, 0) * inverse_root).astype(BF16)


def backward(order, grad_main, grad_low, grad_high, query_rows, key_rows, value_rows, weights):
    rows, width = query_rows.shape
    blocks = width // BLOCK
    absolute = pl.BlockSpec((rows, BLOCK), lambda j, order: (0, order[j]))

    def relative(a):
        return pl.BlockSpec((a.shape[0], BLOCK), lambda j, order: (0, j))

    return pl.pallas_call(
        backward_kernel,
        grid_spec=pltpu.PrefetchScalarGridSpec(
            num_scalar_prefetch=1,
            grid=(blocks,),
            in_specs=[
                relative(grad_main),
                relative(grad_low),
                relative(grad_high),
                absolute,
                absolute,
                absolute,
                pl.BlockSpec((BLOCK_HEADS, rows, rows), lambda j, order: (j, 0, 0)),
            ],
            out_specs=[absolute, absolute, absolute],
        ),
        out_shape=[jax.ShapeDtypeStruct((rows, width), BF16)] * 3,
        compiler_params=pltpu.CompilerParams(vmem_limit_bytes=VMEM_LIMIT),
        cost_estimate=pl.CostEstimate(
            flops=8 * rows * rows * width,
            bytes_accessed=14 * rows * width + 2 * rows * rows * (width // E),
            transcendentals=0,
        ),
        name="attention_backward",
    )(order, grad_main, grad_low, grad_high, query_rows, key_rows, value_rows, weights)


def sum_over_line(part):
    place = lax.axis_index("rep")
    in_middle = (place == 1) | (place == 2)
    arrived = lax.ppermute(part, "rep", [(0, 1), (3, 2)])
    pair = (part.astype(F32) + arrived.astype(F32)).astype(BF16)
    arrived = lax.ppermute(pair, "rep", [(1, 2), (2, 1)])
    total = (pair.astype(F32) + arrived.astype(F32)).astype(BF16)
    arrived = lax.ppermute(total, "rep", [(1, 0), (2, 3)])
    return jnp.where(in_middle, total, arrived).astype(F32)


def pairwise(query_rows, key_rows, value_rows, out_grad, out_weight, segment_ids):
    rows, width = query_rows.shape
    short = rows // 2
    quarter = short // 2
    me = lax.axis_index("fsdp")
    core = me % 2
    order = me ^ jnp.arange(8, dtype=jnp.int32)

    def swap(a, mask):
        return lax.ppermute(a, "fsdp", [(f, f ^ mask) for f in range(8)])

    def own_half(a):
        low, high = a[:quarter], a[quarter:]
        return jnp.where(core == 0, low, high), jnp.where(core == 0, high, low)

    live_ids = segment_ids[short:] >= 0
    main = out_grad[:short]
    extra = jnp.where(live_ids[:, None], out_grad[short:], jnp.zeros((), BF16))

    attended, weights = forward(order, segment_ids, query_rows, key_rows, value_rows)

    part_width = width // PARTS
    planes, others = [], []
    for part in range(PARTS):
        columns = slice(part * part_width, (part + 1) * part_width)
        here, there = own_half(extra[:, columns])
        here = here + swap(there, 1)
        cut = quarter // 2
        mine = main[:, columns]
        from_x = swap(jnp.concatenate([mine, here[:cut]]), 2)
        from_y = swap(jnp.concatenate([mine, here[cut:]]), 4)
        first = here[:cut] + from_x[short:]
        second = here[cut:] + from_y[short:]
        via_y = swap(jnp.concatenate([from_x[:quarter], first]), 4)
        via_x = swap(jnp.concatenate([from_y[quarter:short], second]), 2)
        plane = jnp.concatenate(
            [
                mine,
                from_x[:short],
                from_y[:short],
                via_y[:quarter],
                via_x[:quarter],
                first + via_y[quarter:],
                second + via_x[quarter:],
            ]
        )
        planes.append(plane)
        others.append(swap(plane, 1))

    here, there = own_half(attended[short:])
    there = jnp.concatenate([there[:, (j ^ 1) * BLOCK : ((j ^ 1) + 1) * BLOCK] for j in range(8)], axis=1)
    here = here + swap(there, 1)
    both = jnp.concatenate([attended[:short], here])
    pair_width = 2 * BLOCK
    kept = both[:, :pair_width]
    arrived = [swap(both[:, m // 2 * pair_width : (m // 2 + 1) * pair_width], m) for m in (2, 4, 6)]
    pieces = [a[:short] for a in [kept] + arrived]
    pieces.append(kept[short:] + arrived[0][short:] + arrived[1][short:] + arrived[2][short:])
    gathered = jnp.concatenate(pieces)
    attended_plane = gathered[:, :BLOCK]
    attended_other = swap(gathered[:, BLOCK:], 1)

    root = 1.0 / math.sqrt(rows * lax.axis_size("fsdp") * lax.axis_size("rep"))
    sums = []
    for part in range(PARTS):
        term = dot(attended_plane, planes[part], 0, 0) + dot(attended_other, others[part], 0, 0)
        term = term.astype(BF16)
        sub = SUM_PARTS // PARTS
        sub_width = part_width // sub
        for i in range(sub):
            sums.append(sum_over_line(term[:, i * sub_width : (i + 1) * sub_width]) * root)
    weight_grad = jnp.concatenate(sums, axis=1)

    grad_plane, grad_other = 0.0, 0.0
    for part in range(PARTS):
        weight_part = out_weight[:, part * part_width : (part + 1) * part_width]
        grad_other = grad_other + dot(others[part], weight_part, 1, 1)
        grad_plane = grad_plane + dot(planes[part], weight_part, 1, 1)
    grad = jnp.concatenate([grad_plane.astype(BF16), swap(grad_other.astype(BF16), 1)], axis=1)
    tail = grad[4 * short :]
    moved = [
        swap(jnp.concatenate([grad[i * short : (i + 1) * short], tail]), 2 * i) for i in (1, 2, 3)
    ]
    whole = jnp.concatenate([jnp.concatenate([grad[:short], tail])] + moved, axis=1)
    tail = whole[short:]
    tail_other = swap(tail, 1)
    tail_other = jnp.concatenate(
        [tail_other[:, (j ^ 1) * BLOCK : ((j ^ 1) + 1) * BLOCK] for j in range(8)], axis=1
    )
    low = jnp.where(core == 0, tail, tail_other)
    high = jnp.where(core == 0, tail_other, tail)
    grads = backward(order, whole[:short], low, high, query_rows, key_rows, value_rows, weights)
    return (*grads, weight_grad)


def general(query_rows, key_rows, value_rows, out_grad, out_weight, segment_ids):
    rows, width = query_rows.shape
    short = rows // 2
    count = lax.axis_size("fsdp")
    order = jnp.arange(width // BLOCK, dtype=jnp.int32)
    extra = jnp.where((segment_ids[short:] >= 0)[:, None], out_grad[short:], jnp.zeros((), BF16))
    attended, weights = forward(order, segment_ids, query_rows, key_rows, value_rows)
    live = jnp.concatenate(
        [lax.all_gather(out_grad[:short], "fsdp", axis=0, tiled=True), lax.psum(extra, "fsdp")]
    )
    attended_live = jnp.concatenate(
        [
            lax.all_to_all(attended[:short], "fsdp", split_axis=1, concat_axis=0, tiled=True),
            lax.psum_scatter(attended[short:], "fsdp", scatter_dimension=1, tiled=True),
        ]
    )
    term = dot(attended_live, live, 0, 0).astype(BF16)
    total = lax.psum(term, "rep").astype(F32)
    grad = dot(live, out_weight, 1, 1).astype(BF16)
    grad_main = lax.all_to_all(
        grad[: count * short], "fsdp", split_axis=0, concat_axis=1, tiled=True
    )
    grad_extra = lax.all_gather(grad[count * short :], "fsdp", axis=1, tiled=True)
    half = short // 2
    grads = backward(
        order, grad_main, grad_extra[:half], grad_extra[half:], query_rows, key_rows, value_rows, weights
    )
    return (*grads, total * (1.0 / math.sqrt(rows * count * lax.axis_size("rep"))))


def solution(mesh):
    fits = mesh.shape["fsdp"] == 8 and mesh.shape["rep"] == 4
    split = P(("rep", "fsdp"), None)
    return jax.shard_map(
        pairwise if fits else general,
        mesh=mesh,
        in_specs=(split, split, split, split, P("fsdp", None), P(("rep", "fsdp"))),
        out_specs=(split, split, split, P("fsdp", None)),
        check_vma=False,
    )
```

profile of v0, /device:TPU:0, one launch (start us, length us, event | category | flops | bytes accessed | tf_op | source)
XLA Modules:
  0.0 244.1 jit_solution(7394091423319604480)
XLA Ops:
  2.1 1.7 copy-done
  3.8 15.7 %attention_forward.1 = (bf16[384,3072]{1,0:T(8,128)(2,1)S(1)}, bf16[24,384,384]{2,1,0:T(8,128)(2,1)}) custom-call(s32[8]{0:T(128)S(1)} %iota_xor_fusion.order, s32[384,1]{1,0:T(8,128)S(1)} %reshape.17.ids_column, s32[1,384]{1,0:T(1,128)S(1)} %reshape.16.ids_row, bf16[384,3072]{1,0:T(8,128)(2,1)S(1)} %copy-done, bf16[384,3072]{1,0:T(8,128)(2,1)} %key.3, ...), custom_call_target="tpu_custom_call" | custom-call | flops 1811939328 | bytes 16515072 | tf_op jit(solution)/shard_map/attention_forward/pallas_call | solution.py:49
  27.0 1.5 fusion.21
  28.5 1.1 slice.301
  29.6 1.2 select_add_fusion.2
  31.0 2.5 %collective-permute-start.1 = (bf16[240,1536]{1,0:T(8,128)(2,1)S(1)}, bf16[240,1536]{1,0:T(8,128)(2,1)S(1)}, u32[]{:S(2)}, u32[]{:S(2)}) collective-permute-start(bf16[240,1536]{1,0:T(8,128)(2,1)S(1)} %get-tuple-element.39), channel_id=1, source_target_pairs={{0,2},{1,3},{2,0},{3,1},{4,6},{5,7},{6,4},{7,5},{8,10},{9,11},{10,... | collective-permute-start | bytes 2211848 | tf_op jit(solution)/shard_map/ppermute | solution.py:154
  33.6 1.5 collective-permute-start.2
  36.1 1.2 select_add_fusion
  37.4 1.8 collective-permute-start.18
  39.2 11.7 %collective-permute-done.1 = bf16[240,1536]{1,0:T(8,128)(2,1)S(1)} collective-permute-done((bf16[240,1536]{1,0:T(8,128)(2,1)S(1)}, bf16[240,1536]{1,0:T(8,128)(2,1)S(1)}, u32[]{:S(2)}, u32[]{:S(2)}) %collective-permute-start.1) | collective-permute-done | bytes 737312 | tf_op jit(solution)/shard_map/ppermute | solution.py:154
  50.9 2.0 collective-permute-start.19
  52.9 1.5 collective-permute-start.20
  54.4 12.3 %collective-permute-done.6 = bf16[240,1536]{1,0:T(8,128)(2,1)S(1)} collective-permute-done((bf16[240,1536]{1,0:T(8,128)(2,1)S(1)}, bf16[240,1536]{1,0:T(8,128)(2,1)S(1)}, u32[]{:S(2)}, u32[]{:S(2)}) %collective-permute-start.6) | collective-permute-done | bytes 737312 | tf_op jit(solution)/shard_map/ppermute | solution.py:154
  66.7 2.0 collective-permute-done.7
  68.8 1.6 collective-permute-start.3
  73.2 23.2 %collective-permute-done.3 = bf16[144,1536]{1,0:T(8,128)(2,1)S(1)} collective-permute-done((bf16[144,1536]{1,0:T(8,128)(2,1)S(1)}, bf16[144,1536]{1,0:T(8,128)(2,1)S(1)}, u32[]{:S(2)}, u32[]{:S(2)}) %collective-permute-start.3) | collective-permute-done | bytes 442400 | tf_op jit(solution)/shard_map/ppermute | solution.py:154
  96.8 1.8 collective-permute-start.8
  98.7 9.7 %collective-permute-done.8 = bf16[144,1536]{1,0:T(8,128)(2,1)S(1)} collective-permute-done((bf16[144,1536]{1,0:T(8,128)(2,1)S(1)}, bf16[144,1536]{1,0:T(8,128)(2,1)S(1)}, u32[]{:S(2)}, u32[]{:S(2)}) %collective-permute-start.8) | collective-permute-done | bytes 442400 | tf_op jit(solution)/shard_map/ppermute | solution.py:154
  110.2 1.6 fusion.6
  111.8 1.6 fusion.2
  113.4 4.7 %collective-permute-done.21 = bf16[864,384]{1,0:T(8,128)(2,1)S(1)} collective-permute-done((bf16[864,384]{1,0:T(8,128)(2,1)S(1)}, bf16[864,384]{1,0:T(8,128)(2,1)S(1)}, u32[]{:S(2)}, u32[]{:S(2)}) %collective-permute-start.21) | collective-permute-done | bytes 663584 | tf_op jit(solution)/shard_map/ppermute | solution.py:154
  118.1 1.4 fusion.26
  119.5 1.4 fusion
  121.1 3.4 %collective-permute-start.22 = (bf16[384,768]{1,0:T(8,128)(2,1)S(1)}, bf16[384,768]{1,0:T(8,128)(2,1)S(1)}, u32[]{:S(2)}, u32[]{:S(2)}) collective-permute-start(bf16[384,768]{1,0:T(8,128)(2,1)S(1)} %get-tuple-element.26), channel_id=1, source_target_pairs={{0,8},{24,16},{1,9},{25,17},{2,10},{26,18},{3,11},{27,19},{4,12},{... | collective-permute-start | bytes 1769480 | tf_op jit(solution)/shard_map/ppermute | solution.py:137
  124.5 1.5 collective-permute-start.25
  126.0 1.6 fusion.4
  127.5 1.6 fusion.3
  129.2 1.4 fusion.27
  130.6 1.4 fusion.1
  132.1 1.4 collective-permute-start.28
  133.5 1.3 collective-permute-start.31
  135.1 1.5 collective-permute-start.13
  136.6 1.5 collective-permute-done.22
  138.1 1.5 collective-permute-start.14
  139.6 11.1 %collective-permute-done.25 = bf16[384,768]{1,0:T(8,128)(2,1)S(1)} collective-permute-done((bf16[384,768]{1,0:T(8,128)(2,1)S(1)}, bf16[384,768]{1,0:T(8,128)(2,1)S(1)}, u32[]{:S(2)}, u32[]{:S(2)}) %collective-permute-start.25) | collective-permute-done | bytes 589856 | tf_op jit(solution)/shard_map/ppermute | solution.py:137
  150.7 2.4 collective-permute-start.15
  153.5 9.9 %collective-permute-done.28 = bf16[384,768]{1,0:T(8,128)(2,1)S(1)} collective-permute-done((bf16[384,768]{1,0:T(8,128)(2,1)S(1)}, bf16[384,768]{1,0:T(8,128)(2,1)S(1)}, u32[]{:S(2)}, u32[]{:S(2)}) %collective-permute-start.28) | collective-permute-done | bytes 589856 | tf_op jit(solution)/shard_map/ppermute | solution.py:137
  164.1 11.1 %collective-permute-done.31 = bf16[384,768]{1,0:T(8,128)(2,1)S(1)} collective-permute-done((bf16[384,768]{1,0:T(8,128)(2,1)S(1)}, bf16[384,768]{1,0:T(8,128)(2,1)S(1)}, u32[]{:S(2)}, u32[]{:S(2)}) %collective-permute-start.31) | collective-permute-done | bytes 589856 | tf_op jit(solution)/shard_map/ppermute | solution.py:137
  178.3 1.3 collective-permute-start.24
  179.7 1.3 collective-permute-start.27
  181.2 1.3 collective-permute-start.30
  182.7 1.4 collective-permute-start.33
  184.4 15.5 %attention_backward.1 = (bf16[384,3072]{1,0:T(8,128)(2,1)}, bf16[384,3072]{1,0:T(8,128)(2,1)}, bf16[384,3072]{1,0:T(8,128)(2,1)}) custom-call(s32[8]{0:T(128)S(1)} %iota_xor_fusion.order, bf16[192,3072]{1,0:T(8,128)(2,1)S(1)} %slice.364.grad_main, bf16[96,3072]{1,0:T(8,128)(2,1)S(1)} %get-tuple-element.33.grad_low, ...), custom_call_target="tpu_custom_call" | custom-call | flops 3623878656 | bytes 23592960 | tf_op jit(solution)/shard_map/attention_backward/pallas_call | solution.py:107
  199.8 3.6 %collective-permute-done.24 = bf16[384,768]{1,0:T(8,128)(2,1)S(1)} collective-permute-done((bf16[384,768]{1,0:T(8,128)(2,1)S(1)}, bf16[384,768]{1,0:T(8,128)(2,1)S(1)}, u32[]{:S(2)}, u32[]{:S(2)}) %collective-permute-start.24) | collective-permute-done | bytes 589856 | tf_op jit(solution)/shard_map/ppermute | solution.py:141
  203.6 12.5 %collective-permute-done.27 = bf16[384,768]{1,0:T(8,128)(2,1)S(1)} collective-permute-done((bf16[384,768]{1,0:T(8,128)(2,1)S(1)}, bf16[384,768]{1,0:T(8,128)(2,1)S(1)}, u32[]{:S(2)}, u32[]{:S(2)}) %collective-permute-start.27) | collective-permute-done | bytes 589856 | tf_op jit(solution)/shard_map/ppermute | solution.py:141
  216.2 12.5 %collective-permute-done.30 = bf16[384,768]{1,0:T(8,128)(2,1)S(1)} collective-permute-done((bf16[384,768]{1,0:T(8,128)(2,1)S(1)}, bf16[384,768]{1,0:T(8,128)(2,1)S(1)}, u32[]{:S(2)}, u32[]{:S(2)}) %collective-permute-start.30) | collective-permute-done | bytes 589856 | tf_op jit(solution)/shard_map/ppermute | solution.py:141
  228.9 12.3 %collective-permute-done.33 = bf16[384,768]{1,0:T(8,128)(2,1)S(1)} collective-permute-done((bf16[384,768]{1,0:T(8,128)(2,1)S(1)}, bf16[384,768]{1,0:T(8,128)(2,1)S(1)}, u32[]{:S(2)}, u32[]{:S(2)}) %collective-permute-start.33) | collective-permute-done | bytes 589856 | tf_op jit(solution)/shard_map/ppermute | solution.py:141
  241.3 2.8 %pad_maximum_fusion = f32[384,3072]{1,0:T(8,128)} fusion(f32[384,768]{1,0:T(8,128)S(1)} %convert_multiply_fusion, f32[384,768]{1,0:T(8,128)S(1)} %convert_multiply_fusion.1, f32[384,768]{1,0:T(8,128)S(1)} %convert_multiply_fusion.2, f32[384,768]{1,0:T(8,128)S(1)} %convert_multiply_fusion.3), kind=kLoop, calls=%fused_computation | loop fusion | flops 3538944 | bytes 9437184 | tf_op jit(solution)/shard_map/concatenate | solution.py:216
  (130 shorter events, 20.9 us)
Async XLA Ops:
  2.1 1.7 copy-start
  19.5 5.8 %copy-start.8 = (s32[384]{0:T(512)S(1)}, s32[384]{0:T(512)}, u32[]{:S(2)}) copy-start(s32[384]{0:T(512)} %param.11) | copy-start | bytes 4612
  19.5 5.9 %copy-start.5 = (bf16[384,3072]{1,0:T(8,128)(2,1)S(1)}, bf16[384,3072]{1,0:T(8,128)(2,1)}, u32[]{:S(2)}) copy-start(bf16[384,3072]{1,0:T(8,128)(2,1)} %param.9) | copy-start | bytes 7077892
  24.9 11.3 %collective-permute-start.17 = (bf16[96,3072]{1,0:T(8,128)(2,1)}, bf16[96,3072]{1,0:T(8,128)(2,1)}, u32[]{:S(2)}, u32[]{:S(2)}) collective-permute-start(bf16[96,3072]{1,0:T(8,128)(2,1)} %constant_dynamic-update-slice_fusion.10), channel_id=1, source_target_pairs={{0,1},{1,0},{2,3},{3,2},{4,5},{5,4},{6,7},{7,6},{8,9},{9,8},{10,11... | collective-permute-start | bytes 1769480 | tf_op jit(solution)/shard_map/ppermute | solution.py:154
  26.4 3.2 %collective-permute-start = (bf16[96,1536]{1,0:T(8,128)(2,1)}, bf16[96,1536]{1,0:T(8,128)(2,1)}, u32[]{:S(2)}, u32[]{:S(2)}) collective-permute-start(bf16[96,1536]{1,0:T(8,128)(2,1)} %get-tuple-element.36), channel_id=1, source_target_pairs={{0,1},{1,0},{2,3},{3,2},{4,5},{5,4},{6,7},{7,6},{8,9},{9,8},{10,11... | collective-permute-start | bytes 884744 | tf_op jit(solution)/shard_map/ppermute | solution.py:154
  26.5 3.1 %collective-permute-start.5 = (bf16[96,1536]{1,0:T(8,128)(2,1)}, bf16[96,1536]{1,0:T(8,128)(2,1)}, u32[]{:S(2)}, u32[]{:S(2)}) collective-permute-start(bf16[96,1536]{1,0:T(8,128)(2,1)} %get-tuple-element.37), channel_id=1, source_target_pairs={{0,1},{1,0},{2,3},{3,2},{4,5},{5,4},{6,7},{7,6},{8,9},{9,8},{10,11... | collective-permute-start | bytes 884744 | tf_op jit(solution)/shard_map/ppermute | solution.py:154
  29.6 1.3 copy-start.7
  30.9 4.2 %copy-start.6 = (bf16[192,1536]{1,0:T(8,128)(2,1)S(1)}, bf16[192,1536]{1,0:T(8,128)(2,1)}, u32[]{:S(2)}) copy-start(bf16[192,1536]{1,0:T(8,128)(2,1)} %get-tuple-element.17) | copy-start | bytes 1769476
  31.0 19.9 %collective-permute-start.1 = (bf16[240,1536]{1,0:T(8,128)(2,1)S(1)}, bf16[240,1536]{1,0:T(8,128)(2,1)S(1)}, u32[]{:S(2)}, u32[]{:S(2)}) collective-permute-start(bf16[240,1536]{1,0:T(8,128)(2,1)S(1)} %get-tuple-element.39), channel_id=1, source_target_pairs={{0,2},{1,3},{2,0},{3,1},{4,6},{5,7},{6,4},{7,5},{8,10},{9,11},{10,... | collective-permute-start | bytes 2211848 | tf_op jit(solution)/shard_map/ppermute | solution.py:154
  33.6 19.3 %collective-permute-start.2 = (bf16[240,1536]{1,0:T(8,128)(2,1)S(1)}, bf16[240,1536]{1,0:T(8,128)(2,1)S(1)}, u32[]{:S(2)}, u32[]{:S(2)}) collective-permute-start(bf16[240,1536]{1,0:T(8,128)(2,1)S(1)} %get-tuple-element.38), channel_id=1, source_target_pairs={{0,4},{1,5},{2,6},{3,7},{4,0},{5,1},{6,2},{7,3},{8,12},{9,13},{10,... | collective-permute-start | bytes 2211848 | tf_op jit(solution)/shard_map/ppermute | solution.py:154
  35.2 2.1 copy-start.2
  35.2 31.5 %collective-permute-start.6 = (bf16[240,1536]{1,0:T(8,128)(2,1)S(1)}, bf16[240,1536]{1,0:T(8,128)(2,1)S(1)}, u32[]{:S(2)}, u32[]{:S(2)}) collective-permute-start(bf16[240,1536]{1,0:T(8,128)(2,1)S(1)} %get-tuple-element.41), channel_id=1, source_target_pairs={{0,2},{1,3},{2,0},{3,1},{4,6},{5,7},{6,4},{7,5},{8,10},{9,11},{10,... | collective-permute-start | bytes 2211848 | tf_op jit(solution)/shard_map/ppermute | solution.py:154
  35.9 32.8 %collective-permute-start.7 = (bf16[240,1536]{1,0:T(8,128)(2,1)S(1)}, bf16[240,1536]{1,0:T(8,128)(2,1)S(1)}, u32[]{:S(2)}, u32[]{:S(2)}) collective-permute-start(bf16[240,1536]{1,0:T(8,128)(2,1)S(1)} %get-tuple-element.40), channel_id=1, source_target_pairs={{0,4},{1,5},{2,6},{3,7},{4,0},{5,1},{6,2},{7,3},{8,12},{9,13},{10,... | collective-permute-start | bytes 2211848 | tf_op jit(solution)/shard_map/ppermute | solution.py:154
  37.4 71.7 %collective-permute-start.18 = (bf16[288,768]{1,0:T(8,128)(2,1)S(1)}, bf16[288,768]{1,0:T(8,128)(2,1)S(1)}, u32[]{:S(2)}, u32[]{:S(2)}) collective-permute-start(bf16[288,768]{1,0:T(8,128)(2,1)S(1)} %get-tuple-element.20), channel_id=1, source_target_pairs={{0,2},{1,3},{2,0},{3,1},{4,6},{5,7},{6,4},{7,5},{8,10},{9,11},{10,... | collective-permute-start | bytes 1327112 | tf_op jit(solution)/shard_map/ppermute | solution.py:154
  50.9 58.3 %collective-permute-start.19 = (bf16[288,768]{1,0:T(8,128)(2,1)S(1)}, bf16[288,768]{1,0:T(8,128)(2,1)S(1)}, u32[]{:S(2)}, u32[]{:S(2)}) collective-permute-start(bf16[288,768]{1,0:T(8,128)(2,1)S(1)} %get-tuple-element.19), channel_id=1, source_target_pairs={{0,4},{1,5},{2,6},{3,7},{4,0},{5,1},{6,2},{7,3},{8,12},{9,13},{10,... | collective-permute-start | bytes 1327112 | tf_op jit(solution)/shard_map/ppermute | solution.py:154
  52.9 56.3 %collective-permute-start.20 = (bf16[288,768]{1,0:T(8,128)(2,1)S(1)}, bf16[288,768]{1,0:T(8,128)(2,1)S(1)}, u32[]{:S(2)}, u32[]{:S(2)}) collective-permute-start(bf16[288,768]{1,0:T(8,128)(2,1)S(1)} %get-tuple-element.18), channel_id=1, source_target_pairs={{0,6},{1,7},{2,4},{3,5},{4,2},{5,3},{6,0},{7,1},{8,14},{9,15},{10,... | collective-permute-start | bytes 1327112 | tf_op jit(solution)/shard_map/ppermute | solution.py:154
  68.8 27.6 %collective-permute-start.3 = (bf16[144,1536]{1,0:T(8,128)(2,1)S(1)}, bf16[144,1536]{1,0:T(8,128)(2,1)S(1)}, u32[]{:S(2)}, u32[]{:S(2)}) collective-permute-start(bf16[144,1536]{1,0:T(8,128)(2,1)S(1)} %pad_maximum_fusion.13), channel_id=1, source_target_pairs={{0,4},{1,5},{2,6},{3,7},{4,0},{5,1},{6,2},{7,3},{8,12},{9,13},{10,... | collective-permute-start | bytes 1327112 | tf_op jit(solution)/shard_map/ppermute | solution.py:154
  70.4 1.8 copy-start.4
  70.5 26.4 %collective-permute-start.4 = (bf16[144,1536]{1,0:T(8,128)(2,1)S(1)}, bf16[144,1536]{1,0:T(8,128)(2,1)S(1)}, u32[]{:S(2)}, u32[]{:S(2)}) collective-permute-start(bf16[144,1536]{1,0:T(8,128)(2,1)S(1)} %pad_maximum_fusion.14), channel_id=1, source_target_pairs={{0,2},{1,3},{2,0},{3,1},{4,6},{5,7},{6,4},{7,5},{8,10},{9,11},{10,... | collective-permute-start | bytes 1327112 | tf_op jit(solution)/shard_map/ppermute | solution.py:154
  71.2 2.0 copy-start.3
  96.4 12.0 %collective-permute-start.9 = (bf16[144,1536]{1,0:T(8,128)(2,1)S(1)}, bf16[144,1536]{1,0:T(8,128)(2,1)S(1)}, u32[]{:S(2)}, u32[]{:S(2)}) collective-permute-start(bf16[144,1536]{1,0:T(8,128)(2,1)S(1)} %pad_maximum_fusion.16), channel_id=1, source_target_pairs={{0,2},{1,3},{2,0},{3,1},{4,6},{5,7},{6,4},{7,5},{8,10},{9,11},{10,... | collective-permute-start | bytes 1327112 | tf_op jit(solution)/shard_map/ppermute | solution.py:154
  96.8 11.6 %collective-permute-start.8 = (bf16[144,1536]{1,0:T(8,128)(2,1)S(1)}, bf16[144,1536]{1,0:T(8,128)(2,1)S(1)}, u32[]{:S(2)}, u32[]{:S(2)}) collective-permute-start(bf16[144,1536]{1,0:T(8,128)(2,1)S(1)} %pad_maximum_fusion.15), channel_id=1, source_target_pairs={{0,4},{1,5},{2,6},{3,7},{4,0},{5,1},{6,2},{7,3},{8,12},{9,13},{10,... | collective-permute-start | bytes 1327112 | tf_op jit(solution)/shard_map/ppermute | solution.py:154
  108.4 9.7 %collective-permute-start.10 = (bf16[864,1536]{1,0:T(8,128)(2,1)S(1)}, bf16[864,1536]{1,0:T(8,128)(2,1)S(1)}, u32[]{:S(2)}, u32[]{:S(2)}) collective-permute-start(bf16[864,1536]{1,0:T(8,128)(2,1)S(1)} %fusion.19), channel_id=1, source_target_pairs={{0,1},{1,0},{2,3},{3,2},{4,5},{5,4},{6,7},{7,6},{8,9},{9,8},{10,11... | collective-permute-start | bytes 7962632 | tf_op jit(solution)/shard_map/ppermute | solution.py:154
  108.6 1.7 copy-start.9
  108.6 17.4 %collective-permute-start.11 = (bf16[864,1536]{1,0:T(8,128)(2,1)S(1)}, bf16[864,1536]{1,0:T(8,128)(2,1)S(1)}, u32[]{:S(2)}, u32[]{:S(2)}) collective-permute-start(bf16[864,1536]{1,0:T(8,128)(2,1)S(1)} %fusion.17), channel_id=1, source_target_pairs={{0,1},{1,0},{2,3},{3,2},{4,5},{5,4},{6,7},{7,6},{8,9},{9,8},{10,11... | collective-permute-start | bytes 7962632 | tf_op jit(solution)/shard_map/ppermute | solution.py:154
  109.4 8.7 %collective-permute-start.21 = (bf16[864,384]{1,0:T(8,128)(2,1)S(1)}, bf16[864,384]{1,0:T(8,128)(2,1)S(1)}, u32[]{:S(2)}, u32[]{:S(2)}) collective-permute-start(bf16[864,384]{1,0:T(8,128)(2,1)S(1)} %slice.389), channel_id=1, source_target_pairs={{0,1},{1,0},{2,3},{3,2},{4,5},{5,4},{6,7},{7,6},{8,9},{9,8},{10,11... | collective-permute-start | bytes 1990664 | tf_op jit(solution)/shard_map/ppermute | solution.py:154
  121.1 17.0 %collective-permute-start.22 = (bf16[384,768]{1,0:T(8,128)(2,1)S(1)}, bf16[384,768]{1,0:T(8,128)(2,1)S(1)}, u32[]{:S(2)}, u32[]{:S(2)}) collective-permute-start(bf16[384,768]{1,0:T(8,128)(2,1)S(1)} %get-tuple-element.26), channel_id=1, source_target_pairs={{0,8},{24,16},{1,9},{25,17},{2,10},{26,18},{3,11},{27,19},{4,12},{... | collective-permute-start | bytes 1769480 | tf_op jit(solution)/shard_map/ppermute | solution.py:137
  124.5 26.3 %collective-permute-start.25 = (bf16[384,768]{1,0:T(8,128)(2,1)S(1)}, bf16[384,768]{1,0:T(8,128)(2,1)S(1)}, u32[]{:S(2)}, u32[]{:S(2)}) collective-permute-start(bf16[384,768]{1,0:T(8,128)(2,1)S(1)} %get-tuple-element.27), channel_id=1, source_target_pairs={{0,8},{24,16},{1,9},{25,17},{2,10},{26,18},{3,11},{27,19},{4,12},{... | collective-permute-start | bytes 1769480 | tf_op jit(solution)/shard_map/ppermute | solution.py:137
  129.1 5.7 %collective-permute-start.12 = (bf16[864,384]{1,0:T(8,128)(2,1)S(1)}, bf16[864,384]{1,0:T(8,128)(2,1)S(1)}, u32[]{:S(2)}, u32[]{:S(2)}) collective-permute-start(bf16[864,384]{1,0:T(8,128)(2,1)S(1)} %fusion.3), channel_id=1, source_target_pairs={{0,1},{1,0},{2,3},{3,2},{4,5},{5,4},{6,7},{7,6},{8,9},{9,8},{10,11... | collective-permute-start | bytes 1990664 | tf_op jit(solution)/shard_map/ppermute | solution.py:154
  132.1 31.2 %collective-permute-start.28 = (bf16[384,768]{1,0:T(8,128)(2,1)S(1)}, bf16[384,768]{1,0:T(8,128)(2,1)S(1)}, u32[]{:S(2)}, u32[]{:S(2)}) collective-permute-start(bf16[384,768]{1,0:T(8,128)(2,1)S(1)} %get-tuple-element.30), channel_id=1, source_target_pairs={{0,8},{24,16},{1,9},{25,17},{2,10},{26,18},{3,11},{27,19},{4,12},{... | collective-permute-start | bytes 1769480 | tf_op jit(solution)/shard_map/ppermute | solution.py:137
  133.5 41.7 %collective-permute-start.31 = (bf16[384,768]{1,0:T(8,128)(2,1)S(1)}, bf16[384,768]{1,0:T(8,128)(2,1)S(1)}, u32[]{:S(2)}, u32[]{:S(2)}) collective-permute-start(bf16[384,768]{1,0:T(8,128)(2,1)S(1)} %get-tuple-element.31), channel_id=1, source_target_pairs={{0,8},{24,16},{1,9},{25,17},{2,10},{26,18},{3,11},{27,19},{4,12},{... | collective-permute-start | bytes 1769480 | tf_op jit(solution)/shard_map/ppermute | solution.py:137
  135.1 41.2 %collective-permute-start.13 = (bf16[288,768]{1,0:T(8,128)(2,1)S(1)}, bf16[288,768]{1,0:T(8,128)(2,1)S(1)}, u32[]{:S(2)}, u32[]{:S(2)}) collective-permute-start(bf16[288,768]{1,0:T(8,128)(2,1)S(1)} %get-tuple-element.50), channel_id=1, source_target_pairs={{0,2},{1,3},{2,0},{3,1},{4,6},{5,7},{6,4},{7,5},{8,10},{9,11},{10,... | collective-permute-start | bytes 1327112 | tf_op jit(solution)/shard_map/ppermute | solution.py:154
  138.1 38.9 %collective-permute-start.14 = (bf16[288,768]{1,0:T(8,128)(2,1)S(1)}, bf16[288,768]{1,0:T(8,128)(2,1)S(1)}, u32[]{:S(2)}, u32[]{:S(2)}) collective-permute-start(bf16[288,768]{1,0:T(8,128)(2,1)S(1)} %get-tuple-element.51), channel_id=1, source_target_pairs={{0,4},{1,5},{2,6},{3,7},{4,0},{5,1},{6,2},{7,3},{8,12},{9,13},{10,... | collective-permute-start | bytes 1327112 | tf_op jit(solution)/shard_map/ppermute | solution.py:154
  150.7 26.9 %collective-permute-start.15 = (bf16[288,768]{1,0:T(8,128)(2,1)S(1)}, bf16[288,768]{1,0:T(8,128)(2,1)S(1)}, u32[]{:S(2)}, u32[]{:S(2)}) collective-permute-start(bf16[288,768]{1,0:T(8,128)(2,1)S(1)} %pad_maximum_fusion.12), channel_id=1, source_target_pairs={{0,6},{1,7},{2,4},{3,5},{4,2},{5,3},{6,0},{7,1},{8,14},{9,15},{10,... | collective-permute-start | bytes 1327112 | tf_op jit(solution)/shard_map/ppermute | solution.py:154
  163.4 14.8 %collective-permute-start.23 = (bf16[384,768]{1,0:T(8,128)(2,1)S(1)}, bf16[384,768]{1,0:T(8,128)(2,1)S(1)}, u32[]{:S(2)}, u32[]{:S(2)}) collective-permute-start(bf16[384,768]{1,0:T(8,128)(2,1)S(1)} %get-tuple-element.24), channel_id=1, source_target_pairs={{8,16},{16,8},{9,17},{17,9},{10,18},{18,10},{11,19},{19,11},{12,20... | collective-permute-start | bytes 1769480 | tf_op jit(solution)/shard_map/ppermute | solution.py:139
  175.2 4.4 %collective-permute-start.26 = (bf16[384,768]{1,0:T(8,128)(2,1)S(1)}, bf16[384,768]{1,0:T(8,128)(2,1)S(1)}, u32[]{:S(2)}, u32[]{:S(2)}) collective-permute-start(bf16[384,768]{1,0:T(8,128)(2,1)S(1)} %get-tuple-element.25), channel_id=1, source_target_pairs={{8,16},{16,8},{9,17},{17,9},{10,18},{18,10},{11,19},{19,11},{12,20... | collective-permute-start | bytes 1769480 | tf_op jit(solution)/shard_map/ppermute | solution.py:139
  176.2 4.8 %collective-permute-start.29 = (bf16[384,768]{1,0:T(8,128)(2,1)S(1)}, bf16[384,768]{1,0:T(8,128)(2,1)S(1)}, u32[]{:S(2)}, u32[]{:S(2)}) collective-permute-start(bf16[384,768]{1,0:T(8,128)(2,1)S(1)} %get-tuple-element.28), channel_id=1, source_target_pairs={{8,16},{16,8},{9,17},{17,9},{10,18},{18,10},{11,19},{19,11},{12,20... | collective-permute-start | bytes 1769480 | tf_op jit(solution)/shard_map/ppermute | solution.py:139
  177.0 5.5 %collective-permute-start.32 = (bf16[384,768]{1,0:T(8,128)(2,1)S(1)}, bf16[384,768]{1,0:T(8,128)(2,1)S(1)}, u32[]{:S(2)}, u32[]{:S(2)}) collective-permute-start(bf16[384,768]{1,0:T(8,128)(2,1)S(1)} %get-tuple-element.29), channel_id=1, source_target_pairs={{8,16},{16,8},{9,17},{17,9},{10,18},{18,10},{11,19},{19,11},{12,20... | collective-permute-start | bytes 1769480 | tf_op jit(solution)/shard_map/ppermute | solution.py:139
  177.7 6.4 %collective-permute-start.16 = (bf16[96,3072]{1,0:T(8,128)(2,1)S(1)}, bf16[96,3072]{1,0:T(8,128)(2,1)S(1)}, u32[]{:S(2)}, u32[]{:S(2)}) collective-permute-start(bf16[96,3072]{1,0:T(8,128)(2,1)S(1)} %pad_maximum_fusion.6), channel_id=1, source_target_pairs={{0,1},{1,0},{2,3},{3,2},{4,5},{5,4},{6,7},{7,6},{8,9},{9,8},{10,11... | collective-permute-start | bytes 1769480 | tf_op jit(solution)/shard_map/ppermute | solution.py:154
  178.3 25.2 %collective-permute-start.24 = (bf16[384,768]{1,0:T(8,128)(2,1)S(1)}, bf16[384,768]{1,0:T(8,128)(2,1)S(1)}, u32[]{:S(2)}, u32[]{:S(2)}) collective-permute-start(bf16[384,768]{1,0:T(8,128)(2,1)S(1)} %add_convert_fusion.6), channel_id=1, source_target_pairs={{8,0},{16,24},{9,1},{17,25},{10,2},{18,26},{11,3},{19,27},{12,4},{... | collective-permute-start | bytes 1769480 | tf_op jit(solution)/shard_map/ppermute | solution.py:141
  179.7 36.4 %collective-permute-start.27 = (bf16[384,768]{1,0:T(8,128)(2,1)S(1)}, bf16[384,768]{1,0:T(8,128)(2,1)S(1)}, u32[]{:S(2)}, u32[]{:S(2)}) collective-permute-start(bf16[384,768]{1,0:T(8,128)(2,1)S(1)} %add_convert_fusion.4), channel_id=1, source_target_pairs={{8,0},{16,24},{9,1},{17,25},{10,2},{18,26},{11,3},{19,27},{12,4},{... | collective-permute-start | bytes 1769480 | tf_op jit(solution)/shard_map/ppermute | solution.py:141
  181.2 47.5 %collective-permute-start.30 = (bf16[384,768]{1,0:T(8,128)(2,1)S(1)}, bf16[384,768]{1,0:T(8,128)(2,1)S(1)}, u32[]{:S(2)}, u32[]{:S(2)}) collective-permute-start(bf16[384,768]{1,0:T(8,128)(2,1)S(1)} %add_convert_fusion.2), channel_id=1, source_target_pairs={{8,0},{16,24},{9,1},{17,25},{10,2},{18,26},{11,3},{19,27},{12,4},{... | collective-permute-start | bytes 1769480 | tf_op jit(solution)/shard_map/ppermute | solution.py:141
  182.7 1.7 copy-start.1
  182.7 58.5 %collective-permute-start.33 = (bf16[384,768]{1,0:T(8,128)(2,1)S(1)}, bf16[384,768]{1,0:T(8,128)(2,1)S(1)}, u32[]{:S(2)}, u32[]{:S(2)}) collective-permute-start(bf16[384,768]{1,0:T(8,128)(2,1)S(1)} %add_convert_fusion), channel_id=1, source_target_pairs={{8,0},{16,24},{9,1},{17,25},{10,2},{18,26},{11,3},{19,27},{12,4},{... | collective-permute-start | bytes 1769480 | tf_op jit(solution)/shard_map/ppermute | solution.py:141
where the time goes:
time: 245 us; the launch traced here: 244 us
  waiting for transfers between devices  138 us (56%)
  starting transfers between devices  37.4 us (15%)
  Pallas kernels  31.2 us (13%)
  local copies, waits for them, and re-layouts  14.5 us (6%)
  matrix products  12 us (5%)
  other arithmetic  9.49 us (4%)
    ppermute x22, waiting for transfers between devices, swap(): return lax.ppermute(a, 'fsdp', [(f, f ^ mask) for f in range(8)])  63.6 us
    ppermute x4, waiting for transfers between devices, sum_over_line(): arrived = lax.ppermute(total, 'rep', [(1, 0), (2, 3)])  40.9 us
    ppermute x4, waiting for transfers between devices, sum_over_line(): arrived = lax.ppermute(part, 'rep', [(0, 1), (3, 2)])  33.6 us
    ppermute x22, starting transfers between devices, swap(): return lax.ppermute(a, 'fsdp', [(f, f ^ mask) for f in range(8)])  21.8 us
    pallas_call x1, Pallas kernels, forward(): pl.pallas_call(forward_kernel, grid_spec=pltpu.PrefetchScalarGridSpec(num...  15.7 us
    pallas_call x1, Pallas kernels, backward(): pl.pallas_call(backward_kernel, grid_spec=pltpu.PrefetchScalarGridSpec(nu...  15.5 us
    dot_general x8, matrix products, dot(): lax.dot_general(a, b, (((a_dim,), (b_dim,)), ((), ())), preferred_element...  12 us
    unnamed x46, local copies, waits for them, and re-layouts  9.3 us
  transfers between devices with their start and end apart: 34, of which 14 were waited for; matrix products, arithmetic and copies ran while one was open for 9% of the time, Pallas kernels for 6%

commit v1 on v0

v1 whole, which is shorter than its diff:
```python
import functools
import math

import jax
import jax.numpy as jnp
from jax import lax
from jax.experimental import pallas as pl
from jax.experimental.pallas import tpu as pltpu
from jax.sharding import PartitionSpec as P

E = 128
BLOCK_HEADS = 3
BLOCK = BLOCK_HEADS * E
PAIR = 2 * BLOCK
PARTS = 3
F32 = jnp.float32
BF16 = jnp.bfloat16
LOG2_E = math.log2(math.e)
FAR = -1e30
VMEM_LIMIT = 24 * 1024 * 1024
ATTENTION_VMEM_LIMIT = 40 * 1024 * 1024
NO_COST = pl.CostEstimate(flops=0, bytes_accessed=0, transcendentals=0)


def dot(a, b, a_dim, b_dim):
    return lax.dot_general(a, b, (((a_dim,), (b_dim,)), ((), ())), preferred_element_type=F32)


def forward_kernel(order, ids_column, ids_row, query, key, value, attended, there, weights, bias):
    @pl.when(pl.program_id(0) == 0)
    def _():
        allowed = (ids_column[...] == ids_row[...]) & (ids_column[...] >= 0)
        bias[...] = jnp.where(allowed, 0.0, FAR)

    scale = LOG2_E / math.sqrt(E)
    columns = [slice(head * E, (head + 1) * E) for head in range(BLOCK_HEADS)]
    logits = [dot(key[:, c], query[:, c], 1, 1) * scale + bias[...] for c in columns]
    halves = []
    for head in range(BLOCK_HEADS):
        top = jnp.maximum(jnp.max(logits[head], axis=0, keepdims=True), 0.5 * FAR)
        raw = jnp.exp2(logits[head] - top)
        total = jnp.sum(raw, axis=0, keepdims=True)
        half = (raw * (1.0 / jnp.maximum(total, 0.5))).astype(BF16)
        weights[head] = half
        halves.append(half)
    for head in range(BLOCK_HEADS):
        attended[:, columns[head]] = dot(halves[head], value[:, columns[head]], 0, 0).astype(BF16)
    quarter = there.shape[0]
    start = pl.multiple_of((3 - order[0] % 2) * quarter, 32)
    there[...] = attended[pl.ds(start, quarter), :]


def forward(order, segment_ids, query_rows, key_rows, value_rows):
    rows = query_rows.shape[0]
    blocks = order.shape[0]
    heads = blocks * BLOCK_HEADS
    absolute = pl.BlockSpec((rows, BLOCK), lambda j, order: (0, order[j]))
    return pl.pallas_call(
        forward_kernel,
        grid_spec=pltpu.PrefetchScalarGridSpec(
            num_scalar_prefetch=1,
            grid=(blocks,),
            in_specs=[
                pl.BlockSpec((rows, 1), lambda j, order: (0, 0)),
                pl.BlockSpec((1, rows), lambda j, order: (0, 0)),
                absolute,
                absolute,
                absolute,
            ],
            out_specs=[
                pl.BlockSpec((rows, BLOCK), lambda j, order: (0, j)),
                pl.BlockSpec((rows // 4, BLOCK), lambda j, order: (0, j ^ 1)),
                pl.BlockSpec((BLOCK_HEADS, rows, rows), lambda j, order: (j, 0, 0)),
            ],
            scratch_shapes=[pltpu.VMEM((rows, rows), F32)],
        ),
        out_shape=[
            jax.ShapeDtypeStruct((rows, blocks * BLOCK), BF16),
            jax.ShapeDtypeStruct((rows // 4, blocks * BLOCK), BF16),
            jax.ShapeDtypeStruct((heads, rows, rows), BF16),
        ],
        compiler_params=pltpu.CompilerParams(vmem_limit_bytes=ATTENTION_VMEM_LIMIT),
        cost_estimate=NO_COST,
        name="attention_forward",
    )(order, segment_ids.reshape(rows, 1), segment_ids.reshape(1, rows), query_rows, key_rows, value_rows)


def backward_kernel(order, grad_main, grad_here, grad_there, query, key, value, weights, *rest):
    grad_query, grad_key, grad_value = rest[-3:]
    first = order[0] % 2 == 0
    here, there = grad_here[...], grad_there[...]
    grad_all = jnp.concatenate(
        [grad_main[...], jnp.where(first, here, there), jnp.where(first, there, here)], axis=0
    )
    inverse_root = 1.0 / math.sqrt(E)
    for head in range(BLOCK_HEADS):
        columns = slice(head * E, (head + 1) * E)
        grad = grad_all[:, columns]
        half = weights[head]
        grad_probs = dot(value[:, columns], grad, 1, 1)
        wide = half.astype(F32)
        row_dot = jnp.sum(wide * grad_probs, axis=0, keepdims=True)
        grad_logits = (wide * (grad_probs - row_dot)).astype(BF16)
        grad_value[:, columns] = dot(half, grad, 1, 0).astype(BF16)
        grad_key[:, columns] = (dot(grad_logits, query[:, columns], 1, 0) * inverse_root).astype(BF16)
        grad_query[:, columns] = (dot(grad_logits, key[:, columns], 0, 0) * inverse_root).astype(BF16)


def backward(order, grad, there, flip, there_skip, query_rows, key_rows, value_rows, weights, skip, done):
    rows, width = query_rows.shape
    quarter = there.shape[0]
    blocks = order.shape[0]
    heads = blocks * BLOCK_HEADS
    absolute = pl.BlockSpec((rows, BLOCK), lambda j, order: (0, order[j]))
    shapes = [jax.ShapeDtypeStruct((rows, width), BF16)] * 3
    return pl.pallas_call(
        backward_kernel,
        grid_spec=pltpu.PrefetchScalarGridSpec(
            num_scalar_prefetch=1,
            grid=(blocks,),
            in_specs=[
                pl.BlockSpec((2 * quarter, BLOCK), lambda j, order: (0, j)),
                pl.BlockSpec((quarter, BLOCK), lambda j, order: (2, j)),
                pl.BlockSpec((quarter, BLOCK), lambda j, order: (0, (j ^ flip) + there_skip)),
                absolute,
                absolute,
                absolute,
                pl.BlockSpec((BLOCK_HEADS, rows, rows), lambda j, order: (j + skip, 0, 0)),
            ]
            + [pl.BlockSpec(memory_space=pl.ANY)] * len(done),
            out_specs=[absolute, absolute, absolute],
        ),
        out_shape=shapes,
        input_output_aliases={8 + i: i for i in range(len(done))},
        compiler_params=pltpu.CompilerParams(vmem_limit_bytes=ATTENTION_VMEM_LIMIT),
        cost_estimate=NO_COST,
        name="attention_backward",
    )(order, grad, grad, there, query_rows, key_rows, value_rows, weights, *done)


def whole(kernel, shapes, *arrays, scalars=(), name):
    vmem, smem = pl.BlockSpec(memory_space=pltpu.VMEM), pl.BlockSpec(memory_space=pltpu.SMEM)
    return pl.pallas_call(
        kernel,
        in_specs=[smem] * len(scalars) + [vmem] * len(arrays),
        out_specs=[vmem] * len(shapes),
        out_shape=[jax.ShapeDtypeStruct(shape, BF16) for shape in shapes],
        compiler_params=pltpu.CompilerParams(vmem_limit_bytes=VMEM_LIMIT),
        cost_estimate=NO_COST,
        name=name,
    )(*scalars, *arrays)


def other_quarter_kernel(blocks, ids, extra, out):
    is_full = ids[ids.shape[0] - 1] >= 0
    out[...] = jnp.where(is_full, extra[...], jnp.zeros((), BF16))


def other_quarter(blocks, ids, rows):
    count, width = rows.shape
    quarter = count // 4
    return pl.pallas_call(
        other_quarter_kernel,
        grid_spec=pltpu.PrefetchScalarGridSpec(
            num_scalar_prefetch=2,
            grid=(1,),
            in_specs=[pl.BlockSpec((quarter, width), lambda i, blocks, ids: (3 - blocks[0] % 2, 0))],
            out_specs=pl.BlockSpec((quarter, width), lambda i, blocks, ids: (0, 0)),
        ),
        out_shape=jax.ShapeDtypeStruct((quarter, width), BF16),
        compiler_params=pltpu.CompilerParams(vmem_limit_bytes=ATTENTION_VMEM_LIMIT),
        cost_estimate=NO_COST,
        name="other_quarter",
    )(blocks, ids, rows)


def gather_start_kernel(blocks, ids, rows, arrived, *outs):
    quarter = arrived.shape[0]
    short, cut = 2 * quarter, quarter // 2
    is_full = ids[ids.shape[0] - 1] >= 0
    start = pl.multiple_of(short + quarter * (blocks[0] % 2), 32)
    own = jnp.where(is_full, rows[pl.ds(start, quarter), :], jnp.zeros((), BF16))
    here = own + arrived[...]
    width = outs[0].shape[1]
    for part in range(len(outs) // 2):
        columns = slice(part * width, (part + 1) * width)
        for i in range(2):
            outs[2 * part + i][:short] = rows[:short, columns]
            outs[2 * part + i][short:] = here[i * cut : (i + 1) * cut, columns]


def gather_forward_kernel(to_x, to_y, from_x, from_y, next_y, next_x):
    quarter = from_x.shape[0] * 2 // 5
    short = 2 * quarter
    next_y[:quarter] = from_x[:quarter]
    next_x[:quarter] = from_y[quarter:short]
    next_y[quarter:] = to_x[short:] + from_x[short:]
    next_x[quarter:] = to_y[short:] + from_y[short:]


def gather_end_kernel(to_x, from_x, from_y, next_y, next_x, via_y, via_x, plane):
    quarter = to_x.shape[0] * 2 // 5
    short, cut = 2 * quarter, quarter // 2
    plane[:short] = to_x[:short]
    plane[short : 2 * short] = from_x[:short]
    plane[2 * short : 3 * short] = from_y[:short]
    plane[3 * short : 3 * short + quarter] = via_y[:quarter]
    plane[3 * short + quarter : 4 * short] = via_x[:quarter]
    plane[4 * short : 4 * short + cut] = next_y[quarter:] + via_y[quarter:]
    plane[4 * short + cut :] = next_x[quarter:] + via_x[quarter:]


def pack_kernel(blocks, attended, arrived, *outs):
    quarter = arrived.shape[0]
    short = 2 * quarter
    start = pl.multiple_of(short + quarter * (blocks[0] % 2), 32)
    extra = attended[pl.ds(start, quarter), :] + arrived[...]
    for i, out in enumerate(outs):
        columns = slice(i * PAIR, (i + 1) * PAIR)
        out[:short] = attended[:short, columns]
        out[short:] = extra[:, columns]


def collect_kernel(kept, from_x, from_y, from_far, gathered):
    short = kept.shape[0] * 2 // 3
    parts = [kept, from_x, from_y, from_far]
    for i, part in enumerate(parts):
        gathered[i * short : (i + 1) * short] = part[:short]
    gathered[4 * short :] = (kept[short:] + from_x[short:]) + (from_y[short:] + from_far[short:])


def term_other_kernel(attended, plane, *outs):
    share = dot(attended[:, BLOCK:], plane[...], 0, 0).astype(BF16)
    width = share.shape[1] // len(outs)
    for i, out in enumerate(outs):
        out[...] = share[:, i * width : (i + 1) * width]


def term_own_kernel(attended, plane, left, right, *outs):
    own = dot(attended[:, :BLOCK], plane[...], 0, 0)
    width = left.shape[1]
    total = [(own[:, :width] + left[...].astype(F32)).astype(BF16), (own[:, width:] + right[...].astype(F32)).astype(BF16)]
    for i in range(2):
        if len(outs) == 2:
            outs[i][...] = total[i]
        else:
            outs[0][:, i * width : (i + 1) * width] = total[i]


def grad_kernel(plane, own, other, *rest):
    for i, weight in enumerate((own, other)):
        columns = slice(i * BLOCK, (i + 1) * BLOCK)
        share = dot(plane[...], weight[...], 1, 1)
        if len(rest) == 2:
            share = rest[0][:, columns] + share
        rest[-1][:, columns] = share


def grad_end_kernel(plane, own, other, before, *pieces):
    rows = pieces[0].shape[0]
    short = rows * 2 // 3
    for i, weight in enumerate((own, other)):
        columns = slice(i * BLOCK, (i + 1) * BLOCK)
        total = (before[:, columns] + dot(plane[...], weight[...], 1, 1)).astype(BF16)
        for j, piece in enumerate(pieces):
            piece[:short, columns] = total[j * short : (j + 1) * short]
            piece[short:, columns] = total[4 * short :]


def grad_part(part, plane, own_weight, other_weight, before):
    count, width = plane.shape
    weight = pl.BlockSpec((BLOCK, width), lambda i: (0, part))
    result = pl.BlockSpec((count, PAIR), lambda i: (0, 0))
    last = part == PARTS - 1
    rows = count // 3
    piece = pl.BlockSpec((rows, PAIR), lambda i: (0, 0))
    return pl.pallas_call(
        grad_end_kernel if last else grad_kernel,
        grid=(1,),
        in_specs=[pl.BlockSpec((count, width), lambda i: (0, 0)), weight, weight] + [result] * len(before),
        out_specs=[piece] * 4 if last else [result],
        out_shape=[jax.ShapeDtypeStruct((rows, PAIR), BF16)] * 4
        if last
        else [jax.ShapeDtypeStruct((count, PAIR), F32)],
        compiler_params=pltpu.CompilerParams(vmem_limit_bytes=VMEM_LIMIT),
        cost_estimate=NO_COST,
        name="grad_attended",
    )(plane, own_weight, other_weight, *before)


def add_kernel(a, b, out):
    out[...] = (a[...].astype(F32) + b[...].astype(F32)).astype(BF16)


class Order:
    def __init__(self):
        self.last = ()

    def __call__(self, *arrays):
        held = lax.optimization_barrier((*self.last, *arrays))[len(self.last) :]
        return held[0] if len(held) == 1 else held

    def mark(self, *arrays):
        self.last = tuple(arrays)


def add(a, b):
    return whole(add_kernel, [a.shape], a, b, name="add")[0]


def line_end_kernel(scale, place, total, arrived, *rest):
    in_middle = (place[0] == 1) | (place[0] == 2)
    rest[-1][...] = jnp.where(in_middle, total[...], arrived[...]).astype(F32) * scale


def line_end(scale, place, total, arrived, start, all_width, done):
    rows, width = total.shape
    piece = pl.BlockSpec((rows, width), lambda i, place: (0, 0))
    return pl.pallas_call(
        functools.partial(line_end_kernel, scale),
        grid_spec=pltpu.PrefetchScalarGridSpec(
            num_scalar_prefetch=1,
            grid=(1,),
            in_specs=[piece, piece] + [pl.BlockSpec(memory_space=pl.ANY)] * len(done),
            out_specs=pl.BlockSpec((rows, width), lambda i, place: (0, start // width)),
        ),
        out_shape=jax.ShapeDtypeStruct((rows, all_width), F32),
        input_output_aliases={3 + i: i for i in range(len(done))},
        compiler_params=pltpu.CompilerParams(vmem_limit_bytes=VMEM_LIMIT),
        cost_estimate=NO_COST,
        name="line_end",
    )(place, total, arrived, *done)


class LineSum:
    def __init__(self, order, scale, width):
        self.order, self.scale, self.width = order, scale, width
        self.place = lax.axis_index("rep").astype(jnp.int32).reshape(1)
        self.held, self.arriving, self.done = {}, {}, ()

    def start(self, piece, part):
        self.held[piece] = part
        self.arriving[piece] = lax.ppermute(part, "rep", [(0, 1), (3, 2)])

    def across(self, piece):
        part, arrived = self.order(self.held[piece], self.arriving[piece])
        pair = add(part, arrived)
        self.order.mark(pair)
        self.held[piece] = pair
        self.arriving[piece] = lax.ppermute(pair, "rep", [(1, 2), (2, 1)])

    def back(self, piece):
        pair, arrived = self.order(self.held[piece], self.arriving[piece])
        total = add(pair, arrived)
        self.order.mark(total)
        self.held[piece] = total
        self.arriving[piece] = lax.ppermute(total, "rep", [(1, 0), (2, 3)])

    def finish(self, piece, start):
        held = self.order(self.held[piece], self.arriving[piece], *self.done)
        result = line_end(self.scale, self.place, held[0], held[1], start, self.width, held[2:])
        self.order.mark(result)
        self.done = (result,)


def pairwise(query_rows, key_rows, value_rows, out_grad, out_weight, segment_ids):
    rows, width = query_rows.shape
    short = rows // 2
    quarter = short // 2
    cut = quarter // 2
    part_width = width // PARTS
    me = lax.axis_index("fsdp")
    core = me % 2
    blocks = me ^ jnp.arange(8, dtype=jnp.int32)
    order = Order()
    line = LineSum(order, 1.0 / math.sqrt(rows * lax.axis_size("fsdp") * lax.axis_size("rep")), width)

    def swap(a, mask):
        return lax.ppermute(a, "fsdp", [(f, f ^ mask) for f in range(8)])

    other_weight = swap(out_weight, 1)

    there = other_quarter(blocks, segment_ids, out_grad)
    order.mark(there)
    arrived_extra = swap(there, 1)

    ids, rows_held, arrived = order(segment_ids, out_grad, arrived_extra)
    shape = (short + cut, part_width)
    to_send = whole(
        gather_start_kernel, [shape] * (2 * PARTS), rows_held, arrived, scalars=(blocks, ids), name="gather_start"
    )
    order.mark(*to_send)
    gather = {}

    def gather_start(part):
        to_x, to_y = order(*to_send[2 * part : 2 * part + 2])
        gather[part] = to_x, to_y, swap(to_x, 2), swap(to_y, 4)

    def gather_forward(part, *also):
        to_x, to_y, from_x, from_y, *also = order(*gather[part], *also)
        shape = (quarter + cut, part_width)
        next_y, next_x = whole(
            gather_forward_kernel, [shape] * 2, to_x, to_y, from_x, from_y, name="gather_forward"
        )
        order.mark(next_y, next_x, *also)
        gather[part] = to_x, from_x, from_y, next_y, next_x, swap(next_y, 4), swap(next_x, 2)
        return also

    def gather_end(part):
        held = order(*gather[part])
        (plane,) = whole(gather_end_kernel, [(4 * short + quarter, part_width)], *held, name="gather_end")
        order.mark(plane)
        return plane

    def grad_step(part, plane, before):
        held = order(plane, out_weight, other_weight, *before)
        share = grad_part(part, *held[:3], held[3:])
        order.mark(*share)
        return share

    def term_other(plane, attended):
        plane, attended = order(plane, attended)
        shape = (BLOCK, part_width // 2)
        share = whole(term_other_kernel, [shape] * 2, attended, plane, name="term_other")
        order.mark(*share)
        return [swap(half, 1) for half in share]

    def term_own(plane, attended, arrived, pieces=1):
        held = order(attended, plane, *arrived)
        shape = (BLOCK, part_width // pieces)
        total = whole(term_own_kernel, [shape] * pieces, *held, name="term_own")
        order.mark(*total)
        return total

    def attend(half):
        held = order(segment_ids, query_rows, key_rows, value_rows)
        attended, there, weights = forward(blocks[4 * half : 4 * half + 4], *held)
        order.mark(attended, there)
        return attended, weights, swap(there, 1)

    def pack(attended, arrived):
        attended, arrived = order(attended, arrived)
        shape = (short + quarter, PAIR)
        packed = whole(pack_kernel, [shape] * 2, attended, arrived, scalars=(blocks,), name="pack")
        order.mark(*packed)
        return packed

    gather_start(0)
    near, weights_near, near_arriving = attend(0)
    far, weights_far, far_arriving = attend(1)
    (other_weight,) = gather_forward(0, other_weight)

    kept, to_x = pack(near, near_arriving)
    from_x = swap(to_x, 2)
    to_y, to_far = pack(far, far_arriving)
    arriving = from_x, swap(to_y, 4), swap(to_far, 6)
    plane = gather_end(0)
    held = order(kept, *arriving)
    (gathered,) = whole(collect_kernel, [(4 * short + quarter, PAIR)], *held, name="collect")
    order.mark(gathered)

    arriving = term_other(plane, gathered)
    gather_start(1)
    line.start(0, *term_own(plane, gathered, arriving))
    grad = grad_step(0, plane, ())
    gather_forward(1)
    plane = gather_end(1)
    arriving = term_other(plane, gathered)
    gather_start(2)
    grad = grad_step(1, plane, grad)
    line.across(0)
    line.start(1, *term_own(plane, gathered, arriving))
    gather_forward(2)
    plane = gather_end(2)
    arriving = term_other(plane, gathered)
    piece = grad_step(2, plane, grad)
    moved_x, moved_y = swap(piece[1], 2), swap(piece[2], 4)
    line.back(0)
    line.across(1)
    last = term_own(plane, gathered, arriving, 2)
    line.start(2, last[0])

    own, moved_x, moved_y = order(piece[0], moved_x, moved_y)
    tails = jnp.concatenate([own[short:], moved_x[short:], moved_y[short:]], axis=1)
    order.mark(tails)
    line.start(3, order(last[1]))
    there = swap(tails, 1)
    moved_far = swap(order(piece[3]), 6)
    grads = ()

    def finish(i, grad, there, skip):
        weights = weights_near if i < 2 else weights_far
        held = order(grad, there, query_rows, key_rows, value_rows, weights)
        result = backward(blocks[2 * i : 2 * i + 2], held[0], held[1], 1, skip, *held[2:], 2 * (i % 2), grads)
        order.mark(*result)
        return tuple(result)

    grads = finish(0, own, there, 0)
    line.across(2)
    grads = finish(1, moved_x, there, 2)
    line.back(1)
    line.across(3)
    line.finish(0, 0)
    moved_far = order(moved_far)
    tail = moved_far[short:]
    order.mark(tail)
    far_there = swap(tail, 1)
    grads = finish(2, moved_y, there, 4)
    line.back(2)
    grads = finish(3, moved_far, far_there, 0)
    line.back(3)
    line.finish(1, part_width)
    line.finish(2, 2 * part_width)
    line.finish(3, 2 * part_width + part_width // 2)
    return (*grads, *line.done)


def general(query_rows, key_rows, value_rows, out_grad, out_weight, segment_ids):
    rows, width = query_rows.shape
    short = rows // 2
    count = lax.axis_size("fsdp")
    order = jnp.arange(width // BLOCK, dtype=jnp.int32)
    extra = jnp.where((segment_ids[short:] >= 0)[:, None], out_grad[short:], jnp.zeros((), BF16))
    attended, _, weights = forward(order, segment_ids, query_rows, key_rows, value_rows)
    live = jnp.concatenate(
        [lax.all_gather(out_grad[:short], "fsdp", axis=0, tiled=True), lax.psum(extra, "fsdp")]
    )
    attended_live = jnp.concatenate(
        [
            lax.all_to_all(attended[:short], "fsdp", split_axis=1, concat_axis=0, tiled=True),
            lax.psum_scatter(attended[short:], "fsdp", scatter_dimension=1, tiled=True),
        ]
    )
    term = dot(attended_live, live, 0, 0).astype(BF16)
    total = lax.psum(term, "rep").astype(F32)
    grad = dot(live, out_weight, 1, 1).astype(BF16)
    grad_main = lax.all_to_all(
        grad[: count * short], "fsdp", split_axis=0, concat_axis=1, tiled=True
    )
    grad_extra = lax.all_gather(grad[count * short :], "fsdp", axis=1, tiled=True)
    half = short // 2
    grad = jnp.concatenate([grad_main, grad_extra[:half]])
    there = grad_extra[half:]
    grads = backward(order, grad, there, 0, 0, query_rows, key_rows, value_rows, weights, 0, ())
    return (*grads, total * (1.0 / math.sqrt(rows * count * lax.axis_size("rep"))))


def solution(mesh):
    fits = mesh.shape["fsdp"] == 8 and mesh.shape["rep"] == 4
    split = P(("rep", "fsdp"), None)
    return jax.shard_map(
        pairwise if fits else general,
        mesh=mesh,
        in_specs=(split, split, split, split, P("fsdp", None), P(("rep", "fsdp"))),
        out_specs=(split, split, split, P("fsdp", None)),
        check_vma=False,
    )
```

time: 245 us -> 188 us (0.77)
  waiting for transfers between devices: 138 us -> 64.7 us
  Pallas kernels: 31.2 us -> 64.2 us
  starting transfers between devices: 37.4 us -> 49.7 us
  matrix products: 12 us -> 0 us
  other arithmetic: 9.49 us -> 0.03 us
  local copies, waits for them, and re-layouts: 14.5 us -> 7.34 us
    ppermute x12, waiting for transfers between devices: 74.5 us -> 14.7 us  [the longest x4 13.1 us: back(): self.arriving[piece] = lax.ppermute(total, 'rep', [(1, 0), (2, 3)])]
    pallas_call x0 -> x32, Pallas kernels: none -> 33.8 us  [the longest x24 15.4 us: whole(): pl.pallas_call(kernel, in_specs=[smem] * len(scalars) + [vmem] * len(arra...]
    ppermute x22 -> x30, waiting for transfers between devices: 63.6 us -> 49.9 us  [swap(): return lax.ppermute(a, 'fsdp', [(f, f ^ mask) for f in range(8)])]
    dot_general x8 -> x0, matrix products: 12 us -> none  [dot(): lax.dot_general(a, b, (((a_dim,), (b_dim,)), ((), ())), preferred_element...]
    ppermute x12, starting transfers between devices: 15.7 us -> 26.3 us  [the longest x4 16.9 us: start(): self.arriving[piece] = lax.ppermute(part, 'rep', [(0, 1), (3, 2)])]
    pallas_call x1 -> x2, Pallas kernels: 15.7 us -> 10.9 us  [forward(): pl.pallas_call(forward_kernel, grid_spec=pltpu.PrefetchScalarGridSpec(num...]
    pallas_call x1 -> x4, Pallas kernels: 15.5 us -> 19.6 us  [backward(): pl.pallas_call(backward_kernel, grid_spec=pltpu.PrefetchScalarGridSpec(nu...]
    concatenate x16 -> x1, other arithmetic: 3.73 us -> 0.03 us  [pairwise(): jnp.concatenate([own[short:], moved_x[short:], moved_y[short:]], axis=1)]
  transfers between devices with their start and end apart: 34 -> 42, of which waited for: 14 -> 14; matrix products, arithmetic and copies ran while one was open for 9% -> 1% of each run, Pallas kernels for 6% -> 33%
where the time goes in v1:
time: 188 us; the launch traced here: 187 us
  waiting for transfers between devices  64.7 us (34%)
  Pallas kernels  64.2 us (34%)
  starting transfers between devices  49.7 us (26%)
  local copies, waits for them, and re-layouts  7.34 us (4%)
    ppermute x30, waiting for transfers between devices, swap(): return lax.ppermute(a, 'fsdp', [(f, f ^ mask) for f in range(8)])  49.9 us
    ppermute x30, starting transfers between devices, swap(): return lax.ppermute(a, 'fsdp', [(f, f ^ mask) for f in range(8)])  23.4 us
    pallas_call x4, Pallas kernels, backward(): pl.pallas_call(backward_kernel, grid_spec=pltpu.PrefetchScalarGridSpec(nu...  19.6 us
    ppermute x4, starting transfers between devices, start(): self.arriving[piece] = lax.ppermute(part, 'rep', [(0, 1), (3, 2)])  16.9 us
    pallas_call x24, Pallas kernels, whole(): pl.pallas_call(kernel, in_specs=[smem] * len(scalars) + [vmem] * len(arra...  15.4 us
    ppermute x4, waiting for transfers between devices, back(): self.arriving[piece] = lax.ppermute(total, 'rep', [(1, 0), (2, 3)])  13.1 us
    pallas_call x2, Pallas kernels, forward(): pl.pallas_call(forward_kernel, grid_spec=pltpu.PrefetchScalarGridSpec(num...  10.9 us
    pallas_call x3, Pallas kernels, grad_part(): pl.pallas_call(grad_end_kernel if last else grad_kernel, grid=(1,), in_sp...  10.4 us
  transfers between devices with their start and end apart: 42, of which 14 were waited for; matrix products, arithmetic and copies ran while one was open for 1% of the time, Pallas kernels for 33%

profile of v1, /device:TPU:0, one launch (start us, length us, event | category | flops | bytes accessed | tf_op | source)
XLA Modules:
  0.0 187.2 jit_solution(10835394404817131447)
XLA Ops:
  1.2 1.7 copy-done.8
  4.3 1.9 %collective-permute-done.arrived = bf16[96,3072]{1,0:T(8,128)(2,1)S(1)} collective-permute-done((bf16[96,3072]{1,0:T(8,128)(2,1)S(1)}, bf16[96,3072]{1,0:T(8,128)(2,1)S(1)}, u32[]{:S(2)}, u32[]{:S(2)}) %collective-permute-start) | collective-permute-done | bytes 589856 | tf_op jit(solution)/shard_map/ppermute | solution.py:379
  7.0 2.9 %collective-permute-start.1 = (bf16[240,1024]{1,0:T(8,128)(2,1)S(1)}, bf16[240,1024]{1,0:T(8,128)(2,1)S(1)}, u32[]{:S(2)}, u32[]{:S(2)}) collective-permute-start(bf16[240,1024]{1,0:T(8,128)(2,1)S(1)} %get-tuple-element.233.to_x), channel_id=1, source_target_pairs={{0,2},{1,3},{2,0},{3,1},{4,6},{5,7},{6,4},{7,5},{8,10},{9,11},{10,... | collective-permute-start | bytes 1474568 | tf_op jit(solution)/shard_map/ppermute | solution.py:379
  9.8 1.5 collective-permute-start.2
  11.6 1.7 copy-done.3
  13.2 5.4 %attention_forward.2 = (bf16[384,1536]{1,0:T(8,128)(2,1)S(1)}, bf16[96,1536]{1,0:T(8,128)(2,1)S(1)}, bf16[12,384,384]{2,1,0:T(8,128)(2,1)S(1)}) custom-call(s32[4]{0:T(128)S(1)} %get-tuple-element.386.order, s32[384,1]{1,0:T(8,128)S(1)} %reshape.28.ids_column, s32[1,384]{1,0:T(1,128)S(1)} %reshape.25.ids_row, bf16[384,3072]{1,0:T(8,128)(2,1)S(1)} %copy-done, ...), custom_call_target="tpu_custom_call" | custom-call | tf_op jit(solution)/shard_map/attention_forward/pallas_call | solution.py:58
  18.9 5.4 %attention_forward.3 = (bf16[384,1536]{1,0:T(8,128)(2,1)S(1)}, bf16[96,1536]{1,0:T(8,128)(2,1)S(1)}, bf16[12,384,384]{2,1,0:T(8,128)(2,1)S(1)}) custom-call(s32[4]{0:T(128)S(1)} %get-tuple-element.387.order, s32[384,1]{1,0:T(8,128)S(1)} %reshape.29.ids_column, s32[1,384]{1,0:T(1,128)S(1)} %reshape.27.ids_row, bf16[384,3072]{1,0:T(8,128)(2,1)S(1)} %copy-done, ...), custom_call_target="tpu_custom_call" | custom-call | tf_op jit(solution)/shard_map/attention_forward/pallas_call | solution.py:58
  26.9 2.0 %collective-permute-start.9 = (bf16[288,768]{1,0:T(8,128)(2,1)S(1)}, bf16[288,768]{1,0:T(8,128)(2,1)S(1)}, u32[]{:S(2)}, u32[]{:S(2)}) collective-permute-start(bf16[288,768]{1,0:T(8,128)(2,1)S(1)} %get-tuple-element.231), channel_id=1, source_target_pairs={{0,4},{1,5},{2,6},{3,7},{4,0},{5,1},{6,2},{7,3},{8,12},{9,13},{10,... | collective-permute-start | bytes 1327112 | tf_op jit(solution)/shard_map/ppermute | solution.py:379
  28.8 1.5 collective-permute-start.8
  31.0 24.2 %collective-permute-done.6.via_y = bf16[144,1024]{1,0:T(8,128)(2,1)S(1)} collective-permute-done((bf16[144,1024]{1,0:T(8,128)(2,1)S(1)}, bf16[144,1024]{1,0:T(8,128)(2,1)S(1)}, u32[]{:S(2)}, u32[]{:S(2)}) %collective-permute-start.6) | collective-permute-done | bytes 294944 | tf_op jit(solution)/shard_map/ppermute | solution.py:379
  57.0 1.4 collective-permute-start.13
  60.0 3.5 %collective-permute-start.17 = (bf16[384,1024]{1,0:T(8,128)(2,1)S(1)}, bf16[384,1024]{1,0:T(8,128)(2,1)S(1)}, u32[]{:S(2)}, u32[]{:S(2)}) collective-permute-start(bf16[384,1024]{1,0:T(8,128)(2,1)S(1)} %term_own.3.a), channel_id=1, source_target_pairs={{0,8},{24,16},{1,9},{25,17},{2,10},{26,18},{3,11},{27,19},{4,12},{... | collective-permute-start | bytes 2359304 | tf_op jit(solution)/shard_map/ppermute | solution.py:343
  63.6 3.2 %grad_attended.3.rest_0_ = f32[864,768]{1,0:T(8,128)S(1)} custom-call(bf16[864,1024]{1,0:T(8,128)(2,1)S(1)} %gather_end.3.plane, bf16[384,3072]{1,0:T(8,128)(2,1)S(1)} %copy-done.5, bf16[384,3072]{1,0:T(8,128)(2,1)} %collective-permute-done.3.other), custom_call_target="tpu_custom_call" | custom-call | tf_op jit(solution)/shard_map/grad_attended/pallas_call | solution.py:277
  66.8 3.5 %collective-permute-done.13.from_x = bf16[240,1024]{1,0:T(8,128)(2,1)S(1)} collective-permute-done((bf16[240,1024]{1,0:T(8,128)(2,1)S(1)}, bf16[240,1024]{1,0:T(8,128)(2,1)S(1)}, u32[]{:S(2)}, u32[]{:S(2)}) %collective-permute-start.13) | collective-permute-done | bytes 491552 | tf_op jit(solution)/shard_map/ppermute | solution.py:379
  70.2 1.1 collective-permute-done.14.from_y
  72.0 1.5 collective-permute-start.16
  73.5 5.7 %collective-permute-done.15.via_y = bf16[144,1024]{1,0:T(8,128)(2,1)S(1)} collective-permute-done((bf16[144,1024]{1,0:T(8,128)(2,1)S(1)}, bf16[144,1024]{1,0:T(8,128)(2,1)S(1)}, u32[]{:S(2)}, u32[]{:S(2)}) %collective-permute-start.15) | collective-permute-done | bytes 294944 | tf_op jit(solution)/shard_map/ppermute | solution.py:379
  80.8 1.5 collective-permute-start.20
  83.4 3.2 %grad_attended.4.before = f32[864,768]{1,0:T(8,128)S(1)} custom-call(bf16[864,1024]{1,0:T(8,128)(2,1)S(1)} %gather_end.4.plane, bf16[384,3072]{1,0:T(8,128)(2,1)S(1)} %copy-done.5, bf16[384,3072]{1,0:T(8,128)(2,1)} %collective-permute-done.3.other, f32[864,768]{1,0:T(8,128)S(1)} %grad_attended.3.rest_0_), custom_call_target="tpu_custom_call" | custom-call | tf_op jit(solution)/shard_map/grad_attended/pallas_call | solution.py:277
  88.6 6.6 %collective-permute-start.25 = (bf16[384,1024]{1,0:T(8,128)(2,1)S(1)}, bf16[384,1024]{1,0:T(8,128)(2,1)S(1)}, u32[]{:S(2)}, u32[]{:S(2)}) collective-permute-start(bf16[384,1024]{1,0:T(8,128)(2,1)S(1)} %term_own.4.a), channel_id=1, source_target_pairs={{0,8},{24,16},{1,9},{25,17},{2,10},{26,18},{3,11},{27,19},{4,12},{... | collective-permute-start | bytes 2359304 | tf_op jit(solution)/shard_map/ppermute | solution.py:343
  95.3 1.4 collective-permute-start.22
  97.2 6.5 %collective-permute-done.22.via_y = bf16[144,1024]{1,0:T(8,128)(2,1)S(1)} collective-permute-done((bf16[144,1024]{1,0:T(8,128)(2,1)S(1)}, bf16[144,1024]{1,0:T(8,128)(2,1)S(1)}, u32[]{:S(2)}, u32[]{:S(2)}) %collective-permute-start.22) | collective-permute-done | bytes 294944 | tf_op jit(solution)/shard_map/ppermute | solution.py:379
  105.8 4.0 %grad_attended.5 = (bf16[288,768]{1,0:T(8,128)(2,1)S(1)}, bf16[288,768]{1,0:T(8,128)(2,1)S(1)}, bf16[288,768]{1,0:T(8,128)(2,1)S(1)}, bf16[288,768]{1,0:T(8,128)(2,1)}) custom-call(bf16[864,1024]{1,0:T(8,128)(2,1)S(1)} %gather_end.5.plane, bf16[384,3072]{1,0:T(8,128)(2,1)S(1)} %copy-done.5, bf16[384,3072]{1,0:T(8,128)(2,1)} %collective-permute-done.3.other, ...), custom_call_target="tpu_custom_call" | custom-call | tf_op jit(solution)/shard_map/grad_attended/pallas_call | solution.py:277
  110.5 1.4 collective-permute-start.29
  112.3 1.1 add.9.total
  115.4 4.8 %collective-permute-done.28.grad_main.grad_here = bf16[288,768]{1,0:T(8,128)(2,1)S(1)} collective-permute-done((bf16[288,768]{1,0:T(8,128)(2,1)S(1)}, bf16[288,768]{1,0:T(8,128)(2,1)S(1)}, u32[]{:S(2)}, u32[]{:S(2)}) %collective-permute-start.28) | collective-permute-done | bytes 442400 | tf_op jit(solution)/shard_map/ppermute | solution.py:379
  120.6 1.3 collective-permute-start.34
  121.9 5.4 %collective-permute-start.31 = (bf16[384,512]{1,0:T(8,128)(2,1)S(1)}, bf16[384,512]{1,0:T(8,128)(2,1)S(1)}, u32[]{:S(2)}, u32[]{:S(2)}) collective-permute-start(bf16[384,512]{1,0:T(8,128)(2,1)S(1)} %get-tuple-element.334.a), channel_id=1, source_target_pairs={{0,8},{24,16},{1,9},{25,17},{2,10},{26,18},{3,11},{27,19},{4,12},{... | collective-permute-start | bytes 1179656 | tf_op jit(solution)/shard_map/ppermute | solution.py:343
  127.4 1.3 collective-permute-start.33
  128.7 1.7 collective-permute-start.35
  130.5 4.7 %attention_backward.4 = (bf16[384,3072]{1,0:T(8,128)(2,1)}, bf16[384,3072]{1,0:T(8,128)(2,1)}, bf16[384,3072]{1,0:T(8,128)(2,1)}) custom-call(s32[2]{0:T(128)S(1)} %get-tuple-element.388.order, bf16[288,768]{1,0:T(8,128)(2,1)S(1)} %get-tuple-element.325.grad_main.grad_here, bf16[288,768]{1,0:T(8,128)(2,1)S(1)} %get-tuple-element.325.grad_main.grad_here, ...), custom_call_target="tpu_custom_call" | custom-call | tf_op jit(solution)/shard_map/attention_backward/pallas_call | solution.py:116
  135.2 1.6 collective-permute-done.31.b
  137.7 1.4 collective-permute-start.36
  139.1 4.7 %attention_backward.5 = (bf16[384,3072]{1,0:T(8,128)(2,1)}, bf16[384,3072]{1,0:T(8,128)(2,1)}, bf16[384,3072]{1,0:T(8,128)(2,1)}) custom-call(s32[2]{0:T(128)S(1)} %get-tuple-element.389.order, bf16[288,768]{1,0:T(8,128)(2,1)S(1)} %collective-permute-done.28.grad_main.grad_here, ...), custom_call_target="tpu_custom_call", output_to_operand_aliasing={{0}: (8, {}), {1}: (9, {}), {2}: (10, {})} | custom-call | tf_op jit(solution)/shard_map/attention_backward/pallas_call | solution.py:116
  143.9 1.1 add.12.total
  145.0 1.3 collective-permute-start.41
  147.1 1.4 collective-permute-start.38
  148.5 2.8 %line_end.4.rest_0_ = f32[384,3072]{1,0:T(8,128)} custom-call(s32[1]{0:T(128)} %bitcast.place, bf16[384,1024]{1,0:T(8,128)(2,1)} %add.9.total, bf16[384,1024]{1,0:T(8,128)(2,1)} %collective-permute-done.34.arrived), custom_call_target="tpu_custom_call" | custom-call | tf_op jit(solution)/shard_map/line_end/pallas_call | solution.py:319
  152.3 2.0 %copy-done.7 = bf16[12,384,384]{2,1,0:T(8,128)(2,1)S(1)} copy-done((bf16[12,384,384]{2,1,0:T(8,128)(2,1)S(1)}, bf16[12,384,384]{2,1,0:T(8,128)(2,1)}, u32[]{:S(2)}) %copy-start.7) | copy-done | bytes 3538968
  154.3 4.7 %attention_backward.6 = (bf16[384,3072]{1,0:T(8,128)(2,1)}, bf16[384,3072]{1,0:T(8,128)(2,1)}, bf16[384,3072]{1,0:T(8,128)(2,1)}) custom-call(s32[2]{0:T(128)S(1)} %get-tuple-element.390.order, bf16[288,768]{1,0:T(8,128)(2,1)S(1)} %collective-permute-done.29.grad_main.grad_here, ...), custom_call_target="tpu_custom_call", output_to_operand_aliasing={{0}: (8, {}), {1}: (9, {}), {2}: (10, {})} | custom-call | tf_op jit(solution)/shard_map/attention_backward/pallas_call | solution.py:116
  159.1 1.2 add.14.total
  160.3 1.3 collective-permute-start.40
  161.6 5.4 %attention_backward.7 = (bf16[384,3072]{1,0:T(8,128)(2,1)}, bf16[384,3072]{1,0:T(8,128)(2,1)}, bf16[384,3072]{1,0:T(8,128)(2,1)}) custom-call(s32[2]{0:T(128)S(1)} %get-tuple-element.391.order, bf16[288,768]{1,0:T(8,128)(2,1)} %collective-permute-done.35.grad_main.grad_here, ...), custom_call_target="tpu_custom_call", output_to_operand_aliasing={{0}: (8, {}), {1}: (9, {}), {2}: (10, {})} | custom-call | tf_op jit(solution)/shard_map/attention_backward/pallas_call | solution.py:116
  167.0 1.2 add.15.total
  168.2 1.3 collective-permute-start.39
  169.5 2.7 %line_end.5.rest_0_ = f32[384,3072]{1,0:T(8,128)} custom-call(s32[1]{0:T(128)} %bitcast.place, bf16[384,1024]{1,0:T(8,128)(2,1)} %add.12.total, bf16[384,1024]{1,0:T(8,128)(2,1)} %collective-permute-done.41.arrived, f32[384,3072]{1,0:T(8,128)} %line_end.4.rest_0_), custom_call_target="tpu_custom_call", output_to_operand_aliasing={{}: (3, {})} | custom-call | tf_op jit(solution)/shard_map/line_end/pallas_call | solution.py:319
  172.2 5.8 %collective-permute-done.40.arrived = bf16[384,512]{1,0:T(8,128)(2,1)S(1)} collective-permute-done((bf16[384,512]{1,0:T(8,128)(2,1)S(1)}, bf16[384,512]{1,0:T(8,128)(2,1)S(1)}, u32[]{:S(2)}, u32[]{:S(2)}) %collective-permute-start.40) | collective-permute-done | bytes 393248 | tf_op jit(solution)/shard_map/ppermute | solution.py:357
  178.9 7.3 %collective-permute-done.39.arrived = bf16[384,512]{1,0:T(8,128)(2,1)S(1)} collective-permute-done((bf16[384,512]{1,0:T(8,128)(2,1)S(1)}, bf16[384,512]{1,0:T(8,128)(2,1)S(1)}, u32[]{:S(2)}, u32[]{:S(2)}) %collective-permute-start.39) | collective-permute-done | bytes 393248 | tf_op jit(solution)/shard_map/ppermute | solution.py:357
  (108 shorter events, 26.0 us)
Async XLA Ops:
  0.6 24.3 %collective-permute-start.3 = (bf16[384,3072]{1,0:T(8,128)(2,1)}, bf16[384,3072]{1,0:T(8,128)(2,1)}, u32[]{:S(2)}, u32[]{:S(2)}) collective-permute-start(bf16[384,3072]{1,0:T(8,128)(2,1)} %own.2), channel_id=1, source_target_pairs={{0,1},{1,0},{2,3},{3,2},{4,5},{5,4},{6,7},{7,6},{8,9},{9,8},{10,11... | collective-permute-start | bytes 7077896 | tf_op jit(solution)/shard_map/ppermute | solution.py:379
  3.5 8.1 %copy-start = (bf16[384,3072]{1,0:T(8,128)(2,1)S(1)}, bf16[384,3072]{1,0:T(8,128)(2,1)}, u32[]{:S(2)}) copy-start(bf16[384,3072]{1,0:T(8,128)(2,1)} %query.5) | copy-start | bytes 7077892
  3.5 8.1 %copy-start.1 = (bf16[384,3072]{1,0:T(8,128)(2,1)S(1)}, bf16[384,3072]{1,0:T(8,128)(2,1)}, u32[]{:S(2)}) copy-start(bf16[384,3072]{1,0:T(8,128)(2,1)} %key.5) | copy-start | bytes 7077892
  4.2 2.1 %collective-permute-start = (bf16[96,3072]{1,0:T(8,128)(2,1)S(1)}, bf16[96,3072]{1,0:T(8,128)(2,1)S(1)}, u32[]{:S(2)}, u32[]{:S(2)}) collective-permute-start(bf16[96,3072]{1,0:T(8,128)(2,1)S(1)} %other_quarter.1), channel_id=1, source_target_pairs={{0,1},{1,0},{2,3},{3,2},{4,5},{5,4},{6,7},{7,6},{8,9},{9,8},{10,11... | collective-permute-start | bytes 1769480 | tf_op jit(solution)/shard_map/ppermute | solution.py:379
  7.0 17.9 %collective-permute-start.1 = (bf16[240,1024]{1,0:T(8,128)(2,1)S(1)}, bf16[240,1024]{1,0:T(8,128)(2,1)S(1)}, u32[]{:S(2)}, u32[]{:S(2)}) collective-permute-start(bf16[240,1024]{1,0:T(8,128)(2,1)S(1)} %get-tuple-element.233.to_x), channel_id=1, source_target_pairs={{0,2},{1,3},{2,0},{3,1},{4,6},{5,7},{6,4},{7,5},{8,10},{9,11},{10,... | collective-permute-start | bytes 1474568 | tf_op jit(solution)/shard_map/ppermute | solution.py:379
  9.8 15.1 %collective-permute-start.2 = (bf16[240,1024]{1,0:T(8,128)(2,1)S(1)}, bf16[240,1024]{1,0:T(8,128)(2,1)S(1)}, u32[]{:S(2)}, u32[]{:S(2)}) collective-permute-start(bf16[240,1024]{1,0:T(8,128)(2,1)S(1)} %get-tuple-element.219.to_y), channel_id=1, source_target_pairs={{0,4},{1,5},{2,6},{3,7},{4,0},{5,1},{6,2},{7,3},{8,12},{9,13},{10,... | collective-permute-start | bytes 1474568 | tf_op jit(solution)/shard_map/ppermute | solution.py:379
  13.2 5.5 %copy-start.10 = (s32[384]{0:T(512)S(1)}, s32[384]{0:T(512)}, u32[]{:S(2)}) copy-start(s32[384]{0:T(512)} %ids.2) | copy-start | bytes 4612
  18.7 6.3 %collective-permute-start.4 = (bf16[96,1536]{1,0:T(8,128)(2,1)S(1)}, bf16[96,1536]{1,0:T(8,128)(2,1)S(1)}, u32[]{:S(2)}, u32[]{:S(2)}) collective-permute-start(bf16[96,1536]{1,0:T(8,128)(2,1)S(1)} %get-tuple-element.209), channel_id=1, source_target_pairs={{0,1},{1,0},{2,3},{3,2},{4,5},{5,4},{6,7},{7,6},{8,9},{9,8},{10,11... | collective-permute-start | bytes 884744 | tf_op jit(solution)/shard_map/ppermute | solution.py:379
  24.4 1.8 collective-permute-start.5
  26.8 28.5 %collective-permute-start.10 = (bf16[288,768]{1,0:T(8,128)(2,1)S(1)}, bf16[288,768]{1,0:T(8,128)(2,1)S(1)}, u32[]{:S(2)}, u32[]{:S(2)}) collective-permute-start(bf16[288,768]{1,0:T(8,128)(2,1)S(1)} %get-tuple-element.232), channel_id=1, source_target_pairs={{0,6},{1,7},{2,4},{3,5},{4,2},{5,3},{6,0},{7,1},{8,14},{9,15},{10,... | collective-permute-start | bytes 1327112 | tf_op jit(solution)/shard_map/ppermute | solution.py:379
  26.9 28.4 %collective-permute-start.9 = (bf16[288,768]{1,0:T(8,128)(2,1)S(1)}, bf16[288,768]{1,0:T(8,128)(2,1)S(1)}, u32[]{:S(2)}, u32[]{:S(2)}) collective-permute-start(bf16[288,768]{1,0:T(8,128)(2,1)S(1)} %get-tuple-element.231), channel_id=1, source_target_pairs={{0,4},{1,5},{2,6},{3,7},{4,0},{5,1},{6,2},{7,3},{8,12},{9,13},{10,... | collective-permute-start | bytes 1327112 | tf_op jit(solution)/shard_map/ppermute | solution.py:379
  28.8 26.5 %collective-permute-start.8 = (bf16[288,768]{1,0:T(8,128)(2,1)S(1)}, bf16[288,768]{1,0:T(8,128)(2,1)S(1)}, u32[]{:S(2)}, u32[]{:S(2)}) collective-permute-start(bf16[288,768]{1,0:T(8,128)(2,1)S(1)} %get-tuple-element.228), channel_id=1, source_target_pairs={{0,2},{1,3},{2,0},{3,1},{4,6},{5,7},{6,4},{7,5},{8,10},{9,11},{10,... | collective-permute-start | bytes 1327112 | tf_op jit(solution)/shard_map/ppermute | solution.py:379
  30.3 24.8 %collective-permute-start.6 = (bf16[144,1024]{1,0:T(8,128)(2,1)S(1)}, bf16[144,1024]{1,0:T(8,128)(2,1)S(1)}, u32[]{:S(2)}, u32[]{:S(2)}) collective-permute-start(bf16[144,1024]{1,0:T(8,128)(2,1)S(1)} %get-tuple-element.236.next_y), channel_id=1, source_target_pairs={{0,4},{1,5},{2,6},{3,7},{4,0},{5,1},{6,2},{7,3},{8,12},{9,13},{10,... | collective-permute-start | bytes 884744 | tf_op jit(solution)/shard_map/ppermute | solution.py:379
  30.8 24.3 %collective-permute-start.7 = (bf16[144,1024]{1,0:T(8,128)(2,1)S(1)}, bf16[144,1024]{1,0:T(8,128)(2,1)S(1)}, u32[]{:S(2)}, u32[]{:S(2)}) collective-permute-start(bf16[144,1024]{1,0:T(8,128)(2,1)S(1)} %get-tuple-element.237.next_x), channel_id=1, source_target_pairs={{0,2},{1,3},{2,0},{3,1},{4,6},{5,7},{6,4},{7,5},{8,10},{9,11},{10,... | collective-permute-start | bytes 884744 | tf_op jit(solution)/shard_map/ppermute | solution.py:379
  56.5 7.1 %copy-start.5 = (bf16[384,3072]{1,0:T(8,128)(2,1)S(1)}, bf16[384,3072]{1,0:T(8,128)(2,1)}, u32[]{:S(2)}) copy-start(bf16[384,3072]{1,0:T(8,128)(2,1)} %own.2) | copy-start | bytes 7077892
  56.5 2.5 %collective-permute-start.11 = (bf16[384,512]{1,0:T(8,128)(2,1)S(1)}, bf16[384,512]{1,0:T(8,128)(2,1)S(1)}, u32[]{:S(2)}, u32[]{:S(2)}) collective-permute-start(bf16[384,512]{1,0:T(8,128)(2,1)S(1)} %get-tuple-element.246), channel_id=1, source_target_pairs={{0,1},{1,0},{2,3},{3,2},{4,5},{5,4},{6,7},{7,6},{8,9},{9,8},{10,11... | collective-permute-start | bytes 1179656 | tf_op jit(solution)/shard_map/ppermute | solution.py:379
  56.5 2.5 %collective-permute-start.12 = (bf16[384,512]{1,0:T(8,128)(2,1)S(1)}, bf16[384,512]{1,0:T(8,128)(2,1)S(1)}, u32[]{:S(2)}, u32[]{:S(2)}) collective-permute-start(bf16[384,512]{1,0:T(8,128)(2,1)S(1)} %get-tuple-element.247), channel_id=1, source_target_pairs={{0,1},{1,0},{2,3},{3,2},{4,5},{5,4},{6,7},{7,6},{8,9},{9,8},{10,11... | collective-permute-start | bytes 1179656 | tf_op jit(solution)/shard_map/ppermute | solution.py:379
  57.0 13.2 %collective-permute-start.13 = (bf16[240,1024]{1,0:T(8,128)(2,1)S(1)}, bf16[240,1024]{1,0:T(8,128)(2,1)S(1)}, u32[]{:S(2)}, u32[]{:S(2)}) collective-permute-start(bf16[240,1024]{1,0:T(8,128)(2,1)S(1)} %get-tuple-element.263.to_x), channel_id=1, source_target_pairs={{0,2},{1,3},{2,0},{3,1},{4,6},{5,7},{6,4},{7,5},{8,10},{9,11},{10,... | collective-permute-start | bytes 1474568 | tf_op jit(solution)/shard_map/ppermute | solution.py:379
  58.4 12.9 %collective-permute-start.14 = (bf16[240,1024]{1,0:T(8,128)(2,1)S(1)}, bf16[240,1024]{1,0:T(8,128)(2,1)S(1)}, u32[]{:S(2)}, u32[]{:S(2)}) collective-permute-start(bf16[240,1024]{1,0:T(8,128)(2,1)S(1)} %get-tuple-element.258.to_y), channel_id=1, source_target_pairs={{0,4},{1,5},{2,6},{3,7},{4,0},{5,1},{6,2},{7,3},{8,12},{9,13},{10,... | collective-permute-start | bytes 1474568 | tf_op jit(solution)/shard_map/ppermute | solution.py:379
  60.0 26.6 %collective-permute-start.17 = (bf16[384,1024]{1,0:T(8,128)(2,1)S(1)}, bf16[384,1024]{1,0:T(8,128)(2,1)S(1)}, u32[]{:S(2)}, u32[]{:S(2)}) collective-permute-start(bf16[384,1024]{1,0:T(8,128)(2,1)S(1)} %term_own.3.a), channel_id=1, source_target_pairs={{0,8},{24,16},{1,9},{25,17},{2,10},{26,18},{3,11},{27,19},{4,12},{... | collective-permute-start | bytes 2359304 | tf_op jit(solution)/shard_map/ppermute | solution.py:343
  71.4 7.9 %collective-permute-start.15 = (bf16[144,1024]{1,0:T(8,128)(2,1)S(1)}, bf16[144,1024]{1,0:T(8,128)(2,1)S(1)}, u32[]{:S(2)}, u32[]{:S(2)}) collective-permute-start(bf16[144,1024]{1,0:T(8,128)(2,1)S(1)} %get-tuple-element.266.next_y), channel_id=1, source_target_pairs={{0,4},{1,5},{2,6},{3,7},{4,0},{5,1},{6,2},{7,3},{8,12},{9,13},{10,... | collective-permute-start | bytes 884744 | tf_op jit(solution)/shard_map/ppermute | solution.py:379
  72.0 7.6 %collective-permute-start.16 = (bf16[144,1024]{1,0:T(8,128)(2,1)S(1)}, bf16[144,1024]{1,0:T(8,128)(2,1)S(1)}, u32[]{:S(2)}, u32[]{:S(2)}) collective-permute-start(bf16[144,1024]{1,0:T(8,128)(2,1)S(1)} %get-tuple-element.267.next_x), channel_id=1, source_target_pairs={{0,2},{1,3},{2,0},{3,1},{4,6},{5,7},{6,4},{7,5},{8,10},{9,11},{10,... | collective-permute-start | bytes 884744 | tf_op jit(solution)/shard_map/ppermute | solution.py:379
  80.8 14.4 %collective-permute-start.20 = (bf16[240,1024]{1,0:T(8,128)(2,1)S(1)}, bf16[240,1024]{1,0:T(8,128)(2,1)S(1)}, u32[]{:S(2)}, u32[]{:S(2)}) collective-permute-start(bf16[240,1024]{1,0:T(8,128)(2,1)S(1)} %get-tuple-element.292.to_x), channel_id=1, source_target_pairs={{0,2},{1,3},{2,0},{3,1},{4,6},{5,7},{6,4},{7,5},{8,10},{9,11},{10,... | collective-permute-start | bytes 1474568 | tf_op jit(solution)/shard_map/ppermute | solution.py:379
  82.3 12.9 %collective-permute-start.21 = (bf16[240,1024]{1,0:T(8,128)(2,1)S(1)}, bf16[240,1024]{1,0:T(8,128)(2,1)S(1)}, u32[]{:S(2)}, u32[]{:S(2)}) collective-permute-start(bf16[240,1024]{1,0:T(8,128)(2,1)S(1)} %get-tuple-element.287.to_y), channel_id=1, source_target_pairs={{0,4},{1,5},{2,6},{3,7},{4,0},{5,1},{6,2},{7,3},{8,12},{9,13},{10,... | collective-permute-start | bytes 1474568 | tf_op jit(solution)/shard_map/ppermute | solution.py:379
  82.9 4.6 %collective-permute-start.18 = (bf16[384,512]{1,0:T(8,128)(2,1)S(1)}, bf16[384,512]{1,0:T(8,128)(2,1)S(1)}, u32[]{:S(2)}, u32[]{:S(2)}) collective-permute-start(bf16[384,512]{1,0:T(8,128)(2,1)S(1)} %get-tuple-element.272), channel_id=1, source_target_pairs={{0,1},{1,0},{2,3},{3,2},{4,5},{5,4},{6,7},{7,6},{8,9},{9,8},{10,11... | collective-permute-start | bytes 1179656 | tf_op jit(solution)/shard_map/ppermute | solution.py:379
  82.9 4.7 %collective-permute-start.19 = (bf16[384,512]{1,0:T(8,128)(2,1)S(1)}, bf16[384,512]{1,0:T(8,128)(2,1)S(1)}, u32[]{:S(2)}, u32[]{:S(2)}) collective-permute-start(bf16[384,512]{1,0:T(8,128)(2,1)S(1)} %get-tuple-element.273), channel_id=1, source_target_pairs={{0,1},{1,0},{2,3},{3,2},{4,5},{5,4},{6,7},{7,6},{8,9},{9,8},{10,11... | collective-permute-start | bytes 1179656 | tf_op jit(solution)/shard_map/ppermute | solution.py:379
  86.8 25.0 %collective-permute-start.24 = (bf16[384,1024]{1,0:T(8,128)(2,1)S(1)}, bf16[384,1024]{1,0:T(8,128)(2,1)S(1)}, u32[]{:S(2)}, u32[]{:S(2)}) collective-permute-start(bf16[384,1024]{1,0:T(8,128)(2,1)S(1)} %add.8.a), channel_id=1, source_target_pairs={{8,16},{16,8},{9,17},{17,9},{10,18},{18,10},{11,19},{19,11},{12,20... | collective-permute-start | bytes 2359304 | tf_op jit(solution)/shard_map/ppermute | solution.py:350
  88.6 24.8 %collective-permute-start.25 = (bf16[384,1024]{1,0:T(8,128)(2,1)S(1)}, bf16[384,1024]{1,0:T(8,128)(2,1)S(1)}, u32[]{:S(2)}, u32[]{:S(2)}) collective-permute-start(bf16[384,1024]{1,0:T(8,128)(2,1)S(1)} %term_own.4.a), channel_id=1, source_target_pairs={{0,8},{24,16},{1,9},{25,17},{2,10},{26,18},{3,11},{27,19},{4,12},{... | collective-permute-start | bytes 2359304 | tf_op jit(solution)/shard_map/ppermute | solution.py:343
  95.3 8.4 %collective-permute-start.22 = (bf16[144,1024]{1,0:T(8,128)(2,1)S(1)}, bf16[144,1024]{1,0:T(8,128)(2,1)S(1)}, u32[]{:S(2)}, u32[]{:S(2)}) collective-permute-start(bf16[144,1024]{1,0:T(8,128)(2,1)S(1)} %get-tuple-element.295.next_y), channel_id=1, source_target_pairs={{0,4},{1,5},{2,6},{3,7},{4,0},{5,1},{6,2},{7,3},{8,12},{9,13},{10,... | collective-permute-start | bytes 884744 | tf_op jit(solution)/shard_map/ppermute | solution.py:379
  96.6 8.1 %collective-permute-start.23 = (bf16[144,1024]{1,0:T(8,128)(2,1)S(1)}, bf16[144,1024]{1,0:T(8,128)(2,1)S(1)}, u32[]{:S(2)}, u32[]{:S(2)}) collective-permute-start(bf16[144,1024]{1,0:T(8,128)(2,1)S(1)} %get-tuple-element.296.next_x), channel_id=1, source_target_pairs={{0,2},{1,3},{2,0},{3,1},{4,6},{5,7},{6,4},{7,5},{8,10},{9,11},{10,... | collective-permute-start | bytes 884744 | tf_op jit(solution)/shard_map/ppermute | solution.py:379
  109.8 10.3 %collective-permute-start.28 = (bf16[288,768]{1,0:T(8,128)(2,1)S(1)}, bf16[288,768]{1,0:T(8,128)(2,1)S(1)}, u32[]{:S(2)}, u32[]{:S(2)}) collective-permute-start(bf16[288,768]{1,0:T(8,128)(2,1)S(1)} %get-tuple-element.308), channel_id=1, source_target_pairs={{0,2},{1,3},{2,0},{3,1},{4,6},{5,7},{6,4},{7,5},{8,10},{9,11},{10,... | collective-permute-start | bytes 1327112 | tf_op jit(solution)/shard_map/ppermute | solution.py:379
  110.5 10.0 %collective-permute-start.29 = (bf16[288,768]{1,0:T(8,128)(2,1)S(1)}, bf16[288,768]{1,0:T(8,128)(2,1)S(1)}, u32[]{:S(2)}, u32[]{:S(2)}) collective-permute-start(bf16[288,768]{1,0:T(8,128)(2,1)S(1)} %get-tuple-element.309), channel_id=1, source_target_pairs={{0,4},{1,5},{2,6},{3,7},{4,0},{5,1},{6,2},{7,3},{8,12},{9,13},{10,... | collective-permute-start | bytes 1327112 | tf_op jit(solution)/shard_map/ppermute | solution.py:379
  111.8 2.5 %collective-permute-start.26 = (bf16[384,512]{1,0:T(8,128)(2,1)S(1)}, bf16[384,512]{1,0:T(8,128)(2,1)S(1)}, u32[]{:S(2)}, u32[]{:S(2)}) collective-permute-start(bf16[384,512]{1,0:T(8,128)(2,1)S(1)} %get-tuple-element.301), channel_id=1, source_target_pairs={{0,1},{1,0},{2,3},{3,2},{4,5},{5,4},{6,7},{7,6},{8,9},{9,8},{10,11... | collective-permute-start | bytes 1179656 | tf_op jit(solution)/shard_map/ppermute | solution.py:379
  111.8 2.5 %collective-permute-start.27 = (bf16[384,512]{1,0:T(8,128)(2,1)S(1)}, bf16[384,512]{1,0:T(8,128)(2,1)S(1)}, u32[]{:S(2)}, u32[]{:S(2)}) collective-permute-start(bf16[384,512]{1,0:T(8,128)(2,1)S(1)} %get-tuple-element.302), channel_id=1, source_target_pairs={{0,1},{1,0},{2,3},{3,2},{4,5},{5,4},{6,7},{7,6},{8,9},{9,8},{10,11... | collective-permute-start | bytes 1179656 | tf_op jit(solution)/shard_map/ppermute | solution.py:379
  113.6 30.3 %collective-permute-start.32 = (bf16[384,1024]{1,0:T(8,128)(2,1)S(1)}, bf16[384,1024]{1,0:T(8,128)(2,1)S(1)}, u32[]{:S(2)}, u32[]{:S(2)}) collective-permute-start(bf16[384,1024]{1,0:T(8,128)(2,1)S(1)} %add.10.a), channel_id=1, source_target_pairs={{8,16},{16,8},{9,17},{17,9},{10,18},{18,10},{11,19},{19,11},{12,20... | collective-permute-start | bytes 2359304 | tf_op jit(solution)/shard_map/ppermute | solution.py:350
  120.6 8.1 %collective-permute-start.30 = (bf16[96,2304]{1,0:T(8,128)(2,1)S(1)}, bf16[96,2304]{1,0:T(8,128)(2,1)S(1)}, u32[]{:S(2)}, u32[]{:S(2)}) collective-permute-start(bf16[96,2304]{1,0:T(8,128)(2,1)S(1)} %pad_maximum_fusion), channel_id=1, source_target_pairs={{0,1},{1,0},{2,3},{3,2},{4,5},{5,4},{6,7},{7,6},{8,9},{9,8},{10,11... | collective-permute-start | bytes 1327112 | tf_op jit(solution)/shard_map/ppermute | solution.py:379
  120.6 27.9 %collective-permute-start.34 = (bf16[384,1024]{1,0:T(8,128)(2,1)}, bf16[384,1024]{1,0:T(8,128)(2,1)}, u32[]{:S(2)}, u32[]{:S(2)}) collective-permute-start(bf16[384,1024]{1,0:T(8,128)(2,1)} %add.9.total), channel_id=1, source_target_pairs={{8,0},{16,24},{9,1},{17,25},{10,2},{18,26},{11,3},{19,27},{12,4},{... | collective-permute-start | bytes 2359304 | tf_op jit(solution)/shard_map/ppermute | solution.py:357
  121.9 14.9 %collective-permute-start.31 = (bf16[384,512]{1,0:T(8,128)(2,1)S(1)}, bf16[384,512]{1,0:T(8,128)(2,1)S(1)}, u32[]{:S(2)}, u32[]{:S(2)}) collective-permute-start(bf16[384,512]{1,0:T(8,128)(2,1)S(1)} %get-tuple-element.334.a), channel_id=1, source_target_pairs={{0,8},{24,16},{1,9},{25,17},{2,10},{26,18},{3,11},{27,19},{4,12},{... | collective-permute-start | bytes 1179656 | tf_op jit(solution)/shard_map/ppermute | solution.py:343
  127.4 18.9 %collective-permute-start.33 = (bf16[384,512]{1,0:T(8,128)(2,1)S(1)}, bf16[384,512]{1,0:T(8,128)(2,1)S(1)}, u32[]{:S(2)}, u32[]{:S(2)}) collective-permute-start(bf16[384,512]{1,0:T(8,128)(2,1)S(1)} %get-tuple-element.348.a), channel_id=1, source_target_pairs={{0,8},{24,16},{1,9},{25,17},{2,10},{26,18},{3,11},{27,19},{4,12},{... | collective-permute-start | bytes 1179656 | tf_op jit(solution)/shard_map/ppermute | solution.py:343
  128.7 22.6 %collective-permute-start.35 = (bf16[288,768]{1,0:T(8,128)(2,1)}, bf16[288,768]{1,0:T(8,128)(2,1)}, u32[]{:S(2)}, u32[]{:S(2)}) collective-permute-start(bf16[288,768]{1,0:T(8,128)(2,1)} %get-tuple-element.352), channel_id=1, source_target_pairs={{0,6},{1,7},{2,4},{3,5},{4,2},{5,3},{6,0},{7,1},{8,14},{9,15},{10,... | collective-permute-start | bytes 1327112 | tf_op jit(solution)/shard_map/ppermute | solution.py:379
  137.7 21.4 %collective-permute-start.36 = (bf16[384,512]{1,0:T(8,128)(2,1)}, bf16[384,512]{1,0:T(8,128)(2,1)}, u32[]{:S(2)}, u32[]{:S(2)}) collective-permute-start(bf16[384,512]{1,0:T(8,128)(2,1)} %add.11.a), channel_id=1, source_target_pairs={{8,16},{16,8},{9,17},{17,9},{10,18},{18,10},{11,19},{19,11},{12,20... | collective-permute-start | bytes 1179656 | tf_op jit(solution)/shard_map/ppermute | solution.py:350
  145.0 24.5 %collective-permute-start.41 = (bf16[384,1024]{1,0:T(8,128)(2,1)}, bf16[384,1024]{1,0:T(8,128)(2,1)}, u32[]{:S(2)}, u32[]{:S(2)}) collective-permute-start(bf16[384,1024]{1,0:T(8,128)(2,1)} %add.12.total), channel_id=1, source_target_pairs={{8,0},{16,24},{9,1},{17,25},{10,2},{18,26},{11,3},{19,27},{12,4},{... | collective-permute-start | bytes 2359304 | tf_op jit(solution)/shard_map/ppermute | solution.py:357
  147.1 19.9 %collective-permute-start.38 = (bf16[384,512]{1,0:T(8,128)(2,1)}, bf16[384,512]{1,0:T(8,128)(2,1)}, u32[]{:S(2)}, u32[]{:S(2)}) collective-permute-start(bf16[384,512]{1,0:T(8,128)(2,1)} %add.13.a), channel_id=1, source_target_pairs={{8,16},{16,8},{9,17},{17,9},{10,18},{18,10},{11,19},{19,11},{12,20... | collective-permute-start | bytes 1179656 | tf_op jit(solution)/shard_map/ppermute | solution.py:350
  148.5 3.8 %copy-start.2 = (bf16[384,3072]{1,0:T(8,128)(2,1)S(1)}, bf16[384,3072]{1,0:T(8,128)(2,1)}, u32[]{:S(2)}) copy-start(bf16[384,3072]{1,0:T(8,128)(2,1)} %key.5) | copy-start | bytes 7077892
  148.5 3.8 %copy-start.4 = (bf16[384,3072]{1,0:T(8,128)(2,1)S(1)}, bf16[384,3072]{1,0:T(8,128)(2,1)}, u32[]{:S(2)}) copy-start(bf16[384,3072]{1,0:T(8,128)(2,1)} %value.5) | copy-start | bytes 7077892
  152.2 9.4 %collective-permute-start.37 = (bf16[96,768]{1,0:T(8,128)(2,1)S(1)}, bf16[96,768]{1,0:T(8,128)(2,1)S(1)}, u32[]{:S(2)}, u32[]{:S(2)}) collective-permute-start(bf16[96,768]{1,0:T(8,128)(2,1)S(1)} %slice.39), channel_id=1, source_target_pairs={{0,1},{1,0},{2,3},{3,2},{4,5},{5,4},{6,7},{7,6},{8,9},{9,8},{10,11... | collective-permute-start | bytes 442376 | tf_op jit(solution)/shard_map/ppermute | solution.py:379
  160.3 17.7 %collective-permute-start.40 = (bf16[384,512]{1,0:T(8,128)(2,1)S(1)}, bf16[384,512]{1,0:T(8,128)(2,1)S(1)}, u32[]{:S(2)}, u32[]{:S(2)}) collective-permute-start(bf16[384,512]{1,0:T(8,128)(2,1)S(1)} %add.14.total), channel_id=1, source_target_pairs={{8,0},{16,24},{9,1},{17,25},{10,2},{18,26},{11,3},{19,27},{12,4},{... | collective-permute-start | bytes 1179656 | tf_op jit(solution)/shard_map/ppermute | solution.py:357
  168.2 18.0 %collective-permute-start.39 = (bf16[384,512]{1,0:T(8,128)(2,1)S(1)}, bf16[384,512]{1,0:T(8,128)(2,1)S(1)}, u32[]{:S(2)}, u32[]{:S(2)}) collective-permute-start(bf16[384,512]{1,0:T(8,128)(2,1)S(1)} %add.15.total), channel_id=1, source_target_pairs={{8,0},{16,24},{9,1},{17,25},{10,2},{18,26},{11,3},{19,27},{12,4},{... | collective-permute-start | bytes 1179656 | tf_op jit(solution)/shard_map/ppermute | solution.py:357
  (5 other events, 8.4 us)

commit v2 on v1

--- a/solution.py
+++ b/solution.py
@@ -12,7 +12,8 @@
 BLOCK_HEADS = 3
 BLOCK = BLOCK_HEADS * E
 PAIR = 2 * BLOCK
-PARTS = 3
+PARTS = 2
+SHARES = 3
 F32 = jnp.float32
 BF16 = jnp.bfloat16
 LOG2_E = math.log2(math.e)
@@ -236,15 +237,14 @@
         out[...] = share[:, i * width : (i + 1) * width]
 
 
-def term_own_kernel(attended, plane, left, right, *outs):
+def term_own_kernel(attended, plane, *refs):
+    arrived, outs = refs[:-2], refs[-2:]
     own = dot(attended[:, :BLOCK], plane[...], 0, 0)
-    width = left.shape[1]
-    total = [(own[:, :width] + left[...].astype(F32)).astype(BF16), (own[:, width:] + right[...].astype(F32)).astype(BF16)]
-    for i in range(2):
-        if len(outs) == 2:
-            outs[i][...] = total[i]
-        else:
-            outs[0][:, i * width : (i + 1) * width] = total[i]
+    there = jnp.concatenate([a[...] for a in arrived], axis=1)
+    total = (own + there.astype(F32)).astype(BF16)
+    width = outs[0].shape[1]
+    for i, out in enumerate(outs):
+        out[...] = total[:, i * width : (i + 1) * width]
 
 
 def grad_kernel(plane, own, other, *rest):
@@ -262,9 +262,10 @@
     for i, weight in enumerate((own, other)):
         columns = slice(i * BLOCK, (i + 1) * BLOCK)
         total = (before[:, columns] + dot(plane[...], weight[...], 1, 1)).astype(BF16)
-        for j, piece in enumerate(pieces):
+        for j, piece in enumerate(pieces[:-1]):
             piece[:short, columns] = total[j * short : (j + 1) * short]
             piece[short:, columns] = total[4 * short :]
+        pieces[-1][:, columns] = total[4 * short :]
 
 
 def grad_part(part, plane, own_weight, other_weight, before):
@@ -278,8 +279,8 @@
         grad_end_kernel if last else grad_kernel,
         grid=(1,),
         in_specs=[pl.BlockSpec((count, width), lambda i: (0, 0)), weight, weight] + [result] * len(before),
-        out_specs=[piece] * 4 if last else [result],
-        out_shape=[jax.ShapeDtypeStruct((rows, PAIR), BF16)] * 4
+        out_specs=[piece] * 4 + [pl.BlockSpec((rows // 3, PAIR), lambda i: (0, 0))] if last else [result],
+        out_shape=[jax.ShapeDtypeStruct((rows, PAIR), BF16)] * 4 + [jax.ShapeDtypeStruct((rows // 3, PAIR), BF16)]
         if last
         else [jax.ShapeDtypeStruct((count, PAIR), F32)],
         compiler_params=pltpu.CompilerParams(vmem_limit_bytes=VMEM_LIMIT),
@@ -420,17 +421,16 @@
 
     def term_other(plane, attended):
         plane, attended = order(plane, attended)
-        shape = (BLOCK, part_width // 2)
-        share = whole(term_other_kernel, [shape] * 2, attended, plane, name="term_other")
+        shape = (BLOCK, part_width // SHARES)
+        share = whole(term_other_kernel, [shape] * SHARES, attended, plane, name="term_other")
         order.mark(*share)
-        return [swap(half, 1) for half in share]
-
-    def term_own(plane, attended, arrived, pieces=1):
+        return [swap(piece, 1) for piece in share]
+
+    def term_own(plane, attended, arrived):
         held = order(attended, plane, *arrived)
-        shape = (BLOCK, part_width // pieces)
-        total = whole(term_own_kernel, [shape] * pieces, *held, name="term_own")
-        order.mark(*total)
-        return total
+        pieces = whole(term_own_kernel, [(BLOCK, part_width // 2)] * 2, *held, name="term_own")
+        order.mark(*pieces)
+        return pieces
 
     def attend(half):
         held = order(segment_ids, query_rows, key_rows, value_rows)
@@ -455,63 +455,59 @@
     to_y, to_far = pack(far, far_arriving)
     arriving = from_x, swap(to_y, 4), swap(to_far, 6)
     plane = gather_end(0)
+    grad = grad_step(0, plane, ())
     held = order(kept, *arriving)
     (gathered,) = whole(collect_kernel, [(4 * short + quarter, PAIR)], *held, name="collect")
     order.mark(gathered)
 
     arriving = term_other(plane, gathered)
     gather_start(1)
-    line.start(0, *term_own(plane, gathered, arriving))
-    grad = grad_step(0, plane, ())
+    pieces = term_own(plane, gathered, arriving)
+    line.start(0, pieces[0])
+    line.start(1, pieces[1])
     gather_forward(1)
+    line.across(0)
     plane = gather_end(1)
     arriving = term_other(plane, gathered)
-    gather_start(2)
-    grad = grad_step(1, plane, grad)
-    line.across(0)
-    line.start(1, *term_own(plane, gathered, arriving))
-    gather_forward(2)
-    plane = gather_end(2)
-    arriving = term_other(plane, gathered)
-    piece = grad_step(2, plane, grad)
+    line.across(1)
+    pieces = term_own(plane, gathered, arriving)
+    line.start(2, pieces[0])
+    line.back(0)
+    line.start(3, order(pieces[1]))
+    *piece, own_tail = grad_step(1, plane, grad)
     moved_x, moved_y = swap(piece[1], 2), swap(piece[2], 4)
-    line.back(0)
-    line.across(1)
-    last = term_own(plane, gathered, arriving, 2)
-    line.start(2, last[0])
-
-    own, moved_x, moved_y = order(piece[0], moved_x, moved_y)
-    tails = jnp.concatenate([own[short:], moved_x[short:], moved_y[short:]], axis=1)
-    order.mark(tails)
-    line.start(3, order(last[1]))
-    there = swap(tails, 1)
+    line.back(1)
+    line.across(2)
+    line.finish(0, 0)
+
+    own_tail, moved_x, moved_y = order(own_tail, moved_x, moved_y)
+    tails = [own_tail, moved_x[short:], moved_y[short:]]
+    order.mark(*tails)
+    there = [swap(tail, 1) for tail in tails]
     moved_far = swap(order(piece[3]), 6)
     grads = ()
 
-    def finish(i, grad, there, skip):
+    def finish(i, grad, there):
         weights = weights_near if i < 2 else weights_far
         held = order(grad, there, query_rows, key_rows, value_rows, weights)
-        result = backward(blocks[2 * i : 2 * i + 2], held[0], held[1], 1, skip, *held[2:], 2 * (i % 2), grads)
+        result = backward(blocks[2 * i : 2 * i + 2], held[0], held[1], 1, 0, *held[2:], 2 * (i % 2), grads)
         order.mark(*result)
         return tuple(result)
 
-    grads = finish(0, own, there, 0)
-    line.across(2)
-    grads = finish(1, moved_x, there, 2)
-    line.back(1)
+    grads = finish(0, piece[0], there[0])
     line.across(3)
-    line.finish(0, 0)
+    line.back(2)
+    line.finish(1, part_width // 2)
+    grads = finish(1, moved_x, there[1])
     moved_far = order(moved_far)
     tail = moved_far[short:]
     order.mark(tail)
     far_there = swap(tail, 1)
-    grads = finish(2, moved_y, there, 4)
-    line.back(2)
-    grads = finish(3, moved_far, far_there, 0)
     line.back(3)
-    line.finish(1, part_width)
-    line.finish(2, 2 * part_width)
-    line.finish(3, 2 * part_width + part_width // 2)
+    grads = finish(2, moved_y, there[2])
+    line.finish(2, part_width)
+    grads = finish(3, moved_far, far_there)
+    line.finish(3, part_width + part_width // 2)
     return (*grads, *line.done)
 
 

time: 188 us -> 178 us (0.947)
  waiting for transfers between devices: 64.7 us -> 58.7 us
  Pallas kernels: 64.2 us -> 59.5 us
  local copies, waits for them, and re-layouts: 7.34 us -> 10.7 us
  starting transfers between devices: 49.7 us -> 47 us
    ppermute x30 -> x28, waiting for transfers between devices: 49.9 us -> 36.6 us  [swap(): return lax.ppermute(a, 'fsdp', [(f, f ^ mask) for f in range(8)])]
    ppermute x4, waiting for transfers between devices: 1.62 us -> 9.06 us  [start(): self.arriving[piece] = lax.ppermute(part, 'rep', [(0, 1), (3, 2)])]
    unnamed x22 -> x42, local copies, waits for them, and re-layouts: 6.03 us -> 10.4 us
    ppermute x30 -> x28, starting transfers between devices: 23.4 us -> 20.1 us  [swap(): return lax.ppermute(a, 'fsdp', [(f, f ^ mask) for f in range(8)])]
    ppermute x4, starting transfers between devices: 16.9 us -> 18.8 us  [start(): self.arriving[piece] = lax.ppermute(part, 'rep', [(0, 1), (3, 2)])]
    pallas_call x24 -> x20, Pallas kernels: 15.4 us -> 13.6 us  [whole(): pl.pallas_call(kernel, in_specs=[smem] * len(scalars) + [vmem] * len(arra...]
    pallas_call x3 -> x2, Pallas kernels: 10.4 us -> 9.49 us  [grad_part(): pl.pallas_call(grad_end_kernel if last else grad_kernel, grid=(1,), in_sp...]
  transfers between devices with their start and end apart: 42 -> 40, of which waited for: 14 -> 17; matrix products, arithmetic and copies ran while one was open for 1% -> 0% of each run, Pallas kernels for 33% -> 32%
where the time goes in v2:
time: 178 us; the launch traced here: 177 us
  Pallas kernels  59.5 us (33%)
  waiting for transfers between devices  58.7 us (33%)
  starting transfers between devices  47 us (26%)
  local copies, waits for them, and re-layouts  10.7 us (6%)
    ppermute x28, waiting for transfers between devices, swap(): return lax.ppermute(a, 'fsdp', [(f, f ^ mask) for f in range(8)])  36.6 us
    ppermute x28, starting transfers between devices, swap(): return lax.ppermute(a, 'fsdp', [(f, f ^ mask) for f in range(8)])  20.1 us
    pallas_call x4, Pallas kernels, backward(): pl.pallas_call(backward_kernel, grid_spec=pltpu.PrefetchScalarGridSpec(nu...  19 us
    ppermute x4, starting transfers between devices, start(): self.arriving[piece] = lax.ppermute(part, 'rep', [(0, 1), (3, 2)])  18.8 us
    pallas_call x20, Pallas kernels, whole(): pl.pallas_call(kernel, in_specs=[smem] * len(scalars) + [vmem] * len(arra...  13.6 us
    ppermute x4, waiting for transfers between devices, back(): self.arriving[piece] = lax.ppermute(total, 'rep', [(1, 0), (2, 3)])  13 us
    pallas_call x2, Pallas kernels, forward(): pl.pallas_call(forward_kernel, grid_spec=pltpu.PrefetchScalarGridSpec(num...  10.9 us
    unnamed x42, local copies, waits for them, and re-layouts  10.4 us
  transfers between devices with their start and end apart: 40, of which 17 were waited for; matrix products, arithmetic and copies ran while one was open for 0% of the time, Pallas kernels for 32%

profile of v2, /device:TPU:0, one launch (start us, length us, event | category | flops | bytes accessed | tf_op | source)
XLA Modules:
  0.0 177.1 jit_solution(8486064787363389818)
XLA Ops:
  1.2 1.7 copy-done.10
  4.3 1.9 %collective-permute-done.arrived = bf16[96,3072]{1,0:T(8,128)(2,1)S(1)} collective-permute-done((bf16[96,3072]{1,0:T(8,128)(2,1)S(1)}, bf16[96,3072]{1,0:T(8,128)(2,1)S(1)}, u32[]{:S(2)}, u32[]{:S(2)}) %collective-permute-start) | collective-permute-done | bytes 589856 | tf_op jit(solution)/shard_map/ppermute | solution.py:380
  7.0 2.9 %collective-permute-start.1 = (bf16[240,1536]{1,0:T(8,128)(2,1)S(1)}, bf16[240,1536]{1,0:T(8,128)(2,1)S(1)}, u32[]{:S(2)}, u32[]{:S(2)}) collective-permute-start(bf16[240,1536]{1,0:T(8,128)(2,1)S(1)} %get-tuple-element.209.to_x), channel_id=1, source_target_pairs={{0,2},{1,3},{2,0},{3,1},{4,6},{5,7},{6,4},{7,5},{8,10},{9,11},{10,... | collective-permute-start | bytes 2211848 | tf_op jit(solution)/shard_map/ppermute | solution.py:380
  9.8 1.5 collective-permute-start.2
  11.6 1.7 copy-done.3
  13.2 5.4 %attention_forward.2 = (bf16[384,1536]{1,0:T(8,128)(2,1)S(1)}, bf16[96,1536]{1,0:T(8,128)(2,1)S(1)}, bf16[12,384,384]{2,1,0:T(8,128)(2,1)S(1)}) custom-call(s32[4]{0:T(128)S(1)} %get-tuple-element.342.order, s32[384,1]{1,0:T(8,128)S(1)} %reshape.28.ids_column, s32[1,384]{1,0:T(1,128)S(1)} %reshape.25.ids_row, bf16[384,3072]{1,0:T(8,128)(2,1)S(1)} %copy-done, ...), custom_call_target="tpu_custom_call" | custom-call | tf_op jit(solution)/shard_map/attention_forward/pallas_call | solution.py:59
  18.7 1.8 copy-done.7
  20.7 5.5 %attention_forward.3 = (bf16[384,1536]{1,0:T(8,128)(2,1)S(1)}, bf16[96,1536]{1,0:T(8,128)(2,1)S(1)}, bf16[12,384,384]{2,1,0:T(8,128)(2,1)S(1)}) custom-call(s32[4]{0:T(128)S(1)} %get-tuple-element.343.order, s32[384,1]{1,0:T(8,128)S(1)} %reshape.29.ids_column, s32[1,384]{1,0:T(1,128)S(1)} %reshape.27.ids_row, bf16[384,3072]{1,0:T(8,128)(2,1)S(1)} %copy-done, ...), custom_call_target="tpu_custom_call" | custom-call | tf_op jit(solution)/shard_map/attention_forward/pallas_call | solution.py:59
  26.7 1.5 collective-permute-done.2.from_y
  28.2 1.6 collective-permute-start.6
  32.0 2.6 %collective-permute-start.10 = (bf16[288,768]{1,0:T(8,128)(2,1)S(1)}, bf16[288,768]{1,0:T(8,128)(2,1)S(1)}, u32[]{:S(2)}, u32[]{:S(2)}) collective-permute-start(bf16[288,768]{1,0:T(8,128)(2,1)S(1)} %get-tuple-element.208), channel_id=1, source_target_pairs={{0,6},{1,7},{2,4},{3,5},{4,2},{5,3},{6,0},{7,1},{8,14},{9,15},{10,... | collective-permute-start | bytes 1327112 | tf_op jit(solution)/shard_map/ppermute | solution.py:380
  35.2 14.2 %collective-permute-done.6.via_y = bf16[144,1536]{1,0:T(8,128)(2,1)S(1)} collective-permute-done((bf16[144,1536]{1,0:T(8,128)(2,1)S(1)}, bf16[144,1536]{1,0:T(8,128)(2,1)S(1)}, u32[]{:S(2)}, u32[]{:S(2)}) %collective-permute-start.6) | collective-permute-done | bytes 442400 | tf_op jit(solution)/shard_map/ppermute | solution.py:380
  49.6 4.2 %grad_attended.2.before = f32[864,768]{1,0:T(8,128)S(1)} custom-call(bf16[864,1536]{1,0:T(8,128)(2,1)S(1)} %gather_end.2.plane, bf16[384,3072]{1,0:T(8,128)(2,1)S(1)} %copy-done.9, bf16[384,3072]{1,0:T(8,128)(2,1)} %collective-permute-done.3.other), custom_call_target="tpu_custom_call" | custom-call | tf_op jit(solution)/shard_map/grad_attended/pallas_call | solution.py:278
  53.8 4.6 %collective-permute-done.9.from_y = bf16[288,768]{1,0:T(8,128)(2,1)S(1)} collective-permute-done((bf16[288,768]{1,0:T(8,128)(2,1)S(1)}, bf16[288,768]{1,0:T(8,128)(2,1)S(1)}, u32[]{:S(2)}, u32[]{:S(2)}) %collective-permute-start.9) | collective-permute-done | bytes 442400 | tf_op jit(solution)/shard_map/ppermute | solution.py:380
  58.4 1.3 collective-permute-done.8.from_x
  59.8 1.4 term_other.2
  63.0 1.2 collective-permute-done.11.refs_0_
  65.3 1.4 term_own.2
  66.7 3.4 %collective-permute-start.16 = (bf16[384,768]{1,0:T(8,128)(2,1)S(1)}, bf16[384,768]{1,0:T(8,128)(2,1)S(1)}, u32[]{:S(2)}, u32[]{:S(2)}) collective-permute-start(bf16[384,768]{1,0:T(8,128)(2,1)S(1)} %get-tuple-element.243.a), channel_id=1, source_target_pairs={{0,8},{24,16},{1,9},{25,17},{2,10},{26,18},{3,11},{27,19},{4,12},{... | collective-permute-start | bytes 1769480 | tf_op jit(solution)/shard_map/ppermute | solution.py:344
  70.2 1.3 collective-permute-start.19
  71.5 6.0 %collective-permute-done.14.from_x = bf16[240,1536]{1,0:T(8,128)(2,1)S(1)} collective-permute-done((bf16[240,1536]{1,0:T(8,128)(2,1)S(1)}, bf16[240,1536]{1,0:T(8,128)(2,1)S(1)}, u32[]{:S(2)}, u32[]{:S(2)}) %collective-permute-start.14) | collective-permute-done | bytes 737312 | tf_op jit(solution)/shard_map/ppermute | solution.py:380
  79.1 1.3 collective-permute-start.18
  80.5 3.4 %collective-permute-done.16.b = bf16[384,768]{1,0:T(8,128)(2,1)S(1)} collective-permute-done((bf16[384,768]{1,0:T(8,128)(2,1)S(1)}, bf16[384,768]{1,0:T(8,128)(2,1)S(1)}, u32[]{:S(2)}, u32[]{:S(2)}) %collective-permute-start.16) | collective-permute-done | bytes 589856 | tf_op jit(solution)/shard_map/ppermute | solution.py:344
  84.7 2.8 %collective-permute-done.17.via_y = bf16[144,1536]{1,0:T(8,128)(2,1)S(1)} collective-permute-done((bf16[144,1536]{1,0:T(8,128)(2,1)S(1)}, bf16[144,1536]{1,0:T(8,128)(2,1)S(1)}, u32[]{:S(2)}, u32[]{:S(2)}) %collective-permute-start.17) | collective-permute-done | bytes 442400 | tf_op jit(solution)/shard_map/ppermute | solution.py:380
  87.9 1.4 term_other.3
  89.9 5.7 %collective-permute-done.19.b = bf16[384,768]{1,0:T(8,128)(2,1)S(1)} collective-permute-done((bf16[384,768]{1,0:T(8,128)(2,1)S(1)}, bf16[384,768]{1,0:T(8,128)(2,1)S(1)}, u32[]{:S(2)}, u32[]{:S(2)}) %collective-permute-start.19) | collective-permute-done | bytes 589856 | tf_op jit(solution)/shard_map/ppermute | solution.py:344
  96.5 2.2 %term_own.3 = (bf16[384,768]{1,0:T(8,128)(2,1)}, bf16[384,768]{1,0:T(8,128)(2,1)}) custom-call(bf16[864,768]{1,0:T(8,128)(2,1)S(1)} %collect.1.attended, bf16[864,1536]{1,0:T(8,128)(2,1)S(1)} %gather_end.3.plane, bf16[384,512]{1,0:T(8,128)(2,1)S(1)} %collective-permute-done.20.refs_0_, bf16[384,512]{1,0:T(8,128)(2,1)S(1)} %collective-permute-done.21.refs_1_, ...), custom_call_target="tpu_custom_call" | custom-call | tf_op jit(solution)/shard_map/term_own/pallas_call | solution.py:144
  98.8 8.0 %collective-permute-start.25 = (bf16[384,768]{1,0:T(8,128)(2,1)}, bf16[384,768]{1,0:T(8,128)(2,1)}, u32[]{:S(2)}, u32[]{:S(2)}) collective-permute-start(bf16[384,768]{1,0:T(8,128)(2,1)} %get-tuple-element.279.a), channel_id=1, source_target_pairs={{0,8},{24,16},{1,9},{25,17},{2,10},{26,18},{3,11},{27,19},{4,12},{... | collective-permute-start | bytes 1769480 | tf_op jit(solution)/shard_map/ppermute | solution.py:344
  107.7 1.5 collective-permute-start.26
  109.2 5.2 %grad_attended.3 = (bf16[288,768]{1,0:T(8,128)(2,1)S(1)}, bf16[288,768]{1,0:T(8,128)(2,1)}, bf16[288,768]{1,0:T(8,128)(2,1)}, bf16[288,768]{1,0:T(8,128)(2,1)S(1)}, bf16[96,768]{1,0:T(8,128)(2,1)S(1)}) custom-call(bf16[864,1536]{1,0:T(8,128)(2,1)S(1)} %gather_end.3.plane, bf16[384,3072]{1,0:T(8,128)(2,1)S(1)} %copy-done.9, ...), custom_call_target="tpu_custom_call" | custom-call | tf_op jit(solution)/shard_map/grad_attended/pallas_call | solution.py:278
  116.0 1.4 collective-permute-start.27
  117.5 1.5 collective-permute-start.28
  119.8 6.1 %collective-permute-start.30 = (bf16[384,768]{1,0:T(8,128)(2,1)}, bf16[384,768]{1,0:T(8,128)(2,1)}, u32[]{:S(2)}, u32[]{:S(2)}) collective-permute-start(bf16[384,768]{1,0:T(8,128)(2,1)} %get-tuple-element.297.a), channel_id=1, source_target_pairs={{0,8},{24,16},{1,9},{25,17},{2,10},{26,18},{3,11},{27,19},{4,12},{... | collective-permute-start | bytes 1769480 | tf_op jit(solution)/shard_map/ppermute | solution.py:344
  128.2 1.5 add.12.a
  130.5 2.5 %line_end.4.rest_0_ = f32[384,3072]{1,0:T(8,128)} custom-call(s32[1]{0:T(128)} %bitcast.place, bf16[384,768]{1,0:T(8,128)(2,1)} %add.10.total, bf16[384,768]{1,0:T(8,128)(2,1)} %collective-permute-done.26.arrived), custom_call_target="tpu_custom_call" | custom-call | tf_op jit(solution)/shard_map/line_end/pallas_call | solution.py:320
  133.1 1.3 collective-permute-start.32
  134.4 4.7 %attention_backward.4 = (bf16[384,3072]{1,0:T(8,128)(2,1)}, bf16[384,3072]{1,0:T(8,128)(2,1)}, bf16[384,3072]{1,0:T(8,128)(2,1)}) custom-call(s32[2]{0:T(128)S(1)} %get-tuple-element.344.order, bf16[288,768]{1,0:T(8,128)(2,1)S(1)} %copy-done.14, bf16[288,768]{1,0:T(8,128)(2,1)S(1)} %copy-done.14, bf16[96,768]{1,0:T(8,128)(2,1)S(1)} %collective-permute-done.29.grad_there, ...), custom_call_target="tpu_custom_call" | custom-call | tf_op jit(solution)/shard_map/attention_backward/pallas_call | solution.py:117
  139.2 1.4 add.13.a
  142.3 1.3 collective-permute-start.37
  143.6 7.5 %collective-permute-done.32.arrived = bf16[384,768]{1,0:T(8,128)(2,1)S(1)} collective-permute-done((bf16[384,768]{1,0:T(8,128)(2,1)S(1)}, bf16[384,768]{1,0:T(8,128)(2,1)S(1)}, u32[]{:S(2)}, u32[]{:S(2)}) %collective-permute-start.32) | collective-permute-done | bytes 589856 | tf_op jit(solution)/shard_map/ppermute | solution.py:358
  151.1 1.1 line_end.5.rest_0_
  152.2 4.7 %attention_backward.5 = (bf16[384,3072]{1,0:T(8,128)(2,1)}, bf16[384,3072]{1,0:T(8,128)(2,1)}, bf16[384,3072]{1,0:T(8,128)(2,1)}) custom-call(s32[2]{0:T(128)S(1)} %get-tuple-element.345.order, bf16[288,768]{1,0:T(8,128)(2,1)S(1)} %collective-permute-done.27.grad_main.grad_here, ...), custom_call_target="tpu_custom_call", output_to_operand_aliasing={{0}: (8, {}), {1}: (9, {}), {2}: (10, {})} | custom-call | tf_op jit(solution)/shard_map/attention_backward/pallas_call | solution.py:117
  157.1 1.3 collective-permute-start.39
  159.9 4.7 %attention_backward.6 = (bf16[384,3072]{1,0:T(8,128)(2,1)}, bf16[384,3072]{1,0:T(8,128)(2,1)}, bf16[384,3072]{1,0:T(8,128)(2,1)}) custom-call(s32[2]{0:T(128)S(1)} %get-tuple-element.346.order, bf16[288,768]{1,0:T(8,128)(2,1)S(1)} %collective-permute-done.28.grad_main.grad_here, ...), custom_call_target="tpu_custom_call", output_to_operand_aliasing={{0}: (8, {}), {1}: (9, {}), {2}: (10, {})} | custom-call | tf_op jit(solution)/shard_map/attention_backward/pallas_call | solution.py:117
  164.6 1.1 line_end.6.rest_0_
  165.7 4.7 %attention_backward.7 = (bf16[384,3072]{1,0:T(8,128)(2,1)}, bf16[384,3072]{1,0:T(8,128)(2,1)}, bf16[384,3072]{1,0:T(8,128)(2,1)}) custom-call(s32[2]{0:T(128)S(1)} %get-tuple-element.347.order, bf16[288,768]{1,0:T(8,128)(2,1)S(1)} %collective-permute-done.34.grad_main.grad_here, ...), custom_call_target="tpu_custom_call", output_to_operand_aliasing={{0}: (8, {}), {1}: (9, {}), {2}: (10, {})} | custom-call | tf_op jit(solution)/shard_map/attention_backward/pallas_call | solution.py:117
  170.5 5.5 %collective-permute-done.39.arrived = bf16[384,768]{1,0:T(8,128)(2,1)S(1)} collective-permute-done((bf16[384,768]{1,0:T(8,128)(2,1)S(1)}, bf16[384,768]{1,0:T(8,128)(2,1)S(1)}, u32[]{:S(2)}, u32[]{:S(2)}) %collective-permute-start.39) | collective-permute-done | bytes 589856 | tf_op jit(solution)/shard_map/ppermute | solution.py:358
  176.0 1.1 line_end.7
  (117 shorter events, 23.7 us)
Async XLA Ops:
  0.6 27.5 %collective-permute-start.3 = (bf16[384,3072]{1,0:T(8,128)(2,1)}, bf16[384,3072]{1,0:T(8,128)(2,1)}, u32[]{:S(2)}, u32[]{:S(2)}) collective-permute-start(bf16[384,3072]{1,0:T(8,128)(2,1)} %own.1), channel_id=1, source_target_pairs={{0,1},{1,0},{2,3},{3,2},{4,5},{5,4},{6,7},{7,6},{8,9},{9,8},{10,11... | collective-permute-start | bytes 7077896 | tf_op jit(solution)/shard_map/ppermute | solution.py:380
  3.5 8.1 %copy-start = (bf16[384,3072]{1,0:T(8,128)(2,1)S(1)}, bf16[384,3072]{1,0:T(8,128)(2,1)}, u32[]{:S(2)}) copy-start(bf16[384,3072]{1,0:T(8,128)(2,1)} %query.5) | copy-start | bytes 7077892
  3.5 8.1 %copy-start.1 = (bf16[384,3072]{1,0:T(8,128)(2,1)S(1)}, bf16[384,3072]{1,0:T(8,128)(2,1)}, u32[]{:S(2)}) copy-start(bf16[384,3072]{1,0:T(8,128)(2,1)} %key.5) | copy-start | bytes 7077892
  4.2 2.1 %collective-permute-start = (bf16[96,3072]{1,0:T(8,128)(2,1)S(1)}, bf16[96,3072]{1,0:T(8,128)(2,1)S(1)}, u32[]{:S(2)}, u32[]{:S(2)}) collective-permute-start(bf16[96,3072]{1,0:T(8,128)(2,1)S(1)} %other_quarter.1), channel_id=1, source_target_pairs={{0,1},{1,0},{2,3},{3,2},{4,5},{5,4},{6,7},{7,6},{8,9},{9,8},{10,11... | collective-permute-start | bytes 1769480 | tf_op jit(solution)/shard_map/ppermute | solution.py:380
  7.0 19.7 %collective-permute-start.1 = (bf16[240,1536]{1,0:T(8,128)(2,1)S(1)}, bf16[240,1536]{1,0:T(8,128)(2,1)S(1)}, u32[]{:S(2)}, u32[]{:S(2)}) collective-permute-start(bf16[240,1536]{1,0:T(8,128)(2,1)S(1)} %get-tuple-element.209.to_x), channel_id=1, source_target_pairs={{0,2},{1,3},{2,0},{3,1},{4,6},{5,7},{6,4},{7,5},{8,10},{9,11},{10,... | collective-permute-start | bytes 2211848 | tf_op jit(solution)/shard_map/ppermute | solution.py:380
  9.8 18.3 %collective-permute-start.2 = (bf16[240,1536]{1,0:T(8,128)(2,1)S(1)}, bf16[240,1536]{1,0:T(8,128)(2,1)S(1)}, u32[]{:S(2)}, u32[]{:S(2)}) collective-permute-start(bf16[240,1536]{1,0:T(8,128)(2,1)S(1)} %get-tuple-element.195.to_y), channel_id=1, source_target_pairs={{0,4},{1,5},{2,6},{3,7},{4,0},{5,1},{6,2},{7,3},{8,12},{9,13},{10,... | collective-permute-start | bytes 2211848 | tf_op jit(solution)/shard_map/ppermute | solution.py:380
  13.2 7.2 %copy-start.18 = (s32[384]{0:T(512)S(1)}, s32[384]{0:T(512)}, u32[]{:S(2)}) copy-start(s32[384]{0:T(512)} %ids.2) | copy-start | bytes 4612
  20.6 9.8 %collective-permute-start.4 = (bf16[96,1536]{1,0:T(8,128)(2,1)S(1)}, bf16[96,1536]{1,0:T(8,128)(2,1)S(1)}, u32[]{:S(2)}, u32[]{:S(2)}) collective-permute-start(bf16[96,1536]{1,0:T(8,128)(2,1)S(1)} %get-tuple-element.185), channel_id=1, source_target_pairs={{0,1},{1,0},{2,3},{3,2},{4,5},{5,4},{6,7},{7,6},{8,9},{9,8},{10,11... | collective-permute-start | bytes 884744 | tf_op jit(solution)/shard_map/ppermute | solution.py:380
  26.1 4.9 %collective-permute-start.5 = (bf16[96,1536]{1,0:T(8,128)(2,1)S(1)}, bf16[96,1536]{1,0:T(8,128)(2,1)S(1)}, u32[]{:S(2)}, u32[]{:S(2)}) collective-permute-start(bf16[96,1536]{1,0:T(8,128)(2,1)S(1)} %get-tuple-element.191), channel_id=1, source_target_pairs={{0,1},{1,0},{2,3},{3,2},{4,5},{5,4},{6,7},{7,6},{8,9},{9,8},{10,11... | collective-permute-start | bytes 884744 | tf_op jit(solution)/shard_map/ppermute | solution.py:380
  28.2 21.1 %collective-permute-start.6 = (bf16[144,1536]{1,0:T(8,128)(2,1)S(1)}, bf16[144,1536]{1,0:T(8,128)(2,1)S(1)}, u32[]{:S(2)}, u32[]{:S(2)}) collective-permute-start(bf16[144,1536]{1,0:T(8,128)(2,1)S(1)} %get-tuple-element.212.next_y), channel_id=1, source_target_pairs={{0,4},{1,5},{2,6},{3,7},{4,0},{5,1},{6,2},{7,3},{8,12},{9,13},{10,... | collective-permute-start | bytes 1327112 | tf_op jit(solution)/shard_map/ppermute | solution.py:380
  29.8 19.6 %collective-permute-start.7 = (bf16[144,1536]{1,0:T(8,128)(2,1)S(1)}, bf16[144,1536]{1,0:T(8,128)(2,1)S(1)}, u32[]{:S(2)}, u32[]{:S(2)}) collective-permute-start(bf16[144,1536]{1,0:T(8,128)(2,1)S(1)} %get-tuple-element.213.next_x), channel_id=1, source_target_pairs={{0,2},{1,3},{2,0},{3,1},{4,6},{5,7},{6,4},{7,5},{8,10},{9,11},{10,... | collective-permute-start | bytes 1327112 | tf_op jit(solution)/shard_map/ppermute | solution.py:380
  31.6 26.8 %collective-permute-start.9 = (bf16[288,768]{1,0:T(8,128)(2,1)S(1)}, bf16[288,768]{1,0:T(8,128)(2,1)S(1)}, u32[]{:S(2)}, u32[]{:S(2)}) collective-permute-start(bf16[288,768]{1,0:T(8,128)(2,1)S(1)} %get-tuple-element.207), channel_id=1, source_target_pairs={{0,4},{1,5},{2,6},{3,7},{4,0},{5,1},{6,2},{7,3},{8,12},{9,13},{10,... | collective-permute-start | bytes 1327112 | tf_op jit(solution)/shard_map/ppermute | solution.py:380
  32.0 17.6 %copy-start.9 = (bf16[384,3072]{1,0:T(8,128)(2,1)S(1)}, bf16[384,3072]{1,0:T(8,128)(2,1)}, u32[]{:S(2)}) copy-start(bf16[384,3072]{1,0:T(8,128)(2,1)} %own.1) | copy-start | bytes 7077892
  32.0 26.4 %collective-permute-start.10 = (bf16[288,768]{1,0:T(8,128)(2,1)S(1)}, bf16[288,768]{1,0:T(8,128)(2,1)S(1)}, u32[]{:S(2)}, u32[]{:S(2)}) collective-permute-start(bf16[288,768]{1,0:T(8,128)(2,1)S(1)} %get-tuple-element.208), channel_id=1, source_target_pairs={{0,6},{1,7},{2,4},{3,5},{4,2},{5,3},{6,0},{7,1},{8,14},{9,15},{10,... | collective-permute-start | bytes 1327112 | tf_op jit(solution)/shard_map/ppermute | solution.py:380
  34.6 25.0 %collective-permute-start.8 = (bf16[288,768]{1,0:T(8,128)(2,1)S(1)}, bf16[288,768]{1,0:T(8,128)(2,1)S(1)}, u32[]{:S(2)}, u32[]{:S(2)}) collective-permute-start(bf16[288,768]{1,0:T(8,128)(2,1)S(1)} %get-tuple-element.204), channel_id=1, source_target_pairs={{0,2},{1,3},{2,0},{3,1},{4,6},{5,7},{6,4},{7,5},{8,10},{9,11},{10,... | collective-permute-start | bytes 1327112 | tf_op jit(solution)/shard_map/ppermute | solution.py:380
  61.2 16.3 %collective-permute-start.14 = (bf16[240,1536]{1,0:T(8,128)(2,1)S(1)}, bf16[240,1536]{1,0:T(8,128)(2,1)S(1)}, u32[]{:S(2)}, u32[]{:S(2)}) collective-permute-start(bf16[240,1536]{1,0:T(8,128)(2,1)S(1)} %get-tuple-element.245.to_x), channel_id=1, source_target_pairs={{0,2},{1,3},{2,0},{3,1},{4,6},{5,7},{6,4},{7,5},{8,10},{9,11},{10,... | collective-permute-start | bytes 2211848 | tf_op jit(solution)/shard_map/ppermute | solution.py:380
  61.9 16.5 %collective-permute-start.15 = (bf16[240,1536]{1,0:T(8,128)(2,1)S(1)}, bf16[240,1536]{1,0:T(8,128)(2,1)S(1)}, u32[]{:S(2)}, u32[]{:S(2)}) collective-permute-start(bf16[240,1536]{1,0:T(8,128)(2,1)S(1)} %get-tuple-element.238.to_y), channel_id=1, source_target_pairs={{0,4},{1,5},{2,6},{3,7},{4,0},{5,1},{6,2},{7,3},{8,12},{9,13},{10,... | collective-permute-start | bytes 2211848 | tf_op jit(solution)/shard_map/ppermute | solution.py:380
  62.5 1.7 collective-permute-start.11
  62.5 2.3 %collective-permute-start.12 = (bf16[384,512]{1,0:T(8,128)(2,1)S(1)}, bf16[384,512]{1,0:T(8,128)(2,1)S(1)}, u32[]{:S(2)}, u32[]{:S(2)}) collective-permute-start(bf16[384,512]{1,0:T(8,128)(2,1)S(1)} %get-tuple-element.226), channel_id=1, source_target_pairs={{0,1},{1,0},{2,3},{3,2},{4,5},{5,4},{6,7},{7,6},{8,9},{9,8},{10,11... | collective-permute-start | bytes 1179656 | tf_op jit(solution)/shard_map/ppermute | solution.py:380
  63.0 2.3 %collective-permute-start.13 = (bf16[384,512]{1,0:T(8,128)(2,1)S(1)}, bf16[384,512]{1,0:T(8,128)(2,1)S(1)}, u32[]{:S(2)}, u32[]{:S(2)}) collective-permute-start(bf16[384,512]{1,0:T(8,128)(2,1)S(1)} %get-tuple-element.227), channel_id=1, source_target_pairs={{0,1},{1,0},{2,3},{3,2},{4,5},{5,4},{6,7},{7,6},{8,9},{9,8},{10,11... | collective-permute-start | bytes 1179656 | tf_op jit(solution)/shard_map/ppermute | solution.py:380
  66.7 17.1 %collective-permute-start.16 = (bf16[384,768]{1,0:T(8,128)(2,1)S(1)}, bf16[384,768]{1,0:T(8,128)(2,1)S(1)}, u32[]{:S(2)}, u32[]{:S(2)}) collective-permute-start(bf16[384,768]{1,0:T(8,128)(2,1)S(1)} %get-tuple-element.243.a), channel_id=1, source_target_pairs={{0,8},{24,16},{1,9},{25,17},{2,10},{26,18},{3,11},{27,19},{4,12},{... | collective-permute-start | bytes 1769480 | tf_op jit(solution)/shard_map/ppermute | solution.py:344
  70.2 25.5 %collective-permute-start.19 = (bf16[384,768]{1,0:T(8,128)(2,1)S(1)}, bf16[384,768]{1,0:T(8,128)(2,1)S(1)}, u32[]{:S(2)}, u32[]{:S(2)}) collective-permute-start(bf16[384,768]{1,0:T(8,128)(2,1)S(1)} %get-tuple-element.257.a), channel_id=1, source_target_pairs={{0,8},{24,16},{1,9},{25,17},{2,10},{26,18},{3,11},{27,19},{4,12},{... | collective-permute-start | bytes 1769480 | tf_op jit(solution)/shard_map/ppermute | solution.py:344
  78.5 8.9 %collective-permute-start.17 = (bf16[144,1536]{1,0:T(8,128)(2,1)S(1)}, bf16[144,1536]{1,0:T(8,128)(2,1)S(1)}, u32[]{:S(2)}, u32[]{:S(2)}) collective-permute-start(bf16[144,1536]{1,0:T(8,128)(2,1)S(1)} %get-tuple-element.248.next_y), channel_id=1, source_target_pairs={{0,4},{1,5},{2,6},{3,7},{4,0},{5,1},{6,2},{7,3},{8,12},{9,13},{10,... | collective-permute-start | bytes 1327112 | tf_op jit(solution)/shard_map/ppermute | solution.py:380
  79.1 8.6 %collective-permute-start.18 = (bf16[144,1536]{1,0:T(8,128)(2,1)S(1)}, bf16[144,1536]{1,0:T(8,128)(2,1)S(1)}, u32[]{:S(2)}, u32[]{:S(2)}) collective-permute-start(bf16[144,1536]{1,0:T(8,128)(2,1)S(1)} %get-tuple-element.249.next_x), channel_id=1, source_target_pairs={{0,2},{1,3},{2,0},{3,1},{4,6},{5,7},{6,4},{7,5},{8,10},{9,11},{10,... | collective-permute-start | bytes 1327112 | tf_op jit(solution)/shard_map/ppermute | solution.py:380
  84.0 22.8 %collective-permute-start.23 = (bf16[384,768]{1,0:T(8,128)(2,1)S(1)}, bf16[384,768]{1,0:T(8,128)(2,1)S(1)}, u32[]{:S(2)}, u32[]{:S(2)}) collective-permute-start(bf16[384,768]{1,0:T(8,128)(2,1)S(1)} %add.8.a), channel_id=1, source_target_pairs={{8,16},{16,8},{9,17},{17,9},{10,18},{18,10},{11,19},{19,11},{12,20... | collective-permute-start | bytes 1769480 | tf_op jit(solution)/shard_map/ppermute | solution.py:351
  89.3 7.2 %collective-permute-start.20 = (bf16[384,512]{1,0:T(8,128)(2,1)S(1)}, bf16[384,512]{1,0:T(8,128)(2,1)S(1)}, u32[]{:S(2)}, u32[]{:S(2)}) collective-permute-start(bf16[384,512]{1,0:T(8,128)(2,1)S(1)} %get-tuple-element.254), channel_id=1, source_target_pairs={{0,1},{1,0},{2,3},{3,2},{4,5},{5,4},{6,7},{7,6},{8,9},{9,8},{10,11... | collective-permute-start | bytes 1179656 | tf_op jit(solution)/shard_map/ppermute | solution.py:380
  89.4 7.2 %collective-permute-start.21 = (bf16[384,512]{1,0:T(8,128)(2,1)S(1)}, bf16[384,512]{1,0:T(8,128)(2,1)S(1)}, u32[]{:S(2)}, u32[]{:S(2)}) collective-permute-start(bf16[384,512]{1,0:T(8,128)(2,1)S(1)} %get-tuple-element.255), channel_id=1, source_target_pairs={{0,1},{1,0},{2,3},{3,2},{4,5},{5,4},{6,7},{7,6},{8,9},{9,8},{10,11... | collective-permute-start | bytes 1179656 | tf_op jit(solution)/shard_map/ppermute | solution.py:380
  89.9 6.7 %collective-permute-start.22 = (bf16[384,512]{1,0:T(8,128)(2,1)S(1)}, bf16[384,512]{1,0:T(8,128)(2,1)S(1)}, u32[]{:S(2)}, u32[]{:S(2)}) collective-permute-start(bf16[384,512]{1,0:T(8,128)(2,1)S(1)} %get-tuple-element.256), channel_id=1, source_target_pairs={{0,1},{1,0},{2,3},{3,2},{4,5},{5,4},{6,7},{7,6},{8,9},{9,8},{10,11... | collective-permute-start | bytes 1179656 | tf_op jit(solution)/shard_map/ppermute | solution.py:380
  95.8 23.2 %collective-permute-start.24 = (bf16[384,768]{1,0:T(8,128)(2,1)S(1)}, bf16[384,768]{1,0:T(8,128)(2,1)S(1)}, u32[]{:S(2)}, u32[]{:S(2)}) collective-permute-start(bf16[384,768]{1,0:T(8,128)(2,1)S(1)} %add.9.a), channel_id=1, source_target_pairs={{8,16},{16,8},{9,17},{17,9},{10,18},{18,10},{11,19},{19,11},{12,20... | collective-permute-start | bytes 1769480 | tf_op jit(solution)/shard_map/ppermute | solution.py:351
  98.8 29.4 %collective-permute-start.25 = (bf16[384,768]{1,0:T(8,128)(2,1)}, bf16[384,768]{1,0:T(8,128)(2,1)}, u32[]{:S(2)}, u32[]{:S(2)}) collective-permute-start(bf16[384,768]{1,0:T(8,128)(2,1)} %get-tuple-element.279.a), channel_id=1, source_target_pairs={{0,8},{24,16},{1,9},{25,17},{2,10},{26,18},{3,11},{27,19},{4,12},{... | collective-permute-start | bytes 1769480 | tf_op jit(solution)/shard_map/ppermute | solution.py:344
  107.7 22.7 %collective-permute-start.26 = (bf16[384,768]{1,0:T(8,128)(2,1)}, bf16[384,768]{1,0:T(8,128)(2,1)}, u32[]{:S(2)}, u32[]{:S(2)}) collective-permute-start(bf16[384,768]{1,0:T(8,128)(2,1)} %add.10.total), channel_id=1, source_target_pairs={{8,0},{16,24},{9,1},{17,25},{10,2},{18,26},{11,3},{19,27},{12,4},{... | collective-permute-start | bytes 1769480 | tf_op jit(solution)/shard_map/ppermute | solution.py:358
  116.0 16.9 %collective-permute-start.27 = (bf16[288,768]{1,0:T(8,128)(2,1)}, bf16[288,768]{1,0:T(8,128)(2,1)S(1)}, u32[]{:S(2)}, u32[]{:S(2)}) collective-permute-start(bf16[288,768]{1,0:T(8,128)(2,1)} %get-tuple-element.273), channel_id=1, source_target_pairs={{0,2},{1,3},{2,0},{3,1},{4,6},{5,7},{6,4},{7,5},{8,10},{9,11},{10,... | collective-permute-start | bytes 1327112 | tf_op jit(solution)/shard_map/ppermute | solution.py:380
  117.5 15.5 %collective-permute-start.28 = (bf16[288,768]{1,0:T(8,128)(2,1)}, bf16[288,768]{1,0:T(8,128)(2,1)S(1)}, u32[]{:S(2)}, u32[]{:S(2)}) collective-permute-start(bf16[288,768]{1,0:T(8,128)(2,1)} %get-tuple-element.274), channel_id=1, source_target_pairs={{0,4},{1,5},{2,6},{3,7},{4,0},{5,1},{6,2},{7,3},{8,12},{9,13},{10,... | collective-permute-start | bytes 1327112 | tf_op jit(solution)/shard_map/ppermute | solution.py:380
  119.8 19.4 %collective-permute-start.30 = (bf16[384,768]{1,0:T(8,128)(2,1)}, bf16[384,768]{1,0:T(8,128)(2,1)}, u32[]{:S(2)}, u32[]{:S(2)}) collective-permute-start(bf16[384,768]{1,0:T(8,128)(2,1)} %get-tuple-element.297.a), channel_id=1, source_target_pairs={{0,8},{24,16},{1,9},{25,17},{2,10},{26,18},{3,11},{27,19},{4,12},{... | collective-permute-start | bytes 1769480 | tf_op jit(solution)/shard_map/ppermute | solution.py:344
  128.0 6.4 %copy-start.14 = (bf16[288,768]{1,0:T(8,128)(2,1)S(1)}, bf16[288,768]{1,0:T(8,128)(2,1)}, u32[]{:S(2)}) copy-start(bf16[288,768]{1,0:T(8,128)(2,1)} %copy-done.13) | copy-start | bytes 1327108
  128.2 6.2 %copy-start.8 = (bf16[12,384,384]{2,1,0:T(8,128)(2,1)S(1)}, bf16[12,384,384]{2,1,0:T(8,128)(2,1)}, u32[]{:S(2)}) copy-start(bf16[12,384,384]{2,1,0:T(8,128)(2,1)} %copy-done.7) | copy-start | bytes 10616836
  129.7 12.4 %collective-permute-start.31 = (bf16[384,768]{1,0:T(8,128)(2,1)S(1)}, bf16[384,768]{1,0:T(8,128)(2,1)S(1)}, u32[]{:S(2)}, u32[]{:S(2)}) collective-permute-start(bf16[384,768]{1,0:T(8,128)(2,1)S(1)} %add.12.a), channel_id=1, source_target_pairs={{8,16},{16,8},{9,17},{17,9},{10,18},{18,10},{11,19},{19,11},{12,20... | collective-permute-start | bytes 1769480 | tf_op jit(solution)/shard_map/ppermute | solution.py:351
  133.0 1.4 collective-permute-start.29
  133.1 18.0 %collective-permute-start.32 = (bf16[384,768]{1,0:T(8,128)(2,1)S(1)}, bf16[384,768]{1,0:T(8,128)(2,1)S(1)}, u32[]{:S(2)}, u32[]{:S(2)}) collective-permute-start(bf16[384,768]{1,0:T(8,128)(2,1)S(1)} %add.11.total), channel_id=1, source_target_pairs={{8,0},{16,24},{9,1},{17,25},{10,2},{18,26},{11,3},{19,27},{12,4},{... | collective-permute-start | bytes 1769480 | tf_op jit(solution)/shard_map/ppermute | solution.py:358
  134.4 6.9 %copy-start.20 = (bf16[288,768]{1,0:T(8,128)(2,1)S(1)}, bf16[288,768]{1,0:T(8,128)(2,1)}, u32[]{:S(2)}) copy-start(bf16[288,768]{1,0:T(8,128)(2,1)} %copy-done.19) | copy-start | bytes 1327108
  140.6 16.4 %collective-permute-start.35 = (bf16[384,768]{1,0:T(8,128)(2,1)S(1)}, bf16[384,768]{1,0:T(8,128)(2,1)S(1)}, u32[]{:S(2)}, u32[]{:S(2)}) collective-permute-start(bf16[384,768]{1,0:T(8,128)(2,1)S(1)} %add.13.a), channel_id=1, source_target_pairs={{8,16},{16,8},{9,17},{17,9},{10,18},{18,10},{11,19},{19,11},{12,20... | collective-permute-start | bytes 1769480 | tf_op jit(solution)/shard_map/ppermute | solution.py:351
  141.3 15.6 %collective-permute-start.34 = (bf16[288,768]{1,0:T(8,128)(2,1)S(1)}, bf16[288,768]{1,0:T(8,128)(2,1)S(1)}, u32[]{:S(2)}, u32[]{:S(2)}) collective-permute-start(bf16[288,768]{1,0:T(8,128)(2,1)S(1)} %copy-done.20), channel_id=1, source_target_pairs={{0,6},{1,7},{2,4},{3,5},{4,2},{5,3},{6,0},{7,1},{8,14},{9,15},{10,... | collective-permute-start | bytes 1327112 | tf_op jit(solution)/shard_map/ppermute | solution.py:380
  141.9 10.3 %collective-permute-start.33 = (bf16[96,768]{1,0:T(8,128)(2,1)S(1)}, bf16[96,768]{1,0:T(8,128)(2,1)S(1)}, u32[]{:S(2)}, u32[]{:S(2)}) collective-permute-start(bf16[96,768]{1,0:T(8,128)(2,1)S(1)} %slice.33), channel_id=1, source_target_pairs={{0,1},{1,0},{2,3},{3,2},{4,5},{5,4},{6,7},{7,6},{8,9},{9,8},{10,11... | collective-permute-start | bytes 442376 | tf_op jit(solution)/shard_map/ppermute | solution.py:380
  142.3 22.3 %collective-permute-start.37 = (bf16[384,768]{1,0:T(8,128)(2,1)S(1)}, bf16[384,768]{1,0:T(8,128)(2,1)S(1)}, u32[]{:S(2)}, u32[]{:S(2)}) collective-permute-start(bf16[384,768]{1,0:T(8,128)(2,1)S(1)} %add.14.total), channel_id=1, source_target_pairs={{8,0},{16,24},{9,1},{17,25},{10,2},{18,26},{11,3},{19,27},{12,4},{... | collective-permute-start | bytes 1769480 | tf_op jit(solution)/shard_map/ppermute | solution.py:358
  152.2 7.7 %copy-start.6 = (bf16[12,384,384]{2,1,0:T(8,128)(2,1)S(1)}, bf16[12,384,384]{2,1,0:T(8,128)(2,1)}, u32[]{:S(2)}) copy-start(bf16[12,384,384]{2,1,0:T(8,128)(2,1)} %copy-done.5) | copy-start | bytes 10616836
  157.1 18.8 %collective-permute-start.39 = (bf16[384,768]{1,0:T(8,128)(2,1)S(1)}, bf16[384,768]{1,0:T(8,128)(2,1)S(1)}, u32[]{:S(2)}, u32[]{:S(2)}) collective-permute-start(bf16[384,768]{1,0:T(8,128)(2,1)S(1)} %add.15.total), channel_id=1, source_target_pairs={{8,0},{16,24},{9,1},{17,25},{10,2},{18,26},{11,3},{19,27},{12,4},{... | collective-permute-start | bytes 1769480 | tf_op jit(solution)/shard_map/ppermute | solution.py:358
  158.4 1.4 collective-permute-start.36
  158.5 7.2 %collective-permute-start.38 = (bf16[96,768]{1,0:T(8,128)(2,1)S(1)}, bf16[96,768]{1,0:T(8,128)(2,1)S(1)}, u32[]{:S(2)}, u32[]{:S(2)}) collective-permute-start(bf16[96,768]{1,0:T(8,128)(2,1)S(1)} %slice.35), channel_id=1, source_target_pairs={{0,1},{1,0},{2,3},{3,2},{4,5},{5,4},{6,7},{7,6},{8,9},{9,8},{10,11... | collective-permute-start | bytes 442376 | tf_op jit(solution)/shard_map/ppermute | solution.py:380
  (13 other events, 26.8 us)

commit v3 on v2

--- a/solution.py
+++ b/solution.py
@@ -86,17 +86,12 @@
     )(order, segment_ids.reshape(rows, 1), segment_ids.reshape(1, rows), query_rows, key_rows, value_rows)
 
 
-def backward_kernel(order, grad_main, grad_here, grad_there, query, key, value, weights, *rest):
+def backward_kernel(order, grad_rows, query, key, value, weights, *rest):
     grad_query, grad_key, grad_value = rest[-3:]
-    first = order[0] % 2 == 0
-    here, there = grad_here[...], grad_there[...]
-    grad_all = jnp.concatenate(
-        [grad_main[...], jnp.where(first, here, there), jnp.where(first, there, here)], axis=0
-    )
     inverse_root = 1.0 / math.sqrt(E)
     for head in range(BLOCK_HEADS):
         columns = slice(head * E, (head + 1) * E)
-        grad = grad_all[:, columns]
+        grad = grad_rows[:, columns]
         half = weights[head]
         grad_probs = dot(value[:, columns], grad, 1, 1)
         wide = half.astype(F32)
@@ -107,9 +102,8 @@
         grad_query[:, columns] = (dot(grad_logits, key[:, columns], 0, 0) * inverse_root).astype(BF16)
 
 
-def backward(order, grad, there, flip, there_skip, query_rows, key_rows, value_rows, weights, skip, done):
+def backward(order, grad, query_rows, key_rows, value_rows, weights, skip, done):
     rows, width = query_rows.shape
-    quarter = there.shape[0]
     blocks = order.shape[0]
     heads = blocks * BLOCK_HEADS
     absolute = pl.BlockSpec((rows, BLOCK), lambda j, order: (0, order[j]))
@@ -120,9 +114,7 @@
             num_scalar_prefetch=1,
             grid=(blocks,),
             in_specs=[
-                pl.BlockSpec((2 * quarter, BLOCK), lambda j, order: (0, j)),
-                pl.BlockSpec((quarter, BLOCK), lambda j, order: (2, j)),
-                pl.BlockSpec((quarter, BLOCK), lambda j, order: (0, (j ^ flip) + there_skip)),
+                pl.BlockSpec((rows, BLOCK), lambda j, order: (0, j)),
                 absolute,
                 absolute,
                 absolute,
@@ -132,11 +124,11 @@
             out_specs=[absolute, absolute, absolute],
         ),
         out_shape=shapes,
-        input_output_aliases={8 + i: i for i in range(len(done))},
+        input_output_aliases={6 + i: i for i in range(len(done))},
         compiler_params=pltpu.CompilerParams(vmem_limit_bytes=ATTENTION_VMEM_LIMIT),
         cost_estimate=NO_COST,
         name="attention_backward",
-    )(order, grad, grad, there, query_rows, key_rows, value_rows, weights, *done)
+    )(order, grad, query_rows, key_rows, value_rows, weights, *done)
 
 
 def whole(kernel, shapes, *arrays, scalars=(), name):
@@ -230,21 +222,18 @@
     gathered[4 * short :] = (kept[short:] + from_x[short:]) + (from_y[short:] + from_far[short:])
 
 
-def term_other_kernel(attended, plane, *outs):
-    share = dot(attended[:, BLOCK:], plane[...], 0, 0).astype(BF16)
-    width = share.shape[1] // len(outs)
+def term_other_kernel(begin, attended, plane, *outs):
+    width = outs[0].shape[1]
+    share = dot(attended[:, BLOCK:], plane[:, begin : begin + len(outs) * width], 0, 0).astype(BF16)
     for i, out in enumerate(outs):
         out[...] = share[:, i * width : (i + 1) * width]
 
 
-def term_own_kernel(attended, plane, *refs):
-    arrived, outs = refs[:-2], refs[-2:]
-    own = dot(attended[:, :BLOCK], plane[...], 0, 0)
+def term_own_kernel(begin, attended, plane, *refs):
+    arrived, out = refs[:-1], refs[-1]
+    own = dot(attended[:, :BLOCK], plane[:, begin : begin + out.shape[1]], 0, 0)
     there = jnp.concatenate([a[...] for a in arrived], axis=1)
-    total = (own + there.astype(F32)).astype(BF16)
-    width = outs[0].shape[1]
-    for i, out in enumerate(outs):
-        out[...] = total[:, i * width : (i + 1) * width]
+    out[...] = (own + there.astype(F32)).astype(BF16)
 
 
 def grad_kernel(plane, own, other, *rest):
@@ -256,16 +245,24 @@
         rest[-1][:, columns] = share
 
 
-def grad_end_kernel(plane, own, other, before, *pieces):
-    rows = pieces[0].shape[0]
-    short = rows * 2 // 3
+def grad_end_kernel(plane, own, other, before, main, extra):
+    rows = main.shape[0]
     for i, weight in enumerate((own, other)):
         columns = slice(i * BLOCK, (i + 1) * BLOCK)
         total = (before[:, columns] + dot(plane[...], weight[...], 1, 1)).astype(BF16)
-        for j, piece in enumerate(pieces[:-1]):
-            piece[:short, columns] = total[j * short : (j + 1) * short]
-            piece[short:, columns] = total[4 * short :]
-        pieces[-1][:, columns] = total[4 * short :]
+        main[:, columns] = total[:rows]
+        extra[:, columns] = total[rows:]
+
+
+def grad_pack_kernel(blocks, main, extra, arrived, *outs):
+    short = main.shape[0] // len(outs)
+    quarter = extra.shape[0]
+    first = blocks[0] % 2 == 0
+    there = jnp.concatenate([arrived[:, BLOCK:], arrived[:, :BLOCK]], axis=1)
+    for i, out in enumerate(outs):
+        out[:short] = main[i * short : (i + 1) * short]
+        out[short : short + quarter] = jnp.where(first, extra[...], there)
+        out[short + quarter :] = jnp.where(first, there, extra[...])
 
 
 def grad_part(part, plane, own_weight, other_weight, before):
@@ -273,14 +270,14 @@
     weight = pl.BlockSpec((BLOCK, width), lambda i: (0, part))
     result = pl.BlockSpec((count, PAIR), lambda i: (0, 0))
     last = part == PARTS - 1
-    rows = count // 3
-    piece = pl.BlockSpec((rows, PAIR), lambda i: (0, 0))
+    extra = count // 9
+    outs = [(count - extra, PAIR), (extra, PAIR)]
     return pl.pallas_call(
         grad_end_kernel if last else grad_kernel,
         grid=(1,),
         in_specs=[pl.BlockSpec((count, width), lambda i: (0, 0)), weight, weight] + [result] * len(before),
-        out_specs=[piece] * 4 + [pl.BlockSpec((rows // 3, PAIR), lambda i: (0, 0))] if last else [result],
-        out_shape=[jax.ShapeDtypeStruct((rows, PAIR), BF16)] * 4 + [jax.ShapeDtypeStruct((rows // 3, PAIR), BF16)]
+        out_specs=[pl.BlockSpec(shape, lambda i: (0, 0)) for shape in outs] if last else [result],
+        out_shape=[jax.ShapeDtypeStruct(shape, BF16) for shape in outs]
         if last
         else [jax.ShapeDtypeStruct((count, PAIR), F32)],
         compiler_params=pltpu.CompilerParams(vmem_limit_bytes=VMEM_LIMIT),
@@ -419,18 +416,22 @@
         order.mark(*share)
         return share
 
-    def term_other(plane, attended):
+    piece_width = part_width // 2
+
+    def term_other(piece, plane, attended):
         plane, attended = order(plane, attended)
-        shape = (BLOCK, part_width // SHARES)
-        share = whole(term_other_kernel, [shape] * SHARES, attended, plane, name="term_other")
+        shape = (BLOCK, piece_width // SHARES)
+        kernel = functools.partial(term_other_kernel, piece % 2 * piece_width)
+        share = whole(kernel, [shape] * SHARES, attended, plane, name="term_other")
         order.mark(*share)
-        return [swap(piece, 1) for piece in share]
-
-    def term_own(plane, attended, arrived):
+        return [swap(transfer, 1) for transfer in share]
+
+    def term_own(piece, plane, attended, arrived):
         held = order(attended, plane, *arrived)
-        pieces = whole(term_own_kernel, [(BLOCK, part_width // 2)] * 2, *held, name="term_own")
-        order.mark(*pieces)
-        return pieces
+        kernel = functools.partial(term_own_kernel, piece % 2 * piece_width)
+        (total,) = whole(kernel, [(BLOCK, piece_width)], *held, name="term_own")
+        order.mark(total)
+        line.start(piece, total)
 
     def attend(half):
         held = order(segment_ids, query_rows, key_rows, value_rows)
@@ -460,53 +461,49 @@
     (gathered,) = whole(collect_kernel, [(4 * short + quarter, PAIR)], *held, name="collect")
     order.mark(gathered)
 
-    arriving = term_other(plane, gathered)
+    arriving = term_other(0, plane, gathered)
     gather_start(1)
-    pieces = term_own(plane, gathered, arriving)
-    line.start(0, pieces[0])
-    line.start(1, pieces[1])
+    term_own(0, plane, gathered, arriving)
+    term_own(1, plane, gathered, term_other(1, plane, gathered))
     gather_forward(1)
     line.across(0)
     plane = gather_end(1)
-    arriving = term_other(plane, gathered)
+    term_own(2, plane, gathered, term_other(2, plane, gathered))
     line.across(1)
-    pieces = term_own(plane, gathered, arriving)
-    line.start(2, pieces[0])
+    arriving = term_other(3, plane, gathered)
     line.back(0)
-    line.start(3, order(pieces[1]))
-    *piece, own_tail = grad_step(1, plane, grad)
-    moved_x, moved_y = swap(piece[1], 2), swap(piece[2], 4)
+    term_own(3, plane, gathered, arriving)
+    grad_main, grad_extra = grad_step(1, plane, grad)
+    held = order(grad_main, grad_extra, swap(grad_extra, 1))
+    shape = (rows, PAIR)
+    grad_rows = whole(grad_pack_kernel, [shape] * 4, *held, scalars=(blocks,), name="grad_pack")
+    order.mark(*grad_rows)
+    moved_x, moved_y = swap(grad_rows[1], 2), swap(grad_rows[2], 4)
+    line.across(2)
     line.back(1)
-    line.across(2)
-    line.finish(0, 0)
-
-    own_tail, moved_x, moved_y = order(own_tail, moved_x, moved_y)
-    tails = [own_tail, moved_x[short:], moved_y[short:]]
-    order.mark(*tails)
-    there = [swap(tail, 1) for tail in tails]
-    moved_far = swap(order(piece[3]), 6)
+
     grads = ()
 
-    def finish(i, grad, there):
+    def finish(i, grad):
         weights = weights_near if i < 2 else weights_far
-        held = order(grad, there, query_rows, key_rows, value_rows, weights)
-        result = backward(blocks[2 * i : 2 * i + 2], held[0], held[1], 1, 0, *held[2:], 2 * (i % 2), grads)
+        held = order(grad, query_rows, key_rows, value_rows, weights)
+        result = backward(blocks[2 * i : 2 * i + 2], *held, 2 * (i % 2), grads)
         order.mark(*result)
         return tuple(result)
 
-    grads = finish(0, piece[0], there[0])
+    grads = finish(0, grad_rows[0])
     line.across(3)
+    line.finish(0, 0)
     line.back(2)
     line.finish(1, part_width // 2)
-    grads = finish(1, moved_x, there[1])
-    moved_far = order(moved_far)
-    tail = moved_far[short:]
-    order.mark(tail)
-    far_there = swap(tail, 1)
+    moved_x, moved_y = order(moved_x, moved_y)
+    order.mark(moved_x, moved_y)
+    moved_far = swap(order(grad_rows[3]), 6)
+    grads = finish(1, moved_x)
     line.back(3)
-    grads = finish(2, moved_y, there[2])
+    grads = finish(2, moved_y)
     line.finish(2, part_width)
-    grads = finish(3, moved_far, far_there)
+    grads = finish(3, moved_far)
     line.finish(3, part_width + part_width // 2)
     return (*grads, *line.done)
 
@@ -534,10 +531,8 @@
         grad[: count * short], "fsdp", split_axis=0, concat_axis=1, tiled=True
     )
     grad_extra = lax.all_gather(grad[count * short :], "fsdp", axis=1, tiled=True)
-    half = short // 2
-    grad = jnp.concatenate([grad_main, grad_extra[:half]])
-    there = grad_extra[half:]
-    grads = backward(order, grad, there, 0, 0, query_rows, key_rows, value_rows, weights, 0, ())
+    grad = jnp.concatenate([grad_main, grad_extra])
+    grads = backward(order, grad, query_rows, key_rows, value_rows, weights, 0, ())
     return (*grads, total * (1.0 / math.sqrt(rows * count * lax.axis_size("rep"))))
 
 

time: 178 us -> 169 us (0.949)
  waiting for transfers between devices: 58.7 us -> 47.2 us
  local copies, waits for them, and re-layouts: 10.7 us -> 6.97 us
  starting transfers between devices: 47 us -> 50.4 us
  Pallas kernels: 59.5 us -> 62.4 us
    ppermute x4, waiting for transfers between devices: 9.06 us -> 0.01 us  [start(): self.arriving[piece] = lax.ppermute(part, 'rep', [(0, 1), (3, 2)])]
    ppermute x4, waiting for transfers between devices: 13 us -> 7.73 us  [back(): self.arriving[piece] = lax.ppermute(total, 'rep', [(1, 0), (2, 3)])]
    unnamed x42 -> x34, local copies, waits for them, and re-layouts: 10.4 us -> 6.61 us
    ppermute x28 -> x31, waiting for transfers between devices: 36.6 us -> 39.5 us  [swap(): return lax.ppermute(a, 'fsdp', [(f, f ^ mask) for f in range(8)])]
    pallas_call x20 -> x25, Pallas kernels: 13.6 us -> 16 us  [whole(): pl.pallas_call(kernel, in_specs=[smem] * len(scalars) + [vmem] * len(arra...]
    ppermute x28 -> x31, starting transfers between devices: 20.1 us -> 22.4 us  [swap(): return lax.ppermute(a, 'fsdp', [(f, f ^ mask) for f in range(8)])]
  transfers between devices with their start and end apart: 40 -> 43, of which waited for: 17 -> 26; matrix products, arithmetic and copies ran while one was open for 0% -> 0% of each run, Pallas kernels for 32% -> 36%
where the time goes in v3:
time: 169 us; the launch traced here: 168 us
  Pallas kernels  62.4 us (37%)
  starting transfers between devices  50.4 us (30%)
  waiting for transfers between devices  47.2 us (28%)
  local copies, waits for them, and re-layouts  6.97 us (4%)
    ppermute x31, waiting for transfers between devices, swap(): return lax.ppermute(a, 'fsdp', [(f, f ^ mask) for f in range(8)])  39.5 us
    ppermute x31, starting transfers between devices, swap(): return lax.ppermute(a, 'fsdp', [(f, f ^ mask) for f in range(8)])  22.4 us
    pallas_call x4, Pallas kernels, backward(): pl.pallas_call(backward_kernel, grid_spec=pltpu.PrefetchScalarGridSpec(nu...  20.5 us
    ppermute x4, starting transfers between devices, start(): self.arriving[piece] = lax.ppermute(part, 'rep', [(0, 1), (3, 2)])  17.8 us
    pallas_call x25, Pallas kernels, whole(): pl.pallas_call(kernel, in_specs=[smem] * len(scalars) + [vmem] * len(arra...  16 us
    pallas_call x2, Pallas kernels, forward(): pl.pallas_call(forward_kernel, grid_spec=pltpu.PrefetchScalarGridSpec(num...  10.9 us
    pallas_call x2, Pallas kernels, grad_part(): pl.pallas_call(grad_end_kernel if last else grad_kernel, grid=(1,), in_sp...  8.52 us
    ppermute x4, waiting for transfers between devices, back(): self.arriving[piece] = lax.ppermute(total, 'rep', [(1, 0), (2, 3)])  7.73 us
  transfers between devices with their start and end apart: 43, of which 26 were waited for; matrix products, arithmetic and copies ran while one was open for 0% of the time, Pallas kernels for 36%

profile of v3, /device:TPU:0, one launch (start us, length us, event | category | flops | bytes accessed | tf_op | source)
XLA Modules:
  0.0 168.1 jit_solution(14435720402354756973)
XLA Ops:
  1.2 1.7 copy-done.10
  4.3 1.9 %collective-permute-done.arrived = bf16[96,3072]{1,0:T(8,128)(2,1)S(1)} collective-permute-done((bf16[96,3072]{1,0:T(8,128)(2,1)S(1)}, bf16[96,3072]{1,0:T(8,128)(2,1)S(1)}, u32[]{:S(2)}, u32[]{:S(2)}) %collective-permute-start) | collective-permute-done | bytes 589856 | tf_op jit(solution)/shard_map/ppermute | solution.py:377
  7.0 2.9 %collective-permute-start.1 = (bf16[240,1536]{1,0:T(8,128)(2,1)S(1)}, bf16[240,1536]{1,0:T(8,128)(2,1)S(1)}, u32[]{:S(2)}, u32[]{:S(2)}) collective-permute-start(bf16[240,1536]{1,0:T(8,128)(2,1)S(1)} %get-tuple-element.222.to_x), channel_id=1, source_target_pairs={{0,2},{1,3},{2,0},{3,1},{4,6},{5,7},{6,4},{7,5},{8,10},{9,11},{10,... | collective-permute-start | bytes 2211848 | tf_op jit(solution)/shard_map/ppermute | solution.py:377
  9.8 1.5 collective-permute-start.2
  11.6 1.7 copy-done.3
  13.2 5.4 %attention_forward.2 = (bf16[384,1536]{1,0:T(8,128)(2,1)S(1)}, bf16[96,1536]{1,0:T(8,128)(2,1)S(1)}, bf16[12,384,384]{2,1,0:T(8,128)(2,1)S(1)}) custom-call(s32[4]{0:T(128)S(1)} %get-tuple-element.368.order, s32[384,1]{1,0:T(8,128)S(1)} %reshape.28.ids_column, s32[1,384]{1,0:T(1,128)S(1)} %reshape.25.ids_row, bf16[384,3072]{1,0:T(8,128)(2,1)S(1)} %copy-done, ...), custom_call_target="tpu_custom_call" | custom-call | tf_op jit(solution)/shard_map/attention_forward/pallas_call | solution.py:59
  18.9 5.4 %attention_forward.3 = (bf16[384,1536]{1,0:T(8,128)(2,1)S(1)}, bf16[96,1536]{1,0:T(8,128)(2,1)S(1)}, bf16[12,384,384]{2,1,0:T(8,128)(2,1)S(1)}) custom-call(s32[4]{0:T(128)S(1)} %get-tuple-element.369.order, s32[384,1]{1,0:T(8,128)S(1)} %reshape.29.ids_column, s32[1,384]{1,0:T(1,128)S(1)} %reshape.27.ids_row, bf16[384,3072]{1,0:T(8,128)(2,1)S(1)} %copy-done, ...), custom_call_target="tpu_custom_call" | custom-call | tf_op jit(solution)/shard_map/attention_forward/pallas_call | solution.py:59
  24.9 1.8 %collective-permute-done.1.from_x = bf16[240,1536]{1,0:T(8,128)(2,1)S(1)} collective-permute-done((bf16[240,1536]{1,0:T(8,128)(2,1)S(1)}, bf16[240,1536]{1,0:T(8,128)(2,1)S(1)}, u32[]{:S(2)}, u32[]{:S(2)}) %collective-permute-start.1) | collective-permute-done | bytes 737312 | tf_op jit(solution)/shard_map/ppermute | solution.py:377
  26.7 1.5 collective-permute-done.2.from_y
  28.2 1.6 collective-permute-start.6
  31.0 1.6 collective-permute-start.8
  33.7 1.5 collective-permute-start.10
  35.2 6.2 %collective-permute-done.6.via_y = bf16[144,1536]{1,0:T(8,128)(2,1)S(1)} collective-permute-done((bf16[144,1536]{1,0:T(8,128)(2,1)S(1)}, bf16[144,1536]{1,0:T(8,128)(2,1)S(1)}, u32[]{:S(2)}, u32[]{:S(2)}) %collective-permute-start.6) | collective-permute-done | bytes 442400 | tf_op jit(solution)/shard_map/ppermute | solution.py:377
  41.4 1.5 collective-permute-done.7.via_x
  43.1 4.2 %grad_attended.2.before = f32[864,768]{1,0:T(8,128)S(1)} custom-call(bf16[864,1536]{1,0:T(8,128)(2,1)S(1)} %gather_end.2.plane, bf16[384,3072]{1,0:T(8,128)(2,1)S(1)} %copy-done.9, bf16[384,3072]{1,0:T(8,128)(2,1)} %collective-permute-done.3.other), custom_call_target="tpu_custom_call" | custom-call | tf_op jit(solution)/shard_map/grad_attended/pallas_call | solution.py:275
  47.4 5.0 %collective-permute-done.8.from_x = bf16[288,768]{1,0:T(8,128)(2,1)S(1)} collective-permute-done((bf16[288,768]{1,0:T(8,128)(2,1)S(1)}, bf16[288,768]{1,0:T(8,128)(2,1)S(1)}, u32[]{:S(2)}, u32[]{:S(2)}) %collective-permute-start.8) | collective-permute-done | bytes 442400 | tf_op jit(solution)/shard_map/ppermute | solution.py:377
  52.4 7.2 %collective-permute-done.10.from_far = bf16[288,768]{1,0:T(8,128)(2,1)S(1)} collective-permute-done((bf16[288,768]{1,0:T(8,128)(2,1)S(1)}, bf16[288,768]{1,0:T(8,128)(2,1)S(1)}, u32[]{:S(2)}, u32[]{:S(2)}) %collective-permute-start.10) | collective-permute-done | bytes 442400 | tf_op jit(solution)/shard_map/ppermute | solution.py:377
  61.3 1.4 collective-permute-start.18
  65.6 3.5 %collective-permute-start.19 = (bf16[384,768]{1,0:T(8,128)(2,1)S(1)}, bf16[384,768]{1,0:T(8,128)(2,1)S(1)}, u32[]{:S(2)}, u32[]{:S(2)}) collective-permute-start(bf16[384,768]{1,0:T(8,128)(2,1)S(1)} %term_own.4.a), channel_id=1, source_target_pairs={{0,8},{24,16},{1,9},{25,17},{2,10},{26,18},{3,11},{27,19},{4,12},{... | collective-permute-start | bytes 1769480 | tf_op jit(solution)/shard_map/ppermute | solution.py:341
  71.7 1.2 collective-permute-done.16.refs_2_
  73.7 3.2 %collective-permute-done.17.from_x = bf16[240,1536]{1,0:T(8,128)(2,1)S(1)} collective-permute-done((bf16[240,1536]{1,0:T(8,128)(2,1)S(1)}, bf16[240,1536]{1,0:T(8,128)(2,1)S(1)}, u32[]{:S(2)}, u32[]{:S(2)}) %collective-permute-start.17) | collective-permute-done | bytes 737312 | tf_op jit(solution)/shard_map/ppermute | solution.py:377
  77.9 1.5 collective-permute-start.20
  79.4 1.4 collective-permute-start.21
  80.8 3.5 %collective-permute-start.25 = (bf16[384,768]{1,0:T(8,128)(2,1)S(1)}, bf16[384,768]{1,0:T(8,128)(2,1)S(1)}, u32[]{:S(2)}, u32[]{:S(2)}) collective-permute-start(bf16[384,768]{1,0:T(8,128)(2,1)S(1)} %term_own.5.a), channel_id=1, source_target_pairs={{0,8},{24,16},{1,9},{25,17},{2,10},{26,18},{3,11},{27,19},{4,12},{... | collective-permute-start | bytes 1769480 | tf_op jit(solution)/shard_map/ppermute | solution.py:341
  85.2 1.9 %collective-permute-done.20.via_y = bf16[144,1536]{1,0:T(8,128)(2,1)S(1)} collective-permute-done((bf16[144,1536]{1,0:T(8,128)(2,1)S(1)}, bf16[144,1536]{1,0:T(8,128)(2,1)S(1)}, u32[]{:S(2)}, u32[]{:S(2)}) %collective-permute-start.20) | collective-permute-done | bytes 442400 | tf_op jit(solution)/shard_map/ppermute | solution.py:377
  91.6 3.5 %collective-permute-start.31 = (bf16[384,768]{1,0:T(8,128)(2,1)S(1)}, bf16[384,768]{1,0:T(8,128)(2,1)S(1)}, u32[]{:S(2)}, u32[]{:S(2)}) collective-permute-start(bf16[384,768]{1,0:T(8,128)(2,1)S(1)} %term_own.6.a), channel_id=1, source_target_pairs={{0,8},{24,16},{1,9},{25,17},{2,10},{26,18},{3,11},{27,19},{4,12},{... | collective-permute-start | bytes 1769480 | tf_op jit(solution)/shard_map/ppermute | solution.py:341
  99.9 7.3 %collective-permute-start.33 = (bf16[384,768]{1,0:T(8,128)(2,1)S(1)}, bf16[384,768]{1,0:T(8,128)(2,1)S(1)}, u32[]{:S(2)}, u32[]{:S(2)}) collective-permute-start(bf16[384,768]{1,0:T(8,128)(2,1)S(1)} %term_own.7.a), channel_id=1, source_target_pairs={{0,8},{24,16},{1,9},{25,17},{2,10},{26,18},{3,11},{27,19},{4,12},{... | collective-permute-start | bytes 1769480 | tf_op jit(solution)/shard_map/ppermute | solution.py:341
  107.2 1.3 collective-permute-start.34
  108.5 4.3 %grad_attended.3 = (bf16[768,768]{1,0:T(8,128)(2,1)S(1)}, bf16[96,768]{1,0:T(8,128)(2,1)S(1)}) custom-call(bf16[864,1536]{1,0:T(8,128)(2,1)S(1)} %gather_end.3.plane, bf16[384,3072]{1,0:T(8,128)(2,1)S(1)} %copy-done.9, bf16[384,3072]{1,0:T(8,128)(2,1)} %collective-permute-done.3.other, f32[864,768]{1,0:T(8,128)S(1)} %grad_attended.2.before), custom_call_target="tpu_custom_call" | custom-call | tf_op jit(solution)/shard_map/grad_attended/pallas_call | solution.py:275
  112.8 1.4 collective-permute-done.30.arrived
  114.2 1.7 %grad_pack.1 = (bf16[384,768]{1,0:T(8,128)(2,1)S(1)}, bf16[384,768]{1,0:T(8,128)(2,1)}, bf16[384,768]{1,0:T(8,128)(2,1)}, bf16[384,768]{1,0:T(8,128)(2,1)S(1)}) custom-call(s32[8]{0:T(128)S(1)} %iota_xor_fusion.blocks, bf16[768,768]{1,0:T(8,128)(2,1)S(1)} %get-tuple-element.303.main, bf16[96,768]{1,0:T(8,128)(2,1)S(1)} %get-tuple-element.304.extra, ...), custom_call_target="tpu_custom_call" | custom-call | tf_op jit(solution)/shard_map/grad_pack/pallas_call | solution.py:136
  116.7 1.5 collective-permute-start.35
  119.3 1.3 collective-permute-start.36
  120.6 1.4 collective-permute-start.37
  122.6 4.7 %attention_backward.4 = (bf16[384,3072]{1,0:T(8,128)(2,1)}, bf16[384,3072]{1,0:T(8,128)(2,1)}, bf16[384,3072]{1,0:T(8,128)(2,1)}) custom-call(s32[2]{0:T(128)S(1)} %get-tuple-element.370.order, bf16[384,768]{1,0:T(8,128)(2,1)S(1)} %get-tuple-element.315.grad_rows, bf16[384,3072]{1,0:T(8,128)(2,1)S(1)} %copy-done, bf16[384,3072]{1,0:T(8,128)(2,1)S(1)} %copy-done.1, ...), custom_call_target="tpu_custom_call" | custom-call | tf_op jit(solution)/shard_map/attention_backward/pallas_call | solution.py:111
  129.1 1.5 collective-permute-start.39
  132.7 1.2 add.14.total
  134.0 1.6 collective-permute-start.40
  135.5 3.4 %collective-permute-done.36.arrived = bf16[384,768]{1,0:T(8,128)(2,1)} collective-permute-done((bf16[384,768]{1,0:T(8,128)(2,1)}, bf16[384,768]{1,0:T(8,128)(2,1)}, u32[]{:S(2)}, u32[]{:S(2)}) %collective-permute-start.36) | collective-permute-done | bytes 589856 | tf_op jit(solution)/shard_map/ppermute | solution.py:355
  138.9 2.5 %line_end.5.rest_0_ = f32[384,3072]{1,0:T(8,128)} custom-call(s32[1]{0:T(128)} %bitcast.place, bf16[384,768]{1,0:T(8,128)(2,1)} %add.12.total, bf16[384,768]{1,0:T(8,128)(2,1)} %collective-permute-done.36.arrived, f32[384,3072]{1,0:T(8,128)} %line_end.4.rest_0_), custom_call_target="tpu_custom_call", output_to_operand_aliasing={{}: (3, {})} | custom-call | tf_op jit(solution)/shard_map/line_end/pallas_call | solution.py:317
  141.4 1.4 collective-permute-start.41
  142.8 5.7 %attention_backward.5 = (bf16[384,3072]{1,0:T(8,128)(2,1)}, bf16[384,3072]{1,0:T(8,128)(2,1)}, bf16[384,3072]{1,0:T(8,128)(2,1)}) custom-call(s32[2]{0:T(128)S(1)} %get-tuple-element.371.order, bf16[384,768]{1,0:T(8,128)(2,1)} %collective-permute-done.37.grad_rows, ...), custom_call_target="tpu_custom_call", output_to_operand_aliasing={{0}: (6, {}), {1}: (7, {}), {2}: (8, {})} | custom-call | tf_op jit(solution)/shard_map/attention_backward/pallas_call | solution.py:111
  148.5 1.4 add.15.total
  149.9 1.5 collective-permute-start.42
  151.4 5.4 %attention_backward.6 = (bf16[384,3072]{1,0:T(8,128)(2,1)}, bf16[384,3072]{1,0:T(8,128)(2,1)}, bf16[384,3072]{1,0:T(8,128)(2,1)}) custom-call(s32[2]{0:T(128)S(1)} %get-tuple-element.372.order, bf16[384,768]{1,0:T(8,128)(2,1)} %collective-permute-done.38.grad_rows, ...), custom_call_target="tpu_custom_call", output_to_operand_aliasing={{0}: (6, {}), {1}: (7, {}), {2}: (8, {})} | custom-call | tf_op jit(solution)/shard_map/attention_backward/pallas_call | solution.py:111
  156.8 1.1 line_end.6.rest_0_
  157.9 4.7 %attention_backward.7 = (bf16[384,3072]{1,0:T(8,128)(2,1)}, bf16[384,3072]{1,0:T(8,128)(2,1)}, bf16[384,3072]{1,0:T(8,128)(2,1)}) custom-call(s32[2]{0:T(128)S(1)} %get-tuple-element.373.order, bf16[384,768]{1,0:T(8,128)(2,1)S(1)} %collective-permute-done.41.grad_rows, ...), custom_call_target="tpu_custom_call", output_to_operand_aliasing={{0}: (6, {}), {1}: (7, {}), {2}: (8, {})} | custom-call | tf_op jit(solution)/shard_map/attention_backward/pallas_call | solution.py:111
  162.6 4.4 %collective-permute-done.42.arrived = bf16[384,768]{1,0:T(8,128)(2,1)S(1)} collective-permute-done((bf16[384,768]{1,0:T(8,128)(2,1)S(1)}, bf16[384,768]{1,0:T(8,128)(2,1)S(1)}, u32[]{:S(2)}, u32[]{:S(2)}) %collective-permute-start.42) | collective-permute-done | bytes 589856 | tf_op jit(solution)/shard_map/ppermute | solution.py:355
  (117 shorter events, 32.9 us)
Async XLA Ops:
  0.6 27.5 %collective-permute-start.3 = (bf16[384,3072]{1,0:T(8,128)(2,1)}, bf16[384,3072]{1,0:T(8,128)(2,1)}, u32[]{:S(2)}, u32[]{:S(2)}) collective-permute-start(bf16[384,3072]{1,0:T(8,128)(2,1)} %own.1), channel_id=1, source_target_pairs={{0,1},{1,0},{2,3},{3,2},{4,5},{5,4},{6,7},{7,6},{8,9},{9,8},{10,11... | collective-permute-start | bytes 7077896 | tf_op jit(solution)/shard_map/ppermute | solution.py:377
  4.2 2.1 %collective-permute-start = (bf16[96,3072]{1,0:T(8,128)(2,1)S(1)}, bf16[96,3072]{1,0:T(8,128)(2,1)S(1)}, u32[]{:S(2)}, u32[]{:S(2)}) collective-permute-start(bf16[96,3072]{1,0:T(8,128)(2,1)S(1)} %other_quarter.1), channel_id=1, source_target_pairs={{0,1},{1,0},{2,3},{3,2},{4,5},{5,4},{6,7},{7,6},{8,9},{9,8},{10,11... | collective-permute-start | bytes 1769480 | tf_op jit(solution)/shard_map/ppermute | solution.py:377
  7.0 19.7 %collective-permute-start.1 = (bf16[240,1536]{1,0:T(8,128)(2,1)S(1)}, bf16[240,1536]{1,0:T(8,128)(2,1)S(1)}, u32[]{:S(2)}, u32[]{:S(2)}) collective-permute-start(bf16[240,1536]{1,0:T(8,128)(2,1)S(1)} %get-tuple-element.222.to_x), channel_id=1, source_target_pairs={{0,2},{1,3},{2,0},{3,1},{4,6},{5,7},{6,4},{7,5},{8,10},{9,11},{10,... | collective-permute-start | bytes 2211848 | tf_op jit(solution)/shard_map/ppermute | solution.py:377
  9.8 18.3 %collective-permute-start.2 = (bf16[240,1536]{1,0:T(8,128)(2,1)S(1)}, bf16[240,1536]{1,0:T(8,128)(2,1)S(1)}, u32[]{:S(2)}, u32[]{:S(2)}) collective-permute-start(bf16[240,1536]{1,0:T(8,128)(2,1)S(1)} %get-tuple-element.208.to_y), channel_id=1, source_target_pairs={{0,4},{1,5},{2,6},{3,7},{4,0},{5,1},{6,2},{7,3},{8,12},{9,13},{10,... | collective-permute-start | bytes 2211848 | tf_op jit(solution)/shard_map/ppermute | solution.py:377
  18.7 103.9 %copy-start.5 = (bf16[12,384,384]{2,1,0:T(8,128)(2,1)}, bf16[12,384,384]{2,1,0:T(8,128)(2,1)S(1)}, u32[]{:S(2)}) copy-start(bf16[12,384,384]{2,1,0:T(8,128)(2,1)S(1)} %get-tuple-element.338.weights) | copy-start | bytes 10616836
  18.7 11.7 %collective-permute-start.4 = (bf16[96,1536]{1,0:T(8,128)(2,1)S(1)}, bf16[96,1536]{1,0:T(8,128)(2,1)S(1)}, u32[]{:S(2)}, u32[]{:S(2)}) collective-permute-start(bf16[96,1536]{1,0:T(8,128)(2,1)S(1)} %get-tuple-element.198), channel_id=1, source_target_pairs={{0,1},{1,0},{2,3},{3,2},{4,5},{5,4},{6,7},{7,6},{8,9},{9,8},{10,11... | collective-permute-start | bytes 884744 | tf_op jit(solution)/shard_map/ppermute | solution.py:377
  24.4 8.8 %copy-start.7 = (bf16[12,384,384]{2,1,0:T(8,128)(2,1)}, bf16[12,384,384]{2,1,0:T(8,128)(2,1)S(1)}, u32[]{:S(2)}) copy-start(bf16[12,384,384]{2,1,0:T(8,128)(2,1)S(1)} %get-tuple-element.361.weights) | copy-start | bytes 10616836
  24.4 8.2 %collective-permute-start.5 = (bf16[96,1536]{1,0:T(8,128)(2,1)S(1)}, bf16[96,1536]{1,0:T(8,128)(2,1)S(1)}, u32[]{:S(2)}, u32[]{:S(2)}) collective-permute-start(bf16[96,1536]{1,0:T(8,128)(2,1)S(1)} %get-tuple-element.204), channel_id=1, source_target_pairs={{0,1},{1,0},{2,3},{3,2},{4,5},{5,4},{6,7},{7,6},{8,9},{9,8},{10,11... | collective-permute-start | bytes 884744 | tf_op jit(solution)/shard_map/ppermute | solution.py:377
  28.2 13.2 %collective-permute-start.6 = (bf16[144,1536]{1,0:T(8,128)(2,1)S(1)}, bf16[144,1536]{1,0:T(8,128)(2,1)S(1)}, u32[]{:S(2)}, u32[]{:S(2)}) collective-permute-start(bf16[144,1536]{1,0:T(8,128)(2,1)S(1)} %get-tuple-element.225.next_y), channel_id=1, source_target_pairs={{0,4},{1,5},{2,6},{3,7},{4,0},{5,1},{6,2},{7,3},{8,12},{9,13},{10,... | collective-permute-start | bytes 1327112 | tf_op jit(solution)/shard_map/ppermute | solution.py:377
  29.8 13.1 %collective-permute-start.7 = (bf16[144,1536]{1,0:T(8,128)(2,1)S(1)}, bf16[144,1536]{1,0:T(8,128)(2,1)S(1)}, u32[]{:S(2)}, u32[]{:S(2)}) collective-permute-start(bf16[144,1536]{1,0:T(8,128)(2,1)S(1)} %get-tuple-element.226.next_x), channel_id=1, source_target_pairs={{0,2},{1,3},{2,0},{3,1},{4,6},{5,7},{6,4},{7,5},{8,10},{9,11},{10,... | collective-permute-start | bytes 1327112 | tf_op jit(solution)/shard_map/ppermute | solution.py:377
  31.0 21.4 %collective-permute-start.8 = (bf16[288,768]{1,0:T(8,128)(2,1)S(1)}, bf16[288,768]{1,0:T(8,128)(2,1)S(1)}, u32[]{:S(2)}, u32[]{:S(2)}) collective-permute-start(bf16[288,768]{1,0:T(8,128)(2,1)S(1)} %get-tuple-element.217), channel_id=1, source_target_pairs={{0,2},{1,3},{2,0},{3,1},{4,6},{5,7},{6,4},{7,5},{8,10},{9,11},{10,... | collective-permute-start | bytes 1327112 | tf_op jit(solution)/shard_map/ppermute | solution.py:377
  33.2 19.2 %collective-permute-start.9 = (bf16[288,768]{1,0:T(8,128)(2,1)S(1)}, bf16[288,768]{1,0:T(8,128)(2,1)S(1)}, u32[]{:S(2)}, u32[]{:S(2)}) collective-permute-start(bf16[288,768]{1,0:T(8,128)(2,1)S(1)} %get-tuple-element.220), channel_id=1, source_target_pairs={{0,4},{1,5},{2,6},{3,7},{4,0},{5,1},{6,2},{7,3},{8,12},{9,13},{10,... | collective-permute-start | bytes 1327112 | tf_op jit(solution)/shard_map/ppermute | solution.py:377
  33.7 9.4 %copy-start.9 = (bf16[384,3072]{1,0:T(8,128)(2,1)S(1)}, bf16[384,3072]{1,0:T(8,128)(2,1)}, u32[]{:S(2)}) copy-start(bf16[384,3072]{1,0:T(8,128)(2,1)} %own.1) | copy-start | bytes 7077892
  33.7 25.8 %collective-permute-start.10 = (bf16[288,768]{1,0:T(8,128)(2,1)S(1)}, bf16[288,768]{1,0:T(8,128)(2,1)S(1)}, u32[]{:S(2)}, u32[]{:S(2)}) collective-permute-start(bf16[288,768]{1,0:T(8,128)(2,1)S(1)} %get-tuple-element.221), channel_id=1, source_target_pairs={{0,6},{1,7},{2,4},{3,5},{4,2},{5,3},{6,0},{7,1},{8,14},{9,15},{10,... | collective-permute-start | bytes 1327112 | tf_op jit(solution)/shard_map/ppermute | solution.py:377
  60.5 16.3 %collective-permute-start.17 = (bf16[240,1536]{1,0:T(8,128)(2,1)S(1)}, bf16[240,1536]{1,0:T(8,128)(2,1)S(1)}, u32[]{:S(2)}, u32[]{:S(2)}) collective-permute-start(bf16[240,1536]{1,0:T(8,128)(2,1)S(1)} %get-tuple-element.266.to_x), channel_id=1, source_target_pairs={{0,2},{1,3},{2,0},{3,1},{4,6},{5,7},{6,4},{7,5},{8,10},{9,11},{10,... | collective-permute-start | bytes 2211848 | tf_op jit(solution)/shard_map/ppermute | solution.py:377
  61.3 16.5 %collective-permute-start.18 = (bf16[240,1536]{1,0:T(8,128)(2,1)S(1)}, bf16[240,1536]{1,0:T(8,128)(2,1)S(1)}, u32[]{:S(2)}, u32[]{:S(2)}) collective-permute-start(bf16[240,1536]{1,0:T(8,128)(2,1)S(1)} %get-tuple-element.259.to_y), channel_id=1, source_target_pairs={{0,4},{1,5},{2,6},{3,7},{4,0},{5,1},{6,2},{7,3},{8,12},{9,13},{10,... | collective-permute-start | bytes 2211848 | tf_op jit(solution)/shard_map/ppermute | solution.py:377
  62.7 1.4 collective-permute-start.11
  62.7 1.7 %collective-permute-start.12 = (bf16[384,256]{1,0:T(8,128)(2,1)S(1)}, bf16[384,256]{1,0:T(8,128)(2,1)S(1)}, u32[]{:S(2)}, u32[]{:S(2)}) collective-permute-start(bf16[384,256]{1,0:T(8,128)(2,1)S(1)} %get-tuple-element.239), channel_id=1, source_target_pairs={{0,1},{1,0},{2,3},{3,2},{4,5},{5,4},{6,7},{7,6},{8,9},{9,8},{10,11... | collective-permute-start | bytes 589832 | tf_op jit(solution)/shard_map/ppermute | solution.py:377
  63.2 1.5 collective-permute-start.13
  65.6 18.8 %collective-permute-start.19 = (bf16[384,768]{1,0:T(8,128)(2,1)S(1)}, bf16[384,768]{1,0:T(8,128)(2,1)S(1)}, u32[]{:S(2)}, u32[]{:S(2)}) collective-permute-start(bf16[384,768]{1,0:T(8,128)(2,1)S(1)} %term_own.4.a), channel_id=1, source_target_pairs={{0,8},{24,16},{1,9},{25,17},{2,10},{26,18},{3,11},{27,19},{4,12},{... | collective-permute-start | bytes 1769480 | tf_op jit(solution)/shard_map/ppermute | solution.py:341
  69.9 1.5 collective-permute-start.14
  70.0 1.7 %collective-permute-start.15 = (bf16[384,256]{1,0:T(8,128)(2,1)S(1)}, bf16[384,256]{1,0:T(8,128)(2,1)S(1)}, u32[]{:S(2)}, u32[]{:S(2)}) collective-permute-start(bf16[384,256]{1,0:T(8,128)(2,1)S(1)} %get-tuple-element.249), channel_id=1, source_target_pairs={{0,1},{1,0},{2,3},{3,2},{4,5},{5,4},{6,7},{7,6},{8,9},{9,8},{10,11... | collective-permute-start | bytes 589832 | tf_op jit(solution)/shard_map/ppermute | solution.py:377
  71.4 1.4 collective-permute-start.16
  77.9 9.2 %collective-permute-start.20 = (bf16[144,1536]{1,0:T(8,128)(2,1)S(1)}, bf16[144,1536]{1,0:T(8,128)(2,1)S(1)}, u32[]{:S(2)}, u32[]{:S(2)}) collective-permute-start(bf16[144,1536]{1,0:T(8,128)(2,1)S(1)} %get-tuple-element.269.next_y), channel_id=1, source_target_pairs={{0,4},{1,5},{2,6},{3,7},{4,0},{5,1},{6,2},{7,3},{8,12},{9,13},{10,... | collective-permute-start | bytes 1327112 | tf_op jit(solution)/shard_map/ppermute | solution.py:377
  79.4 8.3 %collective-permute-start.21 = (bf16[144,1536]{1,0:T(8,128)(2,1)S(1)}, bf16[144,1536]{1,0:T(8,128)(2,1)S(1)}, u32[]{:S(2)}, u32[]{:S(2)}) collective-permute-start(bf16[144,1536]{1,0:T(8,128)(2,1)S(1)} %get-tuple-element.270.next_x), channel_id=1, source_target_pairs={{0,2},{1,3},{2,0},{3,1},{4,6},{5,7},{6,4},{7,5},{8,10},{9,11},{10,... | collective-permute-start | bytes 1327112 | tf_op jit(solution)/shard_map/ppermute | solution.py:377
  80.8 14.3 %collective-permute-start.25 = (bf16[384,768]{1,0:T(8,128)(2,1)S(1)}, bf16[384,768]{1,0:T(8,128)(2,1)S(1)}, u32[]{:S(2)}, u32[]{:S(2)}) collective-permute-start(bf16[384,768]{1,0:T(8,128)(2,1)S(1)} %term_own.5.a), channel_id=1, source_target_pairs={{0,8},{24,16},{1,9},{25,17},{2,10},{26,18},{3,11},{27,19},{4,12},{... | collective-permute-start | bytes 1769480 | tf_op jit(solution)/shard_map/ppermute | solution.py:341
  84.5 13.1 %collective-permute-start.26 = (bf16[384,768]{1,0:T(8,128)(2,1)S(1)}, bf16[384,768]{1,0:T(8,128)(2,1)S(1)}, u32[]{:S(2)}, u32[]{:S(2)}) collective-permute-start(bf16[384,768]{1,0:T(8,128)(2,1)S(1)} %add.8.a), channel_id=1, source_target_pairs={{8,16},{16,8},{9,17},{17,9},{10,18},{18,10},{11,19},{19,11},{12,20... | collective-permute-start | bytes 1769480 | tf_op jit(solution)/shard_map/ppermute | solution.py:348
  88.7 1.5 collective-permute-start.22
  88.8 1.7 %collective-permute-start.23 = (bf16[384,256]{1,0:T(8,128)(2,1)S(1)}, bf16[384,256]{1,0:T(8,128)(2,1)S(1)}, u32[]{:S(2)}, u32[]{:S(2)}) collective-permute-start(bf16[384,256]{1,0:T(8,128)(2,1)S(1)} %get-tuple-element.276), channel_id=1, source_target_pairs={{0,1},{1,0},{2,3},{3,2},{4,5},{5,4},{6,7},{7,6},{8,9},{9,8},{10,11... | collective-permute-start | bytes 589832 | tf_op jit(solution)/shard_map/ppermute | solution.py:377
  89.3 1.5 collective-permute-start.24
  91.6 24.3 %collective-permute-start.31 = (bf16[384,768]{1,0:T(8,128)(2,1)S(1)}, bf16[384,768]{1,0:T(8,128)(2,1)S(1)}, u32[]{:S(2)}, u32[]{:S(2)}) collective-permute-start(bf16[384,768]{1,0:T(8,128)(2,1)S(1)} %term_own.6.a), channel_id=1, source_target_pairs={{0,8},{24,16},{1,9},{25,17},{2,10},{26,18},{3,11},{27,19},{4,12},{... | collective-permute-start | bytes 1769480 | tf_op jit(solution)/shard_map/ppermute | solution.py:341
  95.3 23.0 %collective-permute-start.32 = (bf16[384,768]{1,0:T(8,128)(2,1)S(1)}, bf16[384,768]{1,0:T(8,128)(2,1)S(1)}, u32[]{:S(2)}, u32[]{:S(2)}) collective-permute-start(bf16[384,768]{1,0:T(8,128)(2,1)S(1)} %add.9.a), channel_id=1, source_target_pairs={{8,16},{16,8},{9,17},{17,9},{10,18},{18,10},{11,19},{19,11},{12,20... | collective-permute-start | bytes 1769480 | tf_op jit(solution)/shard_map/ppermute | solution.py:348
  97.0 1.5 collective-permute-start.27
  97.1 1.7 %collective-permute-start.28 = (bf16[384,256]{1,0:T(8,128)(2,1)S(1)}, bf16[384,256]{1,0:T(8,128)(2,1)S(1)}, u32[]{:S(2)}, u32[]{:S(2)}) collective-permute-start(bf16[384,256]{1,0:T(8,128)(2,1)S(1)} %get-tuple-element.288), channel_id=1, source_target_pairs={{0,1},{1,0},{2,3},{3,2},{4,5},{5,4},{6,7},{7,6},{8,9},{9,8},{10,11... | collective-permute-start | bytes 589832 | tf_op jit(solution)/shard_map/ppermute | solution.py:377
  97.6 1.5 collective-permute-start.29
  99.9 22.2 %collective-permute-start.33 = (bf16[384,768]{1,0:T(8,128)(2,1)S(1)}, bf16[384,768]{1,0:T(8,128)(2,1)S(1)}, u32[]{:S(2)}, u32[]{:S(2)}) collective-permute-start(bf16[384,768]{1,0:T(8,128)(2,1)S(1)} %term_own.7.a), channel_id=1, source_target_pairs={{0,8},{24,16},{1,9},{25,17},{2,10},{26,18},{3,11},{27,19},{4,12},{... | collective-permute-start | bytes 1769480 | tf_op jit(solution)/shard_map/ppermute | solution.py:341
  107.2 21.1 %collective-permute-start.34 = (bf16[384,768]{1,0:T(8,128)(2,1)S(1)}, bf16[384,768]{1,0:T(8,128)(2,1)S(1)}, u32[]{:S(2)}, u32[]{:S(2)}) collective-permute-start(bf16[384,768]{1,0:T(8,128)(2,1)S(1)} %add.10.total), channel_id=1, source_target_pairs={{8,0},{16,24},{9,1},{17,25},{10,2},{18,26},{11,3},{19,27},{12,4},{... | collective-permute-start | bytes 1769480 | tf_op jit(solution)/shard_map/ppermute | solution.py:355
  112.7 1.4 collective-permute-start.30
  116.7 16.0 %collective-permute-start.35 = (bf16[384,768]{1,0:T(8,128)(2,1)S(1)}, bf16[384,768]{1,0:T(8,128)(2,1)}, u32[]{:S(2)}, u32[]{:S(2)}) collective-permute-start(bf16[384,768]{1,0:T(8,128)(2,1)S(1)} %add.11.a), channel_id=1, source_target_pairs={{8,16},{16,8},{9,17},{17,9},{10,18},{18,10},{11,19},{19,11},{12,20... | collective-permute-start | bytes 1769480 | tf_op jit(solution)/shard_map/ppermute | solution.py:348
  119.3 19.6 %collective-permute-start.36 = (bf16[384,768]{1,0:T(8,128)(2,1)}, bf16[384,768]{1,0:T(8,128)(2,1)}, u32[]{:S(2)}, u32[]{:S(2)}) collective-permute-start(bf16[384,768]{1,0:T(8,128)(2,1)} %add.12.total), channel_id=1, source_target_pairs={{8,0},{16,24},{9,1},{17,25},{10,2},{18,26},{11,3},{19,27},{12,4},{... | collective-permute-start | bytes 1769480 | tf_op jit(solution)/shard_map/ppermute | solution.py:355
  120.6 20.8 %collective-permute-start.37 = (bf16[384,768]{1,0:T(8,128)(2,1)}, bf16[384,768]{1,0:T(8,128)(2,1)}, u32[]{:S(2)}, u32[]{:S(2)}) collective-permute-start(bf16[384,768]{1,0:T(8,128)(2,1)} %get-tuple-element.307), channel_id=1, source_target_pairs={{0,2},{1,3},{2,0},{3,1},{4,6},{5,7},{6,4},{7,5},{8,10},{9,11},{10,... | collective-permute-start | bytes 1769480 | tf_op jit(solution)/shard_map/ppermute | solution.py:377
  122.1 19.3 %collective-permute-start.38 = (bf16[384,768]{1,0:T(8,128)(2,1)}, bf16[384,768]{1,0:T(8,128)(2,1)}, u32[]{:S(2)}, u32[]{:S(2)}) collective-permute-start(bf16[384,768]{1,0:T(8,128)(2,1)} %get-tuple-element.308), channel_id=1, source_target_pairs={{0,4},{1,5},{2,6},{3,7},{4,0},{5,1},{6,2},{7,3},{8,12},{9,13},{10,... | collective-permute-start | bytes 1769480 | tf_op jit(solution)/shard_map/ppermute | solution.py:377
  129.1 19.4 %collective-permute-start.39 = (bf16[384,768]{1,0:T(8,128)(2,1)}, bf16[384,768]{1,0:T(8,128)(2,1)}, u32[]{:S(2)}, u32[]{:S(2)}) collective-permute-start(bf16[384,768]{1,0:T(8,128)(2,1)} %add.13.a), channel_id=1, source_target_pairs={{8,16},{16,8},{9,17},{17,9},{10,18},{18,10},{11,19},{19,11},{12,20... | collective-permute-start | bytes 1769480 | tf_op jit(solution)/shard_map/ppermute | solution.py:348
  133.9 8.9 %copy-start.2 = (bf16[384,3072]{1,0:T(8,128)(2,1)S(1)}, bf16[384,3072]{1,0:T(8,128)(2,1)}, u32[]{:S(2)}) copy-start(bf16[384,3072]{1,0:T(8,128)(2,1)} %key.5) | copy-start | bytes 7077892
  133.9 8.9 %copy-start.4 = (bf16[384,3072]{1,0:T(8,128)(2,1)S(1)}, bf16[384,3072]{1,0:T(8,128)(2,1)}, u32[]{:S(2)}) copy-start(bf16[384,3072]{1,0:T(8,128)(2,1)} %value.5) | copy-start | bytes 7077892
  134.0 22.8 %collective-permute-start.40 = (bf16[384,768]{1,0:T(8,128)(2,1)S(1)}, bf16[384,768]{1,0:T(8,128)(2,1)S(1)}, u32[]{:S(2)}, u32[]{:S(2)}) collective-permute-start(bf16[384,768]{1,0:T(8,128)(2,1)S(1)} %add.14.total), channel_id=1, source_target_pairs={{8,0},{16,24},{9,1},{17,25},{10,2},{18,26},{11,3},{19,27},{12,4},{... | collective-permute-start | bytes 1769480 | tf_op jit(solution)/shard_map/ppermute | solution.py:355
  141.4 16.5 %collective-permute-start.41 = (bf16[384,768]{1,0:T(8,128)(2,1)S(1)}, bf16[384,768]{1,0:T(8,128)(2,1)S(1)}, u32[]{:S(2)}, u32[]{:S(2)}) collective-permute-start(bf16[384,768]{1,0:T(8,128)(2,1)S(1)} %copy-done.16), channel_id=1, source_target_pairs={{0,6},{1,7},{2,4},{3,5},{4,2},{5,3},{6,0},{7,1},{8,14},{9,15},{10,... | collective-permute-start | bytes 1769480 | tf_op jit(solution)/shard_map/ppermute | solution.py:377
  149.9 17.1 %collective-permute-start.42 = (bf16[384,768]{1,0:T(8,128)(2,1)S(1)}, bf16[384,768]{1,0:T(8,128)(2,1)S(1)}, u32[]{:S(2)}, u32[]{:S(2)}) collective-permute-start(bf16[384,768]{1,0:T(8,128)(2,1)S(1)} %add.15.total), channel_id=1, source_target_pairs={{8,0},{16,24},{9,1},{17,25},{10,2},{18,26},{11,3},{19,27},{12,4},{... | collective-permute-start | bytes 1769480 | tf_op jit(solution)/shard_map/ppermute | solution.py:355
  (12 other events, 48.4 us)

commit v4 on v3

--- a/solution.py
+++ b/solution.py
@@ -89,17 +89,18 @@
 def backward_kernel(order, grad_rows, query, key, value, weights, *rest):
     grad_query, grad_key, grad_value = rest[-3:]
     inverse_root = 1.0 / math.sqrt(E)
-    for head in range(BLOCK_HEADS):
-        columns = slice(head * E, (head + 1) * E)
-        grad = grad_rows[:, columns]
-        half = weights[head]
-        grad_probs = dot(value[:, columns], grad, 1, 1)
-        wide = half.astype(F32)
-        row_dot = jnp.sum(wide * grad_probs, axis=0, keepdims=True)
-        grad_logits = (wide * (grad_probs - row_dot)).astype(BF16)
-        grad_value[:, columns] = dot(half, grad, 1, 0).astype(BF16)
-        grad_key[:, columns] = (dot(grad_logits, query[:, columns], 1, 0) * inverse_root).astype(BF16)
-        grad_query[:, columns] = (dot(grad_logits, key[:, columns], 0, 0) * inverse_root).astype(BF16)
+    columns = [slice(head * E, (head + 1) * E) for head in range(BLOCK_HEADS)]
+    grad_probs = [dot(value[:, c], grad_rows[:, c], 1, 1) for c in columns]
+    grad_logits = []
+    for head, c in enumerate(columns):
+        grad_value[:, c] = dot(weights[head], grad_rows[:, c], 1, 0).astype(BF16)
+        wide = weights[head].astype(F32)
+        row_dot = jnp.sum(wide * grad_probs[head], axis=0, keepdims=True)
+        grad_logits.append((wide * (grad_probs[head] - row_dot)).astype(BF16))
+    for head, c in enumerate(columns):
+        grad_key[:, c] = (dot(grad_logits[head], query[:, c], 1, 0) * inverse_root).astype(BF16)
+    for head, c in enumerate(columns):
+        grad_query[:, c] = (dot(grad_logits[head], key[:, c], 0, 0) * inverse_root).astype(BF16)
 
 
 def backward(order, grad, query_rows, key_rows, value_rows, weights, skip, done):
@@ -473,13 +474,13 @@
     arriving = term_other(3, plane, gathered)
     line.back(0)
     term_own(3, plane, gathered, arriving)
+    line.across(2)
     grad_main, grad_extra = grad_step(1, plane, grad)
     held = order(grad_main, grad_extra, swap(grad_extra, 1))
     shape = (rows, PAIR)
     grad_rows = whole(grad_pack_kernel, [shape] * 4, *held, scalars=(blocks,), name="grad_pack")
     order.mark(*grad_rows)
     moved_x, moved_y = swap(grad_rows[1], 2), swap(grad_rows[2], 4)
-    line.across(2)
     line.back(1)
 
     grads = ()

time: 169 us -> 168 us (level)
  Pallas kernels: 62.4 us -> 60.6 us
    pallas_call x4, Pallas kernels: 20.5 us -> 18.7 us  [backward(): pl.pallas_call(backward_kernel, grid_spec=pltpu.PrefetchScalarGridSpec(nu...]
  transfers between devices with their start and end apart: 43 -> 43, of which waited for: 26 -> 25; matrix products, arithmetic and copies ran while one was open for 0% -> 0% of each run, Pallas kernels for 36% -> 35%
where the time goes in v4:
time: 168 us
  Pallas kernels  60.6 us (36%)
  starting transfers between devices  50.7 us (30%)
  waiting for transfers between devices  48.2 us (29%)
  local copies, waits for them, and re-layouts  7.11 us (4%)
    ppermute x31, waiting for transfers between devices, swap(): return lax.ppermute(a, 'fsdp', [(f, f ^ mask) for f in range(8)])  39.1 us
    ppermute x31, starting transfers between devices, swap(): return lax.ppermute(a, 'fsdp', [(f, f ^ mask) for f in range(8)])  21.8 us
    ppermute x4, starting transfers between devices, start(): self.arriving[piece] = lax.ppermute(part, 'rep', [(0, 1), (3, 2)])  18.7 us
    pallas_call x4, Pallas kernels, backward(): pl.pallas_call(backward_kernel, grid_spec=pltpu.PrefetchScalarGridSpec(nu...  18.7 us
    pallas_call x25, Pallas kernels, whole(): pl.pallas_call(kernel, in_specs=[smem] * len(scalars) + [vmem] * len(arra...  16 us
    pallas_call x2, Pallas kernels, forward(): pl.pallas_call(forward_kernel, grid_spec=pltpu.PrefetchScalarGridSpec(num...  10.9 us
    ppermute x4, waiting for transfers between devices, back(): self.arriving[piece] = lax.ppermute(total, 'rep', [(1, 0), (2, 3)])  9.09 us
    pallas_call x2, Pallas kernels, grad_part(): pl.pallas_call(grad_end_kernel if last else grad_kernel, grid=(1,), in_sp...  8.53 us
  transfers between devices with their start and end apart: 43, of which 25 were waited for; matrix products, arithmetic and copies ran while one was open for 0% of the time, Pallas kernels for 35%

profile of v4, /device:TPU:0, one launch (start us, length us, event | category | flops | bytes accessed | tf_op | source)
XLA Modules:
  0.0 167.8 jit_solution(14034141937313150165)
XLA Ops:
  1.2 1.7 copy-done.10
  4.3 1.9 %collective-permute-done.arrived = bf16[96,3072]{1,0:T(8,128)(2,1)S(1)} collective-permute-done((bf16[96,3072]{1,0:T(8,128)(2,1)S(1)}, bf16[96,3072]{1,0:T(8,128)(2,1)S(1)}, u32[]{:S(2)}, u32[]{:S(2)}) %collective-permute-start) | collective-permute-done | bytes 589856 | tf_op jit(solution)/shard_map/ppermute | solution.py:378
  7.0 2.9 %collective-permute-start.1 = (bf16[240,1536]{1,0:T(8,128)(2,1)S(1)}, bf16[240,1536]{1,0:T(8,128)(2,1)S(1)}, u32[]{:S(2)}, u32[]{:S(2)}) collective-permute-start(bf16[240,1536]{1,0:T(8,128)(2,1)S(1)} %get-tuple-element.222.to_x), channel_id=1, source_target_pairs={{0,2},{1,3},{2,0},{3,1},{4,6},{5,7},{6,4},{7,5},{8,10},{9,11},{10,... | collective-permute-start | bytes 2211848 | tf_op jit(solution)/shard_map/ppermute | solution.py:378
  9.8 1.5 collective-permute-start.2
  11.6 1.7 copy-done.3
  13.2 5.4 %attention_forward.2 = (bf16[384,1536]{1,0:T(8,128)(2,1)S(1)}, bf16[96,1536]{1,0:T(8,128)(2,1)S(1)}, bf16[12,384,384]{2,1,0:T(8,128)(2,1)S(1)}) custom-call(s32[4]{0:T(128)S(1)} %get-tuple-element.368.order, s32[384,1]{1,0:T(8,128)S(1)} %reshape.28.ids_column, s32[1,384]{1,0:T(1,128)S(1)} %reshape.25.ids_row, bf16[384,3072]{1,0:T(8,128)(2,1)S(1)} %copy-done, ...), custom_call_target="tpu_custom_call" | custom-call | tf_op jit(solution)/shard_map/attention_forward/pallas_call | solution.py:59
  18.9 5.4 %attention_forward.3 = (bf16[384,1536]{1,0:T(8,128)(2,1)S(1)}, bf16[96,1536]{1,0:T(8,128)(2,1)S(1)}, bf16[12,384,384]{2,1,0:T(8,128)(2,1)S(1)}) custom-call(s32[4]{0:T(128)S(1)} %get-tuple-element.369.order, s32[384,1]{1,0:T(8,128)S(1)} %reshape.29.ids_column, s32[1,384]{1,0:T(1,128)S(1)} %reshape.27.ids_row, bf16[384,3072]{1,0:T(8,128)(2,1)S(1)} %copy-done, ...), custom_call_target="tpu_custom_call" | custom-call | tf_op jit(solution)/shard_map/attention_forward/pallas_call | solution.py:59
  24.9 1.8 %collective-permute-done.1.from_x = bf16[240,1536]{1,0:T(8,128)(2,1)S(1)} collective-permute-done((bf16[240,1536]{1,0:T(8,128)(2,1)S(1)}, bf16[240,1536]{1,0:T(8,128)(2,1)S(1)}, u32[]{:S(2)}, u32[]{:S(2)}) %collective-permute-start.1) | collective-permute-done | bytes 737312 | tf_op jit(solution)/shard_map/ppermute | solution.py:378
  26.7 1.5 collective-permute-done.2.from_y
  28.2 1.6 collective-permute-start.6
  31.0 1.6 collective-permute-start.8
  33.7 1.5 collective-permute-start.10
  35.2 6.2 %collective-permute-done.6.via_y = bf16[144,1536]{1,0:T(8,128)(2,1)S(1)} collective-permute-done((bf16[144,1536]{1,0:T(8,128)(2,1)S(1)}, bf16[144,1536]{1,0:T(8,128)(2,1)S(1)}, u32[]{:S(2)}, u32[]{:S(2)}) %collective-permute-start.6) | collective-permute-done | bytes 442400 | tf_op jit(solution)/shard_map/ppermute | solution.py:378
  41.4 1.5 collective-permute-done.7.via_x
  43.1 4.2 %grad_attended.2.before = f32[864,768]{1,0:T(8,128)S(1)} custom-call(bf16[864,1536]{1,0:T(8,128)(2,1)S(1)} %gather_end.2.plane, bf16[384,3072]{1,0:T(8,128)(2,1)S(1)} %copy-done.9, bf16[384,3072]{1,0:T(8,128)(2,1)} %collective-permute-done.3.other), custom_call_target="tpu_custom_call" | custom-call | tf_op jit(solution)/shard_map/grad_attended/pallas_call | solution.py:276
  47.4 5.0 %collective-permute-done.8.from_x = bf16[288,768]{1,0:T(8,128)(2,1)S(1)} collective-permute-done((bf16[288,768]{1,0:T(8,128)(2,1)S(1)}, bf16[288,768]{1,0:T(8,128)(2,1)S(1)}, u32[]{:S(2)}, u32[]{:S(2)}) %collective-permute-start.8) | collective-permute-done | bytes 442400 | tf_op jit(solution)/shard_map/ppermute | solution.py:378
  52.4 7.2 %collective-permute-done.10.from_far = bf16[288,768]{1,0:T(8,128)(2,1)S(1)} collective-permute-done((bf16[288,768]{1,0:T(8,128)(2,1)S(1)}, bf16[288,768]{1,0:T(8,128)(2,1)S(1)}, u32[]{:S(2)}, u32[]{:S(2)}) %collective-permute-start.10) | collective-permute-done | bytes 442400 | tf_op jit(solution)/shard_map/ppermute | solution.py:378
  61.3 1.4 collective-permute-start.18
  66.7 3.5 %collective-permute-start.19 = (bf16[384,768]{1,0:T(8,128)(2,1)S(1)}, bf16[384,768]{1,0:T(8,128)(2,1)S(1)}, u32[]{:S(2)}, u32[]{:S(2)}) collective-permute-start(bf16[384,768]{1,0:T(8,128)(2,1)S(1)} %term_own.4.a), channel_id=1, source_target_pairs={{0,8},{24,16},{1,9},{25,17},{2,10},{26,18},{3,11},{27,19},{4,12},{... | collective-permute-start | bytes 1769480 | tf_op jit(solution)/shard_map/ppermute | solution.py:342
  72.8 4.0 %collective-permute-done.17.from_x = bf16[240,1536]{1,0:T(8,128)(2,1)S(1)} collective-permute-done((bf16[240,1536]{1,0:T(8,128)(2,1)S(1)}, bf16[240,1536]{1,0:T(8,128)(2,1)S(1)}, u32[]{:S(2)}, u32[]{:S(2)}) %collective-permute-start.17) | collective-permute-done | bytes 737312 | tf_op jit(solution)/shard_map/ppermute | solution.py:378
  77.9 1.5 collective-permute-start.20
  79.4 1.4 collective-permute-start.21
  80.8 3.5 %collective-permute-start.25 = (bf16[384,768]{1,0:T(8,128)(2,1)S(1)}, bf16[384,768]{1,0:T(8,128)(2,1)S(1)}, u32[]{:S(2)}, u32[]{:S(2)}) collective-permute-start(bf16[384,768]{1,0:T(8,128)(2,1)S(1)} %term_own.5.a), channel_id=1, source_target_pairs={{0,8},{24,16},{1,9},{25,17},{2,10},{26,18},{3,11},{27,19},{4,12},{... | collective-permute-start | bytes 1769480 | tf_op jit(solution)/shard_map/ppermute | solution.py:342
  85.2 1.9 %collective-permute-done.20.via_y = bf16[144,1536]{1,0:T(8,128)(2,1)S(1)} collective-permute-done((bf16[144,1536]{1,0:T(8,128)(2,1)S(1)}, bf16[144,1536]{1,0:T(8,128)(2,1)S(1)}, u32[]{:S(2)}, u32[]{:S(2)}) %collective-permute-start.20) | collective-permute-done | bytes 442400 | tf_op jit(solution)/shard_map/ppermute | solution.py:378
  91.6 4.2 %collective-permute-start.30 = (bf16[384,768]{1,0:T(8,128)(2,1)S(1)}, bf16[384,768]{1,0:T(8,128)(2,1)S(1)}, u32[]{:S(2)}, u32[]{:S(2)}) collective-permute-start(bf16[384,768]{1,0:T(8,128)(2,1)S(1)} %term_own.6.a), channel_id=1, source_target_pairs={{0,8},{24,16},{1,9},{25,17},{2,10},{26,18},{3,11},{27,19},{4,12},{... | collective-permute-start | bytes 1769480 | tf_op jit(solution)/shard_map/ppermute | solution.py:342
  100.6 7.5 %collective-permute-start.33 = (bf16[384,768]{1,0:T(8,128)(2,1)S(1)}, bf16[384,768]{1,0:T(8,128)(2,1)S(1)}, u32[]{:S(2)}, u32[]{:S(2)}) collective-permute-start(bf16[384,768]{1,0:T(8,128)(2,1)S(1)} %term_own.7.a), channel_id=1, source_target_pairs={{0,8},{24,16},{1,9},{25,17},{2,10},{26,18},{3,11},{27,19},{4,12},{... | collective-permute-start | bytes 1769480 | tf_op jit(solution)/shard_map/ppermute | solution.py:342
  108.1 1.3 collective-permute-start.34
  109.6 4.3 %grad_attended.3 = (bf16[768,768]{1,0:T(8,128)(2,1)S(1)}, bf16[96,768]{1,0:T(8,128)(2,1)S(1)}) custom-call(bf16[864,1536]{1,0:T(8,128)(2,1)S(1)} %gather_end.3.plane, bf16[384,3072]{1,0:T(8,128)(2,1)S(1)} %copy-done.9, bf16[384,3072]{1,0:T(8,128)(2,1)} %collective-permute-done.3.other, f32[864,768]{1,0:T(8,128)S(1)} %grad_attended.2.before), custom_call_target="tpu_custom_call" | custom-call | tf_op jit(solution)/shard_map/grad_attended/pallas_call | solution.py:276
  113.9 1.5 collective-permute-start.35
  115.5 1.7 %grad_pack.1 = (bf16[384,768]{1,0:T(8,128)(2,1)S(1)}, bf16[384,768]{1,0:T(8,128)(2,1)}, bf16[384,768]{1,0:T(8,128)(2,1)}, bf16[384,768]{1,0:T(8,128)(2,1)S(1)}) custom-call(s32[8]{0:T(128)S(1)} %iota_xor_fusion.blocks, bf16[768,768]{1,0:T(8,128)(2,1)S(1)} %get-tuple-element.305.main, bf16[96,768]{1,0:T(8,128)(2,1)S(1)} %get-tuple-element.306.extra, ...), custom_call_target="tpu_custom_call" | custom-call | tf_op jit(solution)/shard_map/grad_pack/pallas_call | solution.py:137
  119.0 1.3 collective-permute-start.36
  120.4 1.4 collective-permute-start.37
  122.3 4.3 %attention_backward.4 = (bf16[384,3072]{1,0:T(8,128)(2,1)}, bf16[384,3072]{1,0:T(8,128)(2,1)}, bf16[384,3072]{1,0:T(8,128)(2,1)}) custom-call(s32[2]{0:T(128)S(1)} %get-tuple-element.370.order, bf16[384,768]{1,0:T(8,128)(2,1)S(1)} %get-tuple-element.315.grad_rows, bf16[384,3072]{1,0:T(8,128)(2,1)S(1)} %copy-done, bf16[384,3072]{1,0:T(8,128)(2,1)S(1)} %copy-done.1, ...), custom_call_target="tpu_custom_call" | custom-call | tf_op jit(solution)/shard_map/attention_backward/pallas_call | solution.py:112
  128.4 1.5 collective-permute-start.39
  131.0 1.1 line_end.4.rest_0_
  132.1 1.2 add.14.total
  133.3 1.6 collective-permute-start.40
  134.9 4.1 %collective-permute-done.36.arrived = bf16[384,768]{1,0:T(8,128)(2,1)} collective-permute-done((bf16[384,768]{1,0:T(8,128)(2,1)}, bf16[384,768]{1,0:T(8,128)(2,1)}, u32[]{:S(2)}, u32[]{:S(2)}) %collective-permute-start.36) | collective-permute-done | bytes 589856 | tf_op jit(solution)/shard_map/ppermute | solution.py:356
  139.0 2.5 %line_end.5.rest_0_ = f32[384,3072]{1,0:T(8,128)} custom-call(s32[1]{0:T(128)} %bitcast.place, bf16[384,768]{1,0:T(8,128)(2,1)} %add.12.total, bf16[384,768]{1,0:T(8,128)(2,1)} %collective-permute-done.36.arrived, f32[384,3072]{1,0:T(8,128)} %line_end.4.rest_0_), custom_call_target="tpu_custom_call", output_to_operand_aliasing={{}: (3, {})} | custom-call | tf_op jit(solution)/shard_map/line_end/pallas_call | solution.py:318
  142.1 5.1 %attention_backward.5 = (bf16[384,3072]{1,0:T(8,128)(2,1)}, bf16[384,3072]{1,0:T(8,128)(2,1)}, bf16[384,3072]{1,0:T(8,128)(2,1)}) custom-call(s32[2]{0:T(128)S(1)} %get-tuple-element.371.order, bf16[384,768]{1,0:T(8,128)(2,1)} %collective-permute-done.37.grad_rows, ...), custom_call_target="tpu_custom_call", output_to_operand_aliasing={{0}: (6, {}), {1}: (7, {}), {2}: (8, {})} | custom-call | tf_op jit(solution)/shard_map/attention_backward/pallas_call | solution.py:112
  147.3 1.4 add.15.total
  148.6 1.5 collective-permute-start.42
  150.2 5.0 %attention_backward.6 = (bf16[384,3072]{1,0:T(8,128)(2,1)}, bf16[384,3072]{1,0:T(8,128)(2,1)}, bf16[384,3072]{1,0:T(8,128)(2,1)}) custom-call(s32[2]{0:T(128)S(1)} %get-tuple-element.372.order, bf16[384,768]{1,0:T(8,128)(2,1)} %collective-permute-done.38.grad_rows, ...), custom_call_target="tpu_custom_call", output_to_operand_aliasing={{0}: (6, {}), {1}: (7, {}), {2}: (8, {})} | custom-call | tf_op jit(solution)/shard_map/attention_backward/pallas_call | solution.py:112
  155.1 1.1 line_end.6.rest_0_
  156.3 1.1 collective-permute-done.41.grad_rows
  157.4 4.3 %attention_backward.7 = (bf16[384,3072]{1,0:T(8,128)(2,1)}, bf16[384,3072]{1,0:T(8,128)(2,1)}, bf16[384,3072]{1,0:T(8,128)(2,1)}) custom-call(s32[2]{0:T(128)S(1)} %get-tuple-element.373.order, bf16[384,768]{1,0:T(8,128)(2,1)S(1)} %collective-permute-done.41.grad_rows, ...), custom_call_target="tpu_custom_call", output_to_operand_aliasing={{0}: (6, {}), {1}: (7, {}), {2}: (8, {})} | custom-call | tf_op jit(solution)/shard_map/attention_backward/pallas_call | solution.py:112
  161.7 5.0 %collective-permute-done.42.arrived = bf16[384,768]{1,0:T(8,128)(2,1)S(1)} collective-permute-done((bf16[384,768]{1,0:T(8,128)(2,1)S(1)}, bf16[384,768]{1,0:T(8,128)(2,1)S(1)}, u32[]{:S(2)}, u32[]{:S(2)}) %collective-permute-start.42) | collective-permute-done | bytes 589856 | tf_op jit(solution)/shard_map/ppermute | solution.py:356
  166.7 1.1 line_end.7
  (117 shorter events, 31.7 us)
Async XLA Ops:
  0.6 27.5 %collective-permute-start.3 = (bf16[384,3072]{1,0:T(8,128)(2,1)}, bf16[384,3072]{1,0:T(8,128)(2,1)}, u32[]{:S(2)}, u32[]{:S(2)}) collective-permute-start(bf16[384,3072]{1,0:T(8,128)(2,1)} %own.1), channel_id=1, source_target_pairs={{0,1},{1,0},{2,3},{3,2},{4,5},{5,4},{6,7},{7,6},{8,9},{9,8},{10,11... | collective-permute-start | bytes 7077896 | tf_op jit(solution)/shard_map/ppermute | solution.py:378
  4.2 2.1 %collective-permute-start = (bf16[96,3072]{1,0:T(8,128)(2,1)S(1)}, bf16[96,3072]{1,0:T(8,128)(2,1)S(1)}, u32[]{:S(2)}, u32[]{:S(2)}) collective-permute-start(bf16[96,3072]{1,0:T(8,128)(2,1)S(1)} %other_quarter.1), channel_id=1, source_target_pairs={{0,1},{1,0},{2,3},{3,2},{4,5},{5,4},{6,7},{7,6},{8,9},{9,8},{10,11... | collective-permute-start | bytes 1769480 | tf_op jit(solution)/shard_map/ppermute | solution.py:378
  7.0 19.7 %collective-permute-start.1 = (bf16[240,1536]{1,0:T(8,128)(2,1)S(1)}, bf16[240,1536]{1,0:T(8,128)(2,1)S(1)}, u32[]{:S(2)}, u32[]{:S(2)}) collective-permute-start(bf16[240,1536]{1,0:T(8,128)(2,1)S(1)} %get-tuple-element.222.to_x), channel_id=1, source_target_pairs={{0,2},{1,3},{2,0},{3,1},{4,6},{5,7},{6,4},{7,5},{8,10},{9,11},{10,... | collective-permute-start | bytes 2211848 | tf_op jit(solution)/shard_map/ppermute | solution.py:378
  9.8 18.3 %collective-permute-start.2 = (bf16[240,1536]{1,0:T(8,128)(2,1)S(1)}, bf16[240,1536]{1,0:T(8,128)(2,1)S(1)}, u32[]{:S(2)}, u32[]{:S(2)}) collective-permute-start(bf16[240,1536]{1,0:T(8,128)(2,1)S(1)} %get-tuple-element.208.to_y), channel_id=1, source_target_pairs={{0,4},{1,5},{2,6},{3,7},{4,0},{5,1},{6,2},{7,3},{8,12},{9,13},{10,... | collective-permute-start | bytes 2211848 | tf_op jit(solution)/shard_map/ppermute | solution.py:378
  18.7 103.7 %copy-start.5 = (bf16[12,384,384]{2,1,0:T(8,128)(2,1)}, bf16[12,384,384]{2,1,0:T(8,128)(2,1)S(1)}, u32[]{:S(2)}) copy-start(bf16[12,384,384]{2,1,0:T(8,128)(2,1)S(1)} %get-tuple-element.338.weights) | copy-start | bytes 10616836
  18.7 11.7 %collective-permute-start.4 = (bf16[96,1536]{1,0:T(8,128)(2,1)S(1)}, bf16[96,1536]{1,0:T(8,128)(2,1)S(1)}, u32[]{:S(2)}, u32[]{:S(2)}) collective-permute-start(bf16[96,1536]{1,0:T(8,128)(2,1)S(1)} %get-tuple-element.198), channel_id=1, source_target_pairs={{0,1},{1,0},{2,3},{3,2},{4,5},{5,4},{6,7},{7,6},{8,9},{9,8},{10,11... | collective-permute-start | bytes 884744 | tf_op jit(solution)/shard_map/ppermute | solution.py:378
  24.4 8.8 %copy-start.7 = (bf16[12,384,384]{2,1,0:T(8,128)(2,1)}, bf16[12,384,384]{2,1,0:T(8,128)(2,1)S(1)}, u32[]{:S(2)}) copy-start(bf16[12,384,384]{2,1,0:T(8,128)(2,1)S(1)} %get-tuple-element.361.weights) | copy-start | bytes 10616836
  24.4 8.2 %collective-permute-start.5 = (bf16[96,1536]{1,0:T(8,128)(2,1)S(1)}, bf16[96,1536]{1,0:T(8,128)(2,1)S(1)}, u32[]{:S(2)}, u32[]{:S(2)}) collective-permute-start(bf16[96,1536]{1,0:T(8,128)(2,1)S(1)} %get-tuple-element.204), channel_id=1, source_target_pairs={{0,1},{1,0},{2,3},{3,2},{4,5},{5,4},{6,7},{7,6},{8,9},{9,8},{10,11... | collective-permute-start | bytes 884744 | tf_op jit(solution)/shard_map/ppermute | solution.py:378
  28.2 13.2 %collective-permute-start.6 = (bf16[144,1536]{1,0:T(8,128)(2,1)S(1)}, bf16[144,1536]{1,0:T(8,128)(2,1)S(1)}, u32[]{:S(2)}, u32[]{:S(2)}) collective-permute-start(bf16[144,1536]{1,0:T(8,128)(2,1)S(1)} %get-tuple-element.225.next_y), channel_id=1, source_target_pairs={{0,4},{1,5},{2,6},{3,7},{4,0},{5,1},{6,2},{7,3},{8,12},{9,13},{10,... | collective-permute-start | bytes 1327112 | tf_op jit(solution)/shard_map/ppermute | solution.py:378
  29.8 13.1 %collective-permute-start.7 = (bf16[144,1536]{1,0:T(8,128)(2,1)S(1)}, bf16[144,1536]{1,0:T(8,128)(2,1)S(1)}, u32[]{:S(2)}, u32[]{:S(2)}) collective-permute-start(bf16[144,1536]{1,0:T(8,128)(2,1)S(1)} %get-tuple-element.226.next_x), channel_id=1, source_target_pairs={{0,2},{1,3},{2,0},{3,1},{4,6},{5,7},{6,4},{7,5},{8,10},{9,11},{10,... | collective-permute-start | bytes 1327112 | tf_op jit(solution)/shard_map/ppermute | solution.py:378
  31.0 21.4 %collective-permute-start.8 = (bf16[288,768]{1,0:T(8,128)(2,1)S(1)}, bf16[288,768]{1,0:T(8,128)(2,1)S(1)}, u32[]{:S(2)}, u32[]{:S(2)}) collective-permute-start(bf16[288,768]{1,0:T(8,128)(2,1)S(1)} %get-tuple-element.217), channel_id=1, source_target_pairs={{0,2},{1,3},{2,0},{3,1},{4,6},{5,7},{6,4},{7,5},{8,10},{9,11},{10,... | collective-permute-start | bytes 1327112 | tf_op jit(solution)/shard_map/ppermute | solution.py:378
  33.2 19.2 %collective-permute-start.9 = (bf16[288,768]{1,0:T(8,128)(2,1)S(1)}, bf16[288,768]{1,0:T(8,128)(2,1)S(1)}, u32[]{:S(2)}, u32[]{:S(2)}) collective-permute-start(bf16[288,768]{1,0:T(8,128)(2,1)S(1)} %get-tuple-element.220), channel_id=1, source_target_pairs={{0,4},{1,5},{2,6},{3,7},{4,0},{5,1},{6,2},{7,3},{8,12},{9,13},{10,... | collective-permute-start | bytes 1327112 | tf_op jit(solution)/shard_map/ppermute | solution.py:378
  33.7 9.4 %copy-start.9 = (bf16[384,3072]{1,0:T(8,128)(2,1)S(1)}, bf16[384,3072]{1,0:T(8,128)(2,1)}, u32[]{:S(2)}) copy-start(bf16[384,3072]{1,0:T(8,128)(2,1)} %own.1) | copy-start | bytes 7077892
  33.7 25.8 %collective-permute-start.10 = (bf16[288,768]{1,0:T(8,128)(2,1)S(1)}, bf16[288,768]{1,0:T(8,128)(2,1)S(1)}, u32[]{:S(2)}, u32[]{:S(2)}) collective-permute-start(bf16[288,768]{1,0:T(8,128)(2,1)S(1)} %get-tuple-element.221), channel_id=1, source_target_pairs={{0,6},{1,7},{2,4},{3,5},{4,2},{5,3},{6,0},{7,1},{8,14},{9,15},{10,... | collective-permute-start | bytes 1327112 | tf_op jit(solution)/shard_map/ppermute | solution.py:378
  60.5 16.3 %collective-permute-start.17 = (bf16[240,1536]{1,0:T(8,128)(2,1)S(1)}, bf16[240,1536]{1,0:T(8,128)(2,1)S(1)}, u32[]{:S(2)}, u32[]{:S(2)}) collective-permute-start(bf16[240,1536]{1,0:T(8,128)(2,1)S(1)} %get-tuple-element.266.to_x), channel_id=1, source_target_pairs={{0,2},{1,3},{2,0},{3,1},{4,6},{5,7},{6,4},{7,5},{8,10},{9,11},{10,... | collective-permute-start | bytes 2211848 | tf_op jit(solution)/shard_map/ppermute | solution.py:378
  61.3 16.5 %collective-permute-start.18 = (bf16[240,1536]{1,0:T(8,128)(2,1)S(1)}, bf16[240,1536]{1,0:T(8,128)(2,1)S(1)}, u32[]{:S(2)}, u32[]{:S(2)}) collective-permute-start(bf16[240,1536]{1,0:T(8,128)(2,1)S(1)} %get-tuple-element.259.to_y), channel_id=1, source_target_pairs={{0,4},{1,5},{2,6},{3,7},{4,0},{5,1},{6,2},{7,3},{8,12},{9,13},{10,... | collective-permute-start | bytes 2211848 | tf_op jit(solution)/shard_map/ppermute | solution.py:378
  62.7 1.4 collective-permute-start.11
  62.7 1.7 %collective-permute-start.12 = (bf16[384,256]{1,0:T(8,128)(2,1)S(1)}, bf16[384,256]{1,0:T(8,128)(2,1)S(1)}, u32[]{:S(2)}, u32[]{:S(2)}) collective-permute-start(bf16[384,256]{1,0:T(8,128)(2,1)S(1)} %get-tuple-element.239), channel_id=1, source_target_pairs={{0,1},{1,0},{2,3},{3,2},{4,5},{5,4},{6,7},{7,6},{8,9},{9,8},{10,11... | collective-permute-start | bytes 589832 | tf_op jit(solution)/shard_map/ppermute | solution.py:378
  63.2 1.5 collective-permute-start.13
  66.4 3.9 %collective-permute-start.14 = (bf16[384,256]{1,0:T(8,128)(2,1)S(1)}, bf16[384,256]{1,0:T(8,128)(2,1)S(1)}, u32[]{:S(2)}, u32[]{:S(2)}) collective-permute-start(bf16[384,256]{1,0:T(8,128)(2,1)S(1)} %get-tuple-element.248), channel_id=1, source_target_pairs={{0,1},{1,0},{2,3},{3,2},{4,5},{5,4},{6,7},{7,6},{8,9},{9,8},{10,11... | collective-permute-start | bytes 589832 | tf_op jit(solution)/shard_map/ppermute | solution.py:378
  66.7 17.6 %collective-permute-start.19 = (bf16[384,768]{1,0:T(8,128)(2,1)S(1)}, bf16[384,768]{1,0:T(8,128)(2,1)S(1)}, u32[]{:S(2)}, u32[]{:S(2)}) collective-permute-start(bf16[384,768]{1,0:T(8,128)(2,1)S(1)} %term_own.4.a), channel_id=1, source_target_pairs={{0,8},{24,16},{1,9},{25,17},{2,10},{26,18},{3,11},{27,19},{4,12},{... | collective-permute-start | bytes 1769480 | tf_op jit(solution)/shard_map/ppermute | solution.py:342
  70.2 1.5 collective-permute-start.15
  70.3 1.7 %collective-permute-start.16 = (bf16[384,256]{1,0:T(8,128)(2,1)S(1)}, bf16[384,256]{1,0:T(8,128)(2,1)S(1)}, u32[]{:S(2)}, u32[]{:S(2)}) collective-permute-start(bf16[384,256]{1,0:T(8,128)(2,1)S(1)} %get-tuple-element.250), channel_id=1, source_target_pairs={{0,1},{1,0},{2,3},{3,2},{4,5},{5,4},{6,7},{7,6},{8,9},{9,8},{10,11... | collective-permute-start | bytes 589832 | tf_op jit(solution)/shard_map/ppermute | solution.py:378
  77.9 9.2 %collective-permute-start.20 = (bf16[144,1536]{1,0:T(8,128)(2,1)S(1)}, bf16[144,1536]{1,0:T(8,128)(2,1)S(1)}, u32[]{:S(2)}, u32[]{:S(2)}) collective-permute-start(bf16[144,1536]{1,0:T(8,128)(2,1)S(1)} %get-tuple-element.269.next_y), channel_id=1, source_target_pairs={{0,4},{1,5},{2,6},{3,7},{4,0},{5,1},{6,2},{7,3},{8,12},{9,13},{10,... | collective-permute-start | bytes 1327112 | tf_op jit(solution)/shard_map/ppermute | solution.py:378
  79.4 8.3 %collective-permute-start.21 = (bf16[144,1536]{1,0:T(8,128)(2,1)S(1)}, bf16[144,1536]{1,0:T(8,128)(2,1)S(1)}, u32[]{:S(2)}, u32[]{:S(2)}) collective-permute-start(bf16[144,1536]{1,0:T(8,128)(2,1)S(1)} %get-tuple-element.270.next_x), channel_id=1, source_target_pairs={{0,2},{1,3},{2,0},{3,1},{4,6},{5,7},{6,4},{7,5},{8,10},{9,11},{10,... | collective-permute-start | bytes 1327112 | tf_op jit(solution)/shard_map/ppermute | solution.py:378
  80.8 15.0 %collective-permute-start.25 = (bf16[384,768]{1,0:T(8,128)(2,1)S(1)}, bf16[384,768]{1,0:T(8,128)(2,1)S(1)}, u32[]{:S(2)}, u32[]{:S(2)}) collective-permute-start(bf16[384,768]{1,0:T(8,128)(2,1)S(1)} %term_own.5.a), channel_id=1, source_target_pairs={{0,8},{24,16},{1,9},{25,17},{2,10},{26,18},{3,11},{27,19},{4,12},{... | collective-permute-start | bytes 1769480 | tf_op jit(solution)/shard_map/ppermute | solution.py:342
  84.5 13.8 %collective-permute-start.26 = (bf16[384,768]{1,0:T(8,128)(2,1)S(1)}, bf16[384,768]{1,0:T(8,128)(2,1)S(1)}, u32[]{:S(2)}, u32[]{:S(2)}) collective-permute-start(bf16[384,768]{1,0:T(8,128)(2,1)S(1)} %add.8.a), channel_id=1, source_target_pairs={{8,16},{16,8},{9,17},{17,9},{10,18},{18,10},{11,19},{19,11},{12,20... | collective-permute-start | bytes 1769480 | tf_op jit(solution)/shard_map/ppermute | solution.py:349
  88.7 1.5 collective-permute-start.22
  88.8 1.7 %collective-permute-start.23 = (bf16[384,256]{1,0:T(8,128)(2,1)S(1)}, bf16[384,256]{1,0:T(8,128)(2,1)S(1)}, u32[]{:S(2)}, u32[]{:S(2)}) collective-permute-start(bf16[384,256]{1,0:T(8,128)(2,1)S(1)} %get-tuple-element.276), channel_id=1, source_target_pairs={{0,1},{1,0},{2,3},{3,2},{4,5},{5,4},{6,7},{7,6},{8,9},{9,8},{10,11... | collective-permute-start | bytes 589832 | tf_op jit(solution)/shard_map/ppermute | solution.py:378
  89.3 1.5 collective-permute-start.24
  91.6 17.8 %collective-permute-start.30 = (bf16[384,768]{1,0:T(8,128)(2,1)S(1)}, bf16[384,768]{1,0:T(8,128)(2,1)S(1)}, u32[]{:S(2)}, u32[]{:S(2)}) collective-permute-start(bf16[384,768]{1,0:T(8,128)(2,1)S(1)} %term_own.6.a), channel_id=1, source_target_pairs={{0,8},{24,16},{1,9},{25,17},{2,10},{26,18},{3,11},{27,19},{4,12},{... | collective-permute-start | bytes 1769480 | tf_op jit(solution)/shard_map/ppermute | solution.py:342
  96.0 22.0 %collective-permute-start.32 = (bf16[384,768]{1,0:T(8,128)(2,1)S(1)}, bf16[384,768]{1,0:T(8,128)(2,1)S(1)}, u32[]{:S(2)}, u32[]{:S(2)}) collective-permute-start(bf16[384,768]{1,0:T(8,128)(2,1)S(1)} %add.9.a), channel_id=1, source_target_pairs={{8,16},{16,8},{9,17},{17,9},{10,18},{18,10},{11,19},{19,11},{12,20... | collective-permute-start | bytes 1769480 | tf_op jit(solution)/shard_map/ppermute | solution.py:349
  97.7 1.5 collective-permute-start.27
  97.8 1.7 %collective-permute-start.28 = (bf16[384,256]{1,0:T(8,128)(2,1)S(1)}, bf16[384,256]{1,0:T(8,128)(2,1)S(1)}, u32[]{:S(2)}, u32[]{:S(2)}) collective-permute-start(bf16[384,256]{1,0:T(8,128)(2,1)S(1)} %get-tuple-element.288), channel_id=1, source_target_pairs={{0,1},{1,0},{2,3},{3,2},{4,5},{5,4},{6,7},{7,6},{8,9},{9,8},{10,11... | collective-permute-start | bytes 589832 | tf_op jit(solution)/shard_map/ppermute | solution.py:378
  98.3 1.5 collective-permute-start.29
  100.6 21.2 %collective-permute-start.33 = (bf16[384,768]{1,0:T(8,128)(2,1)S(1)}, bf16[384,768]{1,0:T(8,128)(2,1)S(1)}, u32[]{:S(2)}, u32[]{:S(2)}) collective-permute-start(bf16[384,768]{1,0:T(8,128)(2,1)S(1)} %term_own.7.a), channel_id=1, source_target_pairs={{0,8},{24,16},{1,9},{25,17},{2,10},{26,18},{3,11},{27,19},{4,12},{... | collective-permute-start | bytes 1769480 | tf_op jit(solution)/shard_map/ppermute | solution.py:342
  108.1 19.5 %collective-permute-start.34 = (bf16[384,768]{1,0:T(8,128)(2,1)S(1)}, bf16[384,768]{1,0:T(8,128)(2,1)S(1)}, u32[]{:S(2)}, u32[]{:S(2)}) collective-permute-start(bf16[384,768]{1,0:T(8,128)(2,1)S(1)} %add.10.total), channel_id=1, source_target_pairs={{8,0},{16,24},{9,1},{17,25},{10,2},{18,26},{11,3},{19,27},{12,4},{... | collective-permute-start | bytes 1769480 | tf_op jit(solution)/shard_map/ppermute | solution.py:356
  113.9 1.6 collective-permute-start.31
  113.9 18.1 %collective-permute-start.35 = (bf16[384,768]{1,0:T(8,128)(2,1)S(1)}, bf16[384,768]{1,0:T(8,128)(2,1)}, u32[]{:S(2)}, u32[]{:S(2)}) collective-permute-start(bf16[384,768]{1,0:T(8,128)(2,1)S(1)} %add.11.a), channel_id=1, source_target_pairs={{8,16},{16,8},{9,17},{17,9},{10,18},{18,10},{11,19},{19,11},{12,20... | collective-permute-start | bytes 1769480 | tf_op jit(solution)/shard_map/ppermute | solution.py:349
  119.0 19.9 %collective-permute-start.36 = (bf16[384,768]{1,0:T(8,128)(2,1)}, bf16[384,768]{1,0:T(8,128)(2,1)}, u32[]{:S(2)}, u32[]{:S(2)}) collective-permute-start(bf16[384,768]{1,0:T(8,128)(2,1)} %add.12.total), channel_id=1, source_target_pairs={{8,0},{16,24},{9,1},{17,25},{10,2},{18,26},{11,3},{19,27},{12,4},{... | collective-permute-start | bytes 1769480 | tf_op jit(solution)/shard_map/ppermute | solution.py:356
  120.4 21.1 %collective-permute-start.37 = (bf16[384,768]{1,0:T(8,128)(2,1)}, bf16[384,768]{1,0:T(8,128)(2,1)}, u32[]{:S(2)}, u32[]{:S(2)}) collective-permute-start(bf16[384,768]{1,0:T(8,128)(2,1)} %get-tuple-element.309), channel_id=1, source_target_pairs={{0,2},{1,3},{2,0},{3,1},{4,6},{5,7},{6,4},{7,5},{8,10},{9,11},{10,... | collective-permute-start | bytes 1769480 | tf_op jit(solution)/shard_map/ppermute | solution.py:378
  121.8 19.7 %collective-permute-start.38 = (bf16[384,768]{1,0:T(8,128)(2,1)}, bf16[384,768]{1,0:T(8,128)(2,1)}, u32[]{:S(2)}, u32[]{:S(2)}) collective-permute-start(bf16[384,768]{1,0:T(8,128)(2,1)} %get-tuple-element.310), channel_id=1, source_target_pairs={{0,4},{1,5},{2,6},{3,7},{4,0},{5,1},{6,2},{7,3},{8,12},{9,13},{10,... | collective-permute-start | bytes 1769480 | tf_op jit(solution)/shard_map/ppermute | solution.py:378
  128.4 18.8 %collective-permute-start.39 = (bf16[384,768]{1,0:T(8,128)(2,1)}, bf16[384,768]{1,0:T(8,128)(2,1)}, u32[]{:S(2)}, u32[]{:S(2)}) collective-permute-start(bf16[384,768]{1,0:T(8,128)(2,1)} %add.13.a), channel_id=1, source_target_pairs={{8,16},{16,8},{9,17},{17,9},{10,18},{18,10},{11,19},{19,11},{12,20... | collective-permute-start | bytes 1769480 | tf_op jit(solution)/shard_map/ppermute | solution.py:349
  133.3 8.8 %copy-start.2 = (bf16[384,3072]{1,0:T(8,128)(2,1)S(1)}, bf16[384,3072]{1,0:T(8,128)(2,1)}, u32[]{:S(2)}) copy-start(bf16[384,3072]{1,0:T(8,128)(2,1)} %key.5) | copy-start | bytes 7077892
  133.3 8.8 %copy-start.4 = (bf16[384,3072]{1,0:T(8,128)(2,1)S(1)}, bf16[384,3072]{1,0:T(8,128)(2,1)}, u32[]{:S(2)}) copy-start(bf16[384,3072]{1,0:T(8,128)(2,1)} %value.5) | copy-start | bytes 7077892
  133.3 21.8 %collective-permute-start.40 = (bf16[384,768]{1,0:T(8,128)(2,1)S(1)}, bf16[384,768]{1,0:T(8,128)(2,1)S(1)}, u32[]{:S(2)}, u32[]{:S(2)}) collective-permute-start(bf16[384,768]{1,0:T(8,128)(2,1)S(1)} %add.14.total), channel_id=1, source_target_pairs={{8,0},{16,24},{9,1},{17,25},{10,2},{18,26},{11,3},{19,27},{12,4},{... | collective-permute-start | bytes 1769480 | tf_op jit(solution)/shard_map/ppermute | solution.py:356
  141.5 15.9 %collective-permute-start.41 = (bf16[384,768]{1,0:T(8,128)(2,1)S(1)}, bf16[384,768]{1,0:T(8,128)(2,1)S(1)}, u32[]{:S(2)}, u32[]{:S(2)}) collective-permute-start(bf16[384,768]{1,0:T(8,128)(2,1)S(1)} %copy-done.16), channel_id=1, source_target_pairs={{0,6},{1,7},{2,4},{3,5},{4,2},{5,3},{6,0},{7,1},{8,14},{9,15},{10,... | collective-permute-start | bytes 1769480 | tf_op jit(solution)/shard_map/ppermute | solution.py:378
  148.6 18.1 %collective-permute-start.42 = (bf16[384,768]{1,0:T(8,128)(2,1)S(1)}, bf16[384,768]{1,0:T(8,128)(2,1)S(1)}, u32[]{:S(2)}, u32[]{:S(2)}) collective-permute-start(bf16[384,768]{1,0:T(8,128)(2,1)S(1)} %add.15.total), channel_id=1, source_target_pairs={{8,0},{16,24},{9,1},{17,25},{10,2},{18,26},{11,3},{19,27},{12,4},{... | collective-permute-start | bytes 1769480 | tf_op jit(solution)/shard_map/ppermute | solution.py:356
  (12 other events, 47.8 us)
